TPU v7x, 512 devices: a whole 4x4x16 slice. The times are simulated.
512 devices in a mesh: dom: 256 (over x, z, y_hi, core), band: 2 (over y_lo).
Axes of the slice: x: 4, y: 4 (y_hi: 2, y_lo: 2; y = y_hi * 2 + y_lo), z: 16, core: 2. Of those that a mesh axis runs over, the one named last changes fastest.
Arguments:
- residual: float32 [16, 2048, 8, 128], P('band', 'dom'), may hold values from -24 to 24
- potential: float32 [2048, 8, 128], P(('dom', 'band')), may hold values from 0.05 to 1
- shifts: float32 [16], P('band'), may hold values from 0.05 to 0.5
Outputs:
- correction: float32 [16, 2048, 8, 128], P('band', 'dom')
All inputs are finite; a program needn't handle non-finite values.
Results may differ from a plain program's by a relative error of at most 0.00002.
Values sent between devices are 32-bit elements; how exact they have to be, the bound alone decides.
No kernel may reach another device: no remote copies, remote signals or barrier semaphores. Data moves between devices by JAX's collectives and lax.ppermute only.
A program may use at most 64 MiB of HBM per device.

v0:
```python
import jax
import jax.numpy as jnp
from jax import lax
from jax.sharding import PartitionSpec as P

SWEEPS = 2
COARSE = 4


OMEGA = 0.7
KINETIC = 2.0


def from_behind(value, axis, steps):
    count = lax.axis_size(axis)
    initial, last = (max(0, -steps), min(count, count - steps))
    return lax.ppermute(value, axis, [(source, source + steps) for source in range(initial, last)])


def neighbour_sums(padded):
    faces = (
        padded[:, 2:, 1:-1, 1:-1]
        + padded[:, :-2, 1:-1, 1:-1]
        + padded[:, 1:-1, 2:, 1:-1]
        + padded[:, 1:-1, :-2, 1:-1]
        + padded[:, 1:-1, 1:-1, 2:]
        + padded[:, 1:-1, 1:-1, :-2]
    )
    edges = (
        padded[:, 2:, 2:, 1:-1]
        + padded[:, 2:, :-2, 1:-1]
        + padded[:, :-2, 2:, 1:-1]
        + padded[:, :-2, :-2, 1:-1]
        + padded[:, 2:, 1:-1, 2:]
        + padded[:, 2:, 1:-1, :-2]
        + padded[:, :-2, 1:-1, 2:]
        + padded[:, :-2, 1:-1, :-2]
        + padded[:, 1:-1, 2:, 2:]
        + padded[:, 1:-1, 2:, :-2]
        + padded[:, 1:-1, :-2, 2:]
        + padded[:, 1:-1, :-2, :-2]
    )
    return (faces, edges)


def operator(field, weight, kinetic, padder):
    faces, edges = neighbour_sums(padder(field))
    return -(kinetic / 6.0) * (2.0 * faces + edges - 24.0 * field) + weight * field


def smooth(field, source, weight, kinetic, padder):
    return field + OMEGA * (source - operator(field, weight, kinetic, padder)) / (
        4.0 * kinetic + weight
    )


def restrict(field):
    leading, size_x, size_y, size_z = field.shape
    cubes = field.reshape(leading, size_x // 2, 2, size_y // 2, 2, size_z // 2, 2)
    return cubes.mean(axis=(2, 4, 6))


def prolong(field):
    return jnp.repeat(jnp.repeat(jnp.repeat(field, 2, axis=1), 2, axis=2), 2, axis=3)


def domain_layout():
    devices = lax.axis_size("dom")
    count_z = 2
    count_y = min(16, devices // 4)
    count_x = devices // (count_y * count_z)
    position = lax.axis_index("dom")
    coords = (position // (count_y * count_z), position // count_z % count_y, position % count_z)
    return (coords, (count_x, count_y, count_z), (count_y * count_z, count_z, 1))


def ghosts(field):
    coords, counts, strides = domain_layout()
    extended = field
    for dimension in range(3):
        position = dimension + 1
        length = extended.shape[position]
        upper_face = lax.slice_in_dim(extended, length - 1, length, axis=position)
        lower_face = lax.slice_in_dim(extended, 0, 1, axis=position)
        pieces = []
        for direction, face_layer in ((1, upper_face), (-1, lower_face)):
            arrived = from_behind(face_layer, "dom", direction * strides[dimension])
            inside = (coords[dimension] - direction >= 0) & (
                coords[dimension] - direction < counts[dimension]
            )
            pieces.append(jnp.where(inside, arrived, 0.0))
        extended = jnp.concatenate([pieces[0], extended, pieces[1]], axis=position)
    return extended


def run_sweeps(field, source, potential_level, shift_field, kinetic, count):
    weight = potential_level + shift_field
    for sweep in range(count):
        field = smooth(field, source, weight, kinetic, ghosts)
    return field


def solve_coarse(source, potential_coarse, shift_field, kinetic):
    weight = potential_coarse + shift_field
    field = OMEGA * source / (4.0 * kinetic + weight)
    return run_sweeps(field, source, potential_coarse, shift_field, kinetic, COARSE - 1)


def vcycle(residual, potential, shift_field):
    kinetic_fine = KINETIC
    kinetic_middle = KINETIC / 4.0
    kinetic_coarse = KINETIC / 16.0
    potential_fine = potential[None]
    weight_fine = potential_fine + shift_field
    potential_middle = restrict(potential_fine)
    weight_middle = potential_middle + shift_field
    potential_coarse = restrict(potential_middle)
    faces, edges = neighbour_sums(ghosts(residual))
    source = 0.5 * residual + faces / 12.0
    fine = OMEGA * source / (4.0 * kinetic_fine + weight_fine)
    fine = run_sweeps(fine, source, potential_fine, shift_field, kinetic_fine, SWEEPS - 1)
    source_middle = restrict(source - operator(fine, weight_fine, kinetic_fine, ghosts))
    middle = OMEGA * source_middle / (4.0 * kinetic_middle + weight_middle)
    middle = run_sweeps(
        middle, source_middle, potential_middle, shift_field, kinetic_middle, SWEEPS - 1
    )
    source_coarse = restrict(
        source_middle - operator(middle, weight_middle, kinetic_middle, ghosts)
    )
    coarse = solve_coarse(source_coarse, potential_coarse, shift_field, kinetic_coarse)
    middle = middle + prolong(coarse)
    middle = run_sweeps(
        middle, source_middle, potential_middle, shift_field, kinetic_middle, SWEEPS
    )
    fine = fine + prolong(middle)
    fine = run_sweeps(fine, source, potential_fine, shift_field, kinetic_fine, SWEEPS)
    return fine


def body(residual, potential, shifts):
    potential_block = lax.all_gather(potential, "band", axis=0, tiled=True)
    shift_field = shifts.reshape(shifts.shape[0], 1, 1, 1)
    return vcycle(residual, potential_block, shift_field)


def solution(mesh):
    return jax.shard_map(
        body,
        mesh=mesh,
        in_specs=(P("band", "dom", None, None), P(("dom", "band"), None, None), P("band")),
        out_specs=P("band", "dom", None, None),
        check_vma=False,
    )
```

profile of v0, /device:TPU:1, one launch (start us, length us, event | category | flops | bytes accessed | tf_op | source)
XLA Modules:
  0.0 608.8 jit_solution(12580815772360081064)
XLA Ops:
  0.8 16.3 %collective-permute-start.1 = (f32[8,1,8,128]{3,2,1,0:T(8,128)S(1)}, f32[8,1,8,128]{3,2,1,0:T(8,128)S(1)}, u32[]{:S(2)}, u32[]{:S(2)}) collective-permute-start(f32[8,1,8,128]{3,2,1,0:T(8,128)S(1)} %get-tuple-element.85), channel_id=1, source_target_pairs={{0,64},{2,66},{4,68},{6,70},{8,72},{10,74},{12,76},{14,78},{16,80}... | collective-permute-start | bytes 98312 | tf_op jit(solution)/shard_map/ppermute | solution.py:17
  18.5 12.0 %collective-permute-done = f32[8,1,8,128]{3,2,1,0:T(8,128)S(1)} collective-permute-done((f32[8,1,8,128]{3,2,1,0:T(8,128)S(1)}, f32[8,1,8,128]{3,2,1,0:T(8,128)S(1)}, u32[]{:S(2)}, u32[]{:S(2)}) %collective-permute-start) | collective-permute-done | bytes 32800 | tf_op jit(solution)/shard_map/ppermute | solution.py:17
  42.9 5.4 collective-permute-start.4
  48.4 7.0 %all_gather.3 = f32[8,8,128]{2,1,0:T(8,128)S(1)} all-gather(f32[4,8,128]{2,1,0:T(8,128)} %param.4), channel_id=1, replica_groups=mesh['dom'=256,'band'=2] {'band'}, dimensions={0}, use_global_device_ids=true | all-gather | bytes 49152 | tf_op jit(solution)/shard_map/all_gather | solution.py:141
  71.0 12.1 %collective-permute-done.6 = f32[8,1,8,128]{3,2,1,0:T(8,128)S(1)} collective-permute-done((f32[8,1,8,128]{3,2,1,0:T(8,128)S(1)}, f32[8,1,8,128]{3,2,1,0:T(8,128)S(1)}, u32[]{:S(2)}, u32[]{:S(2)}) %collective-permute-start.6) | collective-permute-done | bytes 32800 | tf_op jit(solution)/shard_map/ppermute | solution.py:17
  93.9 10.9 %collective-permute-start.11 = (f32[8,10,10,1]{3,0,2,1:T(8,128)S(1)}, f32[8,10,10,1]{3,0,2,1:T(8,128)S(1)}, u32[]{:S(2)}, u32[]{:S(2)}) collective-permute-start(f32[8,10,10,1]{3,0,2,1:T(8,128)S(1)} %get-tuple-element.54), channel_id=1, source_target_pairs={{0,2},{2,4},{4,6},{6,8},{8,10},{10,12},{12,14},{14,16},{16,18},{18... | collective-permute-start | bytes 9608 | tf_op jit(solution)/shard_map/ppermute | solution.py:17
  106.9 7.2 %collective-permute-done.11 = f32[8,10,10,1]{3,0,2,1:T(8,128)S(1)} collective-permute-done((f32[8,10,10,1]{3,0,2,1:T(8,128)S(1)}, f32[8,10,10,1]{3,0,2,1:T(8,128)S(1)}, u32[]{:S(2)}, u32[]{:S(2)}) %collective-permute-start.11) | collective-permute-done | bytes 3232 | tf_op jit(solution)/shard_map/ppermute | solution.py:17
  117.2 14.3 %collective-permute-start.13 = (f32[8,1,8,128]{3,2,1,0:T(8,128)S(1)}, f32[8,1,8,128]{3,2,1,0:T(8,128)S(1)}, u32[]{:S(2)}, u32[]{:S(2)}) collective-permute-start(f32[8,1,8,128]{3,2,1,0:T(8,128)S(1)} %get-tuple-element.81), channel_id=1, source_target_pairs={{0,64},{2,66},{4,68},{6,70},{8,72},{10,74},{12,76},{14,78},{16,80}... | collective-permute-start | bytes 98312 | tf_op jit(solution)/shard_map/ppermute | solution.py:17
  135.2 12.3 %collective-permute-done.12 = f32[8,1,8,128]{3,2,1,0:T(8,128)S(1)} collective-permute-done((f32[8,1,8,128]{3,2,1,0:T(8,128)S(1)}, f32[8,1,8,128]{3,2,1,0:T(8,128)S(1)}, u32[]{:S(2)}, u32[]{:S(2)}) %collective-permute-start.12) | collective-permute-done | bytes 32800 | tf_op jit(solution)/shard_map/ppermute | solution.py:17
  155.5 5.6 collective-permute-start.17
  166.3 5.6 collective-permute-done.16
  176.1 4.8 reduce_sum.36
  181.2 10.4 %collective-permute-start.19 = (f32[8,1,4,64]{3,0,2,1:T(8,128)S(1)}, f32[8,1,4,64]{3,0,2,1:T(8,128)S(1)}, u32[]{:S(2)}, u32[]{:S(2)}) collective-permute-start(f32[8,1,4,64]{3,0,2,1:T(8,128)S(1)} %get-tuple-element.173), channel_id=1, source_target_pairs={{0,64},{2,66},{4,68},{6,70},{8,72},{10,74},{12,76},{14,78},{16,80}... | collective-permute-start | bytes 24584 | tf_op jit(solution)/shard_map/ppermute | solution.py:17
  192.9 11.9 %collective-permute-done.18 = f32[8,1,4,64]{3,0,2,1:T(8,128)S(1)} collective-permute-done((f32[8,1,4,64]{3,0,2,1:T(8,128)S(1)}, f32[8,1,4,64]{3,0,2,1:T(8,128)S(1)}, u32[]{:S(2)}, u32[]{:S(2)}) %collective-permute-start.18) | collective-permute-done | bytes 8224 | tf_op jit(solution)/shard_map/ppermute | solution.py:17
  212.3 5.3 collective-permute-start.22
  222.5 13.8 %collective-permute-start.25 = (f32[8,1,4,64]{3,0,2,1:T(8,128)S(1)}, f32[8,1,4,64]{3,0,2,1:T(8,128)S(1)}, u32[]{:S(2)}, u32[]{:S(2)}) collective-permute-start(f32[8,1,4,64]{3,0,2,1:T(8,128)S(1)} %get-tuple-element.171), channel_id=1, source_target_pairs={{0,64},{2,66},{4,68},{6,70},{8,72},{10,74},{12,76},{14,78},{16,80}... | collective-permute-start | bytes 24584 | tf_op jit(solution)/shard_map/ppermute | solution.py:17
  238.0 11.9 %collective-permute-done.24 = f32[8,1,4,64]{3,0,2,1:T(8,128)S(1)} collective-permute-done((f32[8,1,4,64]{3,0,2,1:T(8,128)S(1)}, f32[8,1,4,64]{3,0,2,1:T(8,128)S(1)}, u32[]{:S(2)}, u32[]{:S(2)}) %collective-permute-start.24) | collective-permute-done | bytes 8224 | tf_op jit(solution)/shard_map/ppermute | solution.py:17
  252.5 5.0 collective-permute-done.26
  257.7 11.7 %collective-permute-start.28 = (f32[8,6,6,1]{3,0,2,1:T(8,128)S(1)}, f32[8,6,6,1]{3,0,2,1:T(8,128)S(1)}, u32[]{:S(2)}, u32[]{:S(2)}) collective-permute-start(f32[8,6,6,1]{3,0,2,1:T(8,128)S(1)} %get-tuple-element.97), channel_id=1, source_target_pairs={{2,0},{4,2},{6,4},{8,6},{10,8},{12,10},{14,12},{16,14},{18,16},{20... | collective-permute-start | bytes 3464 | tf_op jit(solution)/shard_map/ppermute | solution.py:17
  274.4 8.9 %collective-permute-start.31 = (f32[8,1,2,32]{0,3,2,1:T(8,128)S(1)}, f32[8,1,2,32]{0,3,2,1:T(8,128)S(1)}, u32[]{:S(2)}, u32[]{:S(2)}) collective-permute-start(f32[8,1,2,32]{0,3,2,1:T(8,128)S(1)} %get-tuple-element.169), channel_id=1, source_target_pairs={{0,64},{2,66},{4,68},{6,70},{8,72},{10,74},{12,76},{14,78},{16,80}... | collective-permute-start | bytes 6152 | tf_op jit(solution)/shard_map/ppermute | solution.py:17
  284.8 12.0 %collective-permute-done.30 = f32[8,1,2,32]{0,3,2,1:T(8,128)S(1)} collective-permute-done((f32[8,1,2,32]{0,3,2,1:T(8,128)S(1)}, f32[8,1,2,32]{0,3,2,1:T(8,128)S(1)}, u32[]{:S(2)}, u32[]{:S(2)}) %collective-permute-start.30) | collective-permute-done | bytes 2080 | tf_op jit(solution)/shard_map/ppermute | solution.py:17
  299.5 5.0 collective-permute-done.32
  304.5 10.9 %collective-permute-start.34 = (f32[8,4,4,1]{3,0,2,1:T(8,128)S(1)}, f32[8,4,4,1]{3,0,2,1:T(8,128)S(1)}, u32[]{:S(2)}, u32[]{:S(2)}) collective-permute-start(f32[8,4,4,1]{3,0,2,1:T(8,128)S(1)} %get-tuple-element.167), channel_id=1, source_target_pairs={{2,0},{4,2},{6,4},{8,6},{10,8},{12,10},{14,12},{16,14},{18,16},{20... | collective-permute-start | bytes 1544 | tf_op jit(solution)/shard_map/ppermute | solution.py:17
  319.9 13.2 %collective-permute-start.37 = (f32[8,1,2,32]{0,3,2,1:T(8,128)S(1)}, f32[8,1,2,32]{0,3,2,1:T(8,128)S(1)}, u32[]{:S(2)}, u32[]{:S(2)}) collective-permute-start(f32[8,1,2,32]{0,3,2,1:T(8,128)S(1)} %get-tuple-element.153), channel_id=1, source_target_pairs={{0,64},{2,66},{4,68},{6,70},{8,72},{10,74},{12,76},{14,78},{16,80}... | collective-permute-start | bytes 6152 | tf_op jit(solution)/shard_map/ppermute | solution.py:17
  334.6 12.0 %collective-permute-done.36 = f32[8,1,2,32]{0,3,2,1:T(8,128)S(1)} collective-permute-done((f32[8,1,2,32]{0,3,2,1:T(8,128)S(1)}, f32[8,1,2,32]{0,3,2,1:T(8,128)S(1)}, u32[]{:S(2)}, u32[]{:S(2)}) %collective-permute-start.36) | collective-permute-done | bytes 2080 | tf_op jit(solution)/shard_map/ppermute | solution.py:17
  349.2 5.0 collective-permute-done.38
  354.3 10.8 %collective-permute-start.40 = (f32[8,4,4,1]{3,0,2,1:T(8,128)S(1)}, f32[8,4,4,1]{3,0,2,1:T(8,128)S(1)}, u32[]{:S(2)}, u32[]{:S(2)}) collective-permute-start(f32[8,4,4,1]{3,0,2,1:T(8,128)S(1)} %get-tuple-element.151), channel_id=1, source_target_pairs={{2,0},{4,2},{6,4},{8,6},{10,8},{12,10},{14,12},{16,14},{18,16},{20... | collective-permute-start | bytes 1544 | tf_op jit(solution)/shard_map/ppermute | solution.py:17
  369.6 9.8 %collective-permute-start.43 = (f32[8,1,2,32]{0,3,2,1:T(8,128)S(1)}, f32[8,1,2,32]{0,3,2,1:T(8,128)S(1)}, u32[]{:S(2)}, u32[]{:S(2)}) collective-permute-start(f32[8,1,2,32]{0,3,2,1:T(8,128)S(1)} %get-tuple-element.137), channel_id=1, source_target_pairs={{0,64},{2,66},{4,68},{6,70},{8,72},{10,74},{12,76},{14,78},{16,80}... | collective-permute-start | bytes 6152 | tf_op jit(solution)/shard_map/ppermute | solution.py:17
  380.9 12.0 %collective-permute-done.42 = f32[8,1,2,32]{0,3,2,1:T(8,128)S(1)} collective-permute-done((f32[8,1,2,32]{0,3,2,1:T(8,128)S(1)}, f32[8,1,2,32]{0,3,2,1:T(8,128)S(1)}, u32[]{:S(2)}, u32[]{:S(2)}) %collective-permute-start.42) | collective-permute-done | bytes 2080 | tf_op jit(solution)/shard_map/ppermute | solution.py:17
  395.6 5.0 collective-permute-done.44
  400.7 10.8 %collective-permute-start.46 = (f32[8,4,4,1]{3,0,2,1:T(8,128)S(1)}, f32[8,4,4,1]{3,0,2,1:T(8,128)S(1)}, u32[]{:S(2)}, u32[]{:S(2)}) collective-permute-start(f32[8,4,4,1]{3,0,2,1:T(8,128)S(1)} %get-tuple-element.135), channel_id=1, source_target_pairs={{2,0},{4,2},{6,4},{8,6},{10,8},{12,10},{14,12},{16,14},{18,16},{20... | collective-permute-start | bytes 1544 | tf_op jit(solution)/shard_map/ppermute | solution.py:17
  416.4 6.5 %collective-permute-start.49 = (f32[8,1,4,64]{3,0,2,1:T(8,128)S(1)}, f32[8,1,4,64]{3,0,2,1:T(8,128)S(1)}, u32[]{:S(2)}, u32[]{:S(2)}) collective-permute-start(f32[8,1,4,64]{3,0,2,1:T(8,128)S(1)} %get-tuple-element.121), channel_id=1, source_target_pairs={{0,64},{2,66},{4,68},{6,70},{8,72},{10,74},{12,76},{14,78},{16,80}... | collective-permute-start | bytes 24584 | tf_op jit(solution)/shard_map/ppermute | solution.py:17
  424.3 11.9 %collective-permute-done.48 = f32[8,1,4,64]{3,0,2,1:T(8,128)S(1)} collective-permute-done((f32[8,1,4,64]{3,0,2,1:T(8,128)S(1)}, f32[8,1,4,64]{3,0,2,1:T(8,128)S(1)}, u32[]{:S(2)}, u32[]{:S(2)}) %collective-permute-start.48) | collective-permute-done | bytes 8224 | tf_op jit(solution)/shard_map/ppermute | solution.py:17
  438.8 5.0 collective-permute-done.50
  443.9 10.8 %collective-permute-start.52 = (f32[8,6,6,1]{3,0,2,1:T(8,128)S(1)}, f32[8,6,6,1]{3,0,2,1:T(8,128)S(1)}, u32[]{:S(2)}, u32[]{:S(2)}) collective-permute-start(f32[8,6,6,1]{3,0,2,1:T(8,128)S(1)} %get-tuple-element.93), channel_id=1, source_target_pairs={{2,0},{4,2},{6,4},{8,6},{10,8},{12,10},{14,12},{16,14},{18,16},{20... | collective-permute-start | bytes 3464 | tf_op jit(solution)/shard_map/ppermute | solution.py:17
  459.2 6.7 %collective-permute-start.55 = (f32[8,1,4,64]{3,0,2,1:T(8,128)S(1)}, f32[8,1,4,64]{3,0,2,1:T(8,128)S(1)}, u32[]{:S(2)}, u32[]{:S(2)}) collective-permute-start(f32[8,1,4,64]{3,0,2,1:T(8,128)S(1)} %get-tuple-element.119), channel_id=1, source_target_pairs={{0,64},{2,66},{4,68},{6,70},{8,72},{10,74},{12,76},{14,78},{16,80}... | collective-permute-start | bytes 24584 | tf_op jit(solution)/shard_map/ppermute | solution.py:17
  467.2 11.9 %collective-permute-done.54 = f32[8,1,4,64]{3,0,2,1:T(8,128)S(1)} collective-permute-done((f32[8,1,4,64]{3,0,2,1:T(8,128)S(1)}, f32[8,1,4,64]{3,0,2,1:T(8,128)S(1)}, u32[]{:S(2)}, u32[]{:S(2)}) %collective-permute-start.54) | collective-permute-done | bytes 8224 | tf_op jit(solution)/shard_map/ppermute | solution.py:17
  481.8 5.0 collective-permute-done.56
  486.9 11.1 %collective-permute-start.58 = (f32[8,6,6,1]{3,0,2,1:T(8,128)S(1)}, f32[8,6,6,1]{3,0,2,1:T(8,128)S(1)}, u32[]{:S(2)}, u32[]{:S(2)}) collective-permute-start(f32[8,6,6,1]{3,0,2,1:T(8,128)S(1)} %get-tuple-element.89), channel_id=1, source_target_pairs={{2,0},{4,2},{6,4},{8,6},{10,8},{12,10},{14,12},{16,14},{18,16},{20... | collective-permute-start | bytes 3464 | tf_op jit(solution)/shard_map/ppermute | solution.py:17
  508.5 6.8 %collective-permute-start.61 = (f32[8,1,8,128]{3,2,1,0:T(8,128)S(1)}, f32[8,1,8,128]{3,2,1,0:T(8,128)S(1)}, u32[]{:S(2)}, u32[]{:S(2)}) collective-permute-start(f32[8,1,8,128]{3,2,1,0:T(8,128)S(1)} %get-tuple-element.79), channel_id=1, source_target_pairs={{0,64},{2,66},{4,68},{6,70},{8,72},{10,74},{12,76},{14,78},{16,80}... | collective-permute-start | bytes 98312 | tf_op jit(solution)/shard_map/ppermute | solution.py:17
  516.6 12.0 %collective-permute-done.60 = f32[8,1,8,128]{3,2,1,0:T(8,128)S(1)} collective-permute-done((f32[8,1,8,128]{3,2,1,0:T(8,128)S(1)}, f32[8,1,8,128]{3,2,1,0:T(8,128)S(1)}, u32[]{:S(2)}, u32[]{:S(2)}) %collective-permute-start.60) | collective-permute-done | bytes 32800 | tf_op jit(solution)/shard_map/ppermute | solution.py:17
  531.6 4.9 collective-permute-done.62
  536.7 10.4 %collective-permute-start.65 = (f32[8,10,10,1]{3,0,2,1:T(8,128)S(1)}, f32[8,10,10,1]{3,0,2,1:T(8,128)S(1)}, u32[]{:S(2)}, u32[]{:S(2)}) collective-permute-start(f32[8,10,10,1]{3,0,2,1:T(8,128)S(1)} %get-tuple-element.50), channel_id=1, source_target_pairs={{0,2},{2,4},{4,6},{6,8},{8,10},{10,12},{12,14},{14,16},{16,18},{18... | collective-permute-start | bytes 9608 | tf_op jit(solution)/shard_map/ppermute | solution.py:17
  549.3 7.1 %collective-permute-done.65 = f32[8,10,10,1]{3,0,2,1:T(8,128)S(1)} collective-permute-done((f32[8,10,10,1]{3,0,2,1:T(8,128)S(1)}, f32[8,10,10,1]{3,0,2,1:T(8,128)S(1)}, u32[]{:S(2)}, u32[]{:S(2)}) %collective-permute-start.65) | collective-permute-done | bytes 3232 | tf_op jit(solution)/shard_map/ppermute | solution.py:17
  559.5 9.1 %collective-permute-start.67 = (f32[8,1,8,128]{3,2,1,0:T(8,128)S(1)}, f32[8,1,8,128]{3,2,1,0:T(8,128)S(1)}, u32[]{:S(2)}, u32[]{:S(2)}) collective-permute-start(f32[8,1,8,128]{3,2,1,0:T(8,128)S(1)} %get-tuple-element.77), channel_id=1, source_target_pairs={{0,64},{2,66},{4,68},{6,70},{8,72},{10,74},{12,76},{14,78},{16,80}... | collective-permute-start | bytes 98312 | tf_op jit(solution)/shard_map/ppermute | solution.py:17
  570.1 11.8 %collective-permute-done.66 = f32[8,1,8,128]{3,2,1,0:T(8,128)S(1)} collective-permute-done((f32[8,1,8,128]{3,2,1,0:T(8,128)S(1)}, f32[8,1,8,128]{3,2,1,0:T(8,128)S(1)}, u32[]{:S(2)}, u32[]{:S(2)}) %collective-permute-start.66) | collective-permute-done | bytes 32800 | tf_op jit(solution)/shard_map/ppermute | solution.py:17
  589.9 5.9 collective-permute-start.71
  597.8 7.2 %collective-permute-done.71 = f32[8,10,10,1]{3,0,2,1:T(8,128)S(1)} collective-permute-done((f32[8,10,10,1]{3,0,2,1:T(8,128)S(1)}, f32[8,10,10,1]{3,0,2,1:T(8,128)S(1)}, u32[]{:S(2)}, u32[]{:S(2)}) %collective-permute-start.71) | collective-permute-done | bytes 3232 | tf_op jit(solution)/shard_map/ppermute | solution.py:17
  (380 shorter events, 163.6 us)
Async XLA Ops:
  0.8 17.6 %collective-permute-start.1 = (f32[8,1,8,128]{3,2,1,0:T(8,128)S(1)}, f32[8,1,8,128]{3,2,1,0:T(8,128)S(1)}, u32[]{:S(2)}, u32[]{:S(2)}) collective-permute-start(f32[8,1,8,128]{3,2,1,0:T(8,128)S(1)} %get-tuple-element.85), channel_id=1, source_target_pairs={{0,64},{2,66},{4,68},{6,70},{8,72},{10,74},{12,76},{14,78},{16,80}... | collective-permute-start | bytes 98312 | tf_op jit(solution)/shard_map/ppermute | solution.py:17
  17.1 13.4 %collective-permute-start = (f32[8,1,8,128]{3,2,1,0:T(8,128)S(1)}, f32[8,1,8,128]{3,2,1,0:T(8,128)S(1)}, u32[]{:S(2)}, u32[]{:S(2)}) collective-permute-start(f32[8,1,8,128]{3,2,1,0:T(8,128)S(1)} %get-tuple-element.86), channel_id=1, source_target_pairs={{64,0},{66,2},{68,4},{70,6},{72,8},{74,10},{76,12},{78,14},{80,16}... | collective-permute-start | bytes 98312 | tf_op jit(solution)/shard_map/ppermute | solution.py:17
  36.4 6.3 %collective-permute-start.2 = (f32[8,10,1,128]{3,0,2,1:T(8,128)S(1)}, f32[8,10,1,128]{3,0,2,1:T(8,128)S(1)}, u32[]{:S(2)}, u32[]{:S(2)}) collective-permute-start(f32[8,10,1,128]{3,0,2,1:T(8,128)S(1)} %copy.1377), channel_id=1, source_target_pairs={{4,0},{6,2},{8,4},{10,6},{12,8},{14,10},{16,12},{18,14},{20,16},{2... | collective-permute-start | bytes 122888 | tf_op jit(solution)/shard_map/ppermute | solution.py:17
  42.9 17.1 %collective-permute-start.4 = (f32[8,10,10,1]{3,0,2,1:T(8,128)S(1)}, f32[8,10,10,1]{3,0,2,1:T(8,128)S(1)}, u32[]{:S(2)}, u32[]{:S(2)}) collective-permute-start(f32[8,10,10,1]{3,0,2,1:T(8,128)S(1)} %get-tuple-element.57), channel_id=1, source_target_pairs={{2,0},{4,2},{6,4},{8,6},{10,8},{12,10},{14,12},{16,14},{18,16},{20... | collective-permute-start | bytes 9608 | tf_op jit(solution)/shard_map/ppermute | solution.py:17
  55.4 9.5 %collective-permute-start.5 = (f32[8,10,10,1]{3,0,2,1:T(8,128)S(1)}, f32[8,10,10,1]{3,0,2,1:T(8,128)S(1)}, u32[]{:S(2)}, u32[]{:S(2)}) collective-permute-start(f32[8,10,10,1]{3,0,2,1:T(8,128)S(1)} %get-tuple-element.58), channel_id=1, source_target_pairs={{0,2},{2,4},{4,6},{6,8},{8,10},{10,12},{12,14},{14,16},{16,18},{18... | collective-permute-start | bytes 9608 | tf_op jit(solution)/shard_map/ppermute | solution.py:17
  69.7 13.4 %collective-permute-start.6 = (f32[8,1,8,128]{3,2,1,0:T(8,128)S(1)}, f32[8,1,8,128]{3,2,1,0:T(8,128)S(1)}, u32[]{:S(2)}, u32[]{:S(2)}) collective-permute-start(f32[8,1,8,128]{3,2,1,0:T(8,128)S(1)} %get-tuple-element.84), channel_id=1, source_target_pairs={{64,0},{66,2},{68,4},{70,6},{72,8},{74,10},{76,12},{78,14},{80,16}... | collective-permute-start | bytes 98312 | tf_op jit(solution)/shard_map/ppermute | solution.py:17
  93.9 20.2 %collective-permute-start.11 = (f32[8,10,10,1]{3,0,2,1:T(8,128)S(1)}, f32[8,10,10,1]{3,0,2,1:T(8,128)S(1)}, u32[]{:S(2)}, u32[]{:S(2)}) collective-permute-start(f32[8,10,10,1]{3,0,2,1:T(8,128)S(1)} %get-tuple-element.54), channel_id=1, source_target_pairs={{0,2},{2,4},{4,6},{6,8},{8,10},{10,12},{12,14},{14,16},{16,18},{18... | collective-permute-start | bytes 9608 | tf_op jit(solution)/shard_map/ppermute | solution.py:17
  105.0 10.8 %collective-permute-start.10 = (f32[8,10,10,1]{3,0,2,1:T(8,128)S(1)}, f32[8,10,10,1]{3,0,2,1:T(8,128)S(1)}, u32[]{:S(2)}, u32[]{:S(2)}) collective-permute-start(f32[8,10,10,1]{3,0,2,1:T(8,128)S(1)} %get-tuple-element.53), channel_id=1, source_target_pairs={{2,0},{4,2},{6,4},{8,6},{10,8},{12,10},{14,12},{16,14},{18,16},{20... | collective-permute-start | bytes 9608 | tf_op jit(solution)/shard_map/ppermute | solution.py:17
  117.2 18.0 %collective-permute-start.13 = (f32[8,1,8,128]{3,2,1,0:T(8,128)S(1)}, f32[8,1,8,128]{3,2,1,0:T(8,128)S(1)}, u32[]{:S(2)}, u32[]{:S(2)}) collective-permute-start(f32[8,1,8,128]{3,2,1,0:T(8,128)S(1)} %get-tuple-element.81), channel_id=1, source_target_pairs={{0,64},{2,66},{4,68},{6,70},{8,72},{10,74},{12,76},{14,78},{16,80}... | collective-permute-start | bytes 98312 | tf_op jit(solution)/shard_map/ppermute | solution.py:17
  133.8 13.7 %collective-permute-start.12 = (f32[8,1,8,128]{3,2,1,0:T(8,128)S(1)}, f32[8,1,8,128]{3,2,1,0:T(8,128)S(1)}, u32[]{:S(2)}, u32[]{:S(2)}) collective-permute-start(f32[8,1,8,128]{3,2,1,0:T(8,128)S(1)} %get-tuple-element.82), channel_id=1, source_target_pairs={{64,0},{66,2},{68,4},{70,6},{72,8},{74,10},{76,12},{78,14},{80,16}... | collective-permute-start | bytes 98312 | tf_op jit(solution)/shard_map/ppermute | solution.py:17
  155.5 10.4 %collective-permute-start.17 = (f32[8,10,10,1]{3,0,2,1:T(8,128)S(1)}, f32[8,10,10,1]{3,0,2,1:T(8,128)S(1)}, u32[]{:S(2)}, u32[]{:S(2)}) collective-permute-start(f32[8,10,10,1]{3,0,2,1:T(8,128)S(1)} %get-tuple-element.52), channel_id=1, source_target_pairs={{0,2},{2,4},{4,6},{6,8},{8,10},{10,12},{12,14},{14,16},{16,18},{18... | collective-permute-start | bytes 9608 | tf_op jit(solution)/shard_map/ppermute | solution.py:17
  161.2 10.8 %collective-permute-start.16 = (f32[8,10,10,1]{3,0,2,1:T(8,128)S(1)}, f32[8,10,10,1]{3,0,2,1:T(8,128)S(1)}, u32[]{:S(2)}, u32[]{:S(2)}) collective-permute-start(f32[8,10,10,1]{3,0,2,1:T(8,128)S(1)} %get-tuple-element.51), channel_id=1, source_target_pairs={{2,0},{4,2},{6,4},{8,6},{10,8},{12,10},{14,12},{16,14},{18,16},{20... | collective-permute-start | bytes 9608 | tf_op jit(solution)/shard_map/ppermute | solution.py:17
  181.2 11.7 %collective-permute-start.19 = (f32[8,1,4,64]{3,0,2,1:T(8,128)S(1)}, f32[8,1,4,64]{3,0,2,1:T(8,128)S(1)}, u32[]{:S(2)}, u32[]{:S(2)}) collective-permute-start(f32[8,1,4,64]{3,0,2,1:T(8,128)S(1)} %get-tuple-element.173), channel_id=1, source_target_pairs={{0,64},{2,66},{4,68},{6,70},{8,72},{10,74},{12,76},{14,78},{16,80}... | collective-permute-start | bytes 24584 | tf_op jit(solution)/shard_map/ppermute | solution.py:17
  191.6 13.2 %collective-permute-start.18 = (f32[8,1,4,64]{3,0,2,1:T(8,128)S(1)}, f32[8,1,4,64]{3,0,2,1:T(8,128)S(1)}, u32[]{:S(2)}, u32[]{:S(2)}) collective-permute-start(f32[8,1,4,64]{3,0,2,1:T(8,128)S(1)} %get-tuple-element.174), channel_id=1, source_target_pairs={{64,0},{66,2},{68,4},{70,6},{72,8},{74,10},{76,12},{78,14},{80,16}... | collective-permute-start | bytes 24584 | tf_op jit(solution)/shard_map/ppermute | solution.py:17
  212.3 8.7 %collective-permute-start.22 = (f32[8,6,6,1]{3,0,2,1:T(8,128)S(1)}, f32[8,6,6,1]{3,0,2,1:T(8,128)S(1)}, u32[]{:S(2)}, u32[]{:S(2)}) collective-permute-start(f32[8,6,6,1]{3,0,2,1:T(8,128)S(1)} %get-tuple-element.101), channel_id=1, source_target_pairs={{2,0},{4,2},{6,4},{8,6},{10,8},{12,10},{14,12},{16,14},{18,16},{20... | collective-permute-start | bytes 3464 | tf_op jit(solution)/shard_map/ppermute | solution.py:17
  222.5 15.5 %collective-permute-start.25 = (f32[8,1,4,64]{3,0,2,1:T(8,128)S(1)}, f32[8,1,4,64]{3,0,2,1:T(8,128)S(1)}, u32[]{:S(2)}, u32[]{:S(2)}) collective-permute-start(f32[8,1,4,64]{3,0,2,1:T(8,128)S(1)} %get-tuple-element.171), channel_id=1, source_target_pairs={{0,64},{2,66},{4,68},{6,70},{8,72},{10,74},{12,76},{14,78},{16,80}... | collective-permute-start | bytes 24584 | tf_op jit(solution)/shard_map/ppermute | solution.py:17
  236.7 13.2 %collective-permute-start.24 = (f32[8,1,4,64]{3,0,2,1:T(8,128)S(1)}, f32[8,1,4,64]{3,0,2,1:T(8,128)S(1)}, u32[]{:S(2)}, u32[]{:S(2)}) collective-permute-start(f32[8,1,4,64]{3,0,2,1:T(8,128)S(1)} %get-tuple-element.172), channel_id=1, source_target_pairs={{64,0},{66,2},{68,4},{70,6},{72,8},{74,10},{76,12},{78,14},{80,16}... | collective-permute-start | bytes 24584 | tf_op jit(solution)/shard_map/ppermute | solution.py:17
  251.2 6.4 %collective-permute-start.26 = (f32[8,6,1,64]{3,0,2,1:T(8,128)S(1)}, f32[8,6,1,64]{3,0,2,1:T(8,128)S(1)}, u32[]{:S(2)}, u32[]{:S(2)}) collective-permute-start(f32[8,6,1,64]{3,0,2,1:T(8,128)S(1)} %get-tuple-element.114), channel_id=1, source_target_pairs={{4,0},{6,2},{8,4},{10,6},{12,8},{14,10},{16,12},{18,14},{20,16},{2... | collective-permute-start | bytes 36872 | tf_op jit(solution)/shard_map/ppermute | solution.py:17
  257.7 13.8 %collective-permute-start.28 = (f32[8,6,6,1]{3,0,2,1:T(8,128)S(1)}, f32[8,6,6,1]{3,0,2,1:T(8,128)S(1)}, u32[]{:S(2)}, u32[]{:S(2)}) collective-permute-start(f32[8,6,6,1]{3,0,2,1:T(8,128)S(1)} %get-tuple-element.97), channel_id=1, source_target_pairs={{2,0},{4,2},{6,4},{8,6},{10,8},{12,10},{14,12},{16,14},{18,16},{20... | collective-permute-start | bytes 3464 | tf_op jit(solution)/shard_map/ppermute | solution.py:17
  274.4 10.2 %collective-permute-start.31 = (f32[8,1,2,32]{0,3,2,1:T(8,128)S(1)}, f32[8,1,2,32]{0,3,2,1:T(8,128)S(1)}, u32[]{:S(2)}, u32[]{:S(2)}) collective-permute-start(f32[8,1,2,32]{0,3,2,1:T(8,128)S(1)} %get-tuple-element.169), channel_id=1, source_target_pairs={{0,64},{2,66},{4,68},{6,70},{8,72},{10,74},{12,76},{14,78},{16,80}... | collective-permute-start | bytes 6152 | tf_op jit(solution)/shard_map/ppermute | solution.py:17
  283.4 13.4 %collective-permute-start.30 = (f32[8,1,2,32]{0,3,2,1:T(8,128)S(1)}, f32[8,1,2,32]{0,3,2,1:T(8,128)S(1)}, u32[]{:S(2)}, u32[]{:S(2)}) collective-permute-start(f32[8,1,2,32]{0,3,2,1:T(8,128)S(1)} %get-tuple-element.170), channel_id=1, source_target_pairs={{64,0},{66,2},{68,4},{70,6},{72,8},{74,10},{76,12},{78,14},{80,16}... | collective-permute-start | bytes 6152 | tf_op jit(solution)/shard_map/ppermute | solution.py:17
  298.1 6.3 %collective-permute-start.32 = (f32[8,4,1,32]{3,0,2,1:T(8,128)S(1)}, f32[8,4,1,32]{3,0,2,1:T(8,128)S(1)}, u32[]{:S(2)}, u32[]{:S(2)}) collective-permute-start(f32[8,4,1,32]{3,0,2,1:T(8,128)S(1)} %get-tuple-element.204), channel_id=1, source_target_pairs={{4,0},{6,2},{8,4},{10,6},{12,8},{14,10},{16,12},{18,14},{20,16},{2... | collective-permute-start | bytes 12296 | tf_op jit(solution)/shard_map/ppermute | solution.py:17
  304.5 13.4 %collective-permute-start.34 = (f32[8,4,4,1]{3,0,2,1:T(8,128)S(1)}, f32[8,4,4,1]{3,0,2,1:T(8,128)S(1)}, u32[]{:S(2)}, u32[]{:S(2)}) collective-permute-start(f32[8,4,4,1]{3,0,2,1:T(8,128)S(1)} %get-tuple-element.167), channel_id=1, source_target_pairs={{2,0},{4,2},{6,4},{8,6},{10,8},{12,10},{14,12},{16,14},{18,16},{20... | collective-permute-start | bytes 1544 | tf_op jit(solution)/shard_map/ppermute | solution.py:17
  319.9 14.5 %collective-permute-start.37 = (f32[8,1,2,32]{0,3,2,1:T(8,128)S(1)}, f32[8,1,2,32]{0,3,2,1:T(8,128)S(1)}, u32[]{:S(2)}, u32[]{:S(2)}) collective-permute-start(f32[8,1,2,32]{0,3,2,1:T(8,128)S(1)} %get-tuple-element.153), channel_id=1, source_target_pairs={{0,64},{2,66},{4,68},{6,70},{8,72},{10,74},{12,76},{14,78},{16,80}... | collective-permute-start | bytes 6152 | tf_op jit(solution)/shard_map/ppermute | solution.py:17
  333.2 13.4 %collective-permute-start.36 = (f32[8,1,2,32]{0,3,2,1:T(8,128)S(1)}, f32[8,1,2,32]{0,3,2,1:T(8,128)S(1)}, u32[]{:S(2)}, u32[]{:S(2)}) collective-permute-start(f32[8,1,2,32]{0,3,2,1:T(8,128)S(1)} %get-tuple-element.154), channel_id=1, source_target_pairs={{64,0},{66,2},{68,4},{70,6},{72,8},{74,10},{76,12},{78,14},{80,16}... | collective-permute-start | bytes 6152 | tf_op jit(solution)/shard_map/ppermute | solution.py:17
  347.9 6.3 %collective-permute-start.38 = (f32[8,4,1,32]{3,0,2,1:T(8,128)S(1)}, f32[8,4,1,32]{3,0,2,1:T(8,128)S(1)}, u32[]{:S(2)}, u32[]{:S(2)}) collective-permute-start(f32[8,4,1,32]{3,0,2,1:T(8,128)S(1)} %get-tuple-element.200), channel_id=1, source_target_pairs={{4,0},{6,2},{8,4},{10,6},{12,8},{14,10},{16,12},{18,14},{20,16},{2... | collective-permute-start | bytes 12296 | tf_op jit(solution)/shard_map/ppermute | solution.py:17
  354.3 13.3 %collective-permute-start.40 = (f32[8,4,4,1]{3,0,2,1:T(8,128)S(1)}, f32[8,4,4,1]{3,0,2,1:T(8,128)S(1)}, u32[]{:S(2)}, u32[]{:S(2)}) collective-permute-start(f32[8,4,4,1]{3,0,2,1:T(8,128)S(1)} %get-tuple-element.151), channel_id=1, source_target_pairs={{2,0},{4,2},{6,4},{8,6},{10,8},{12,10},{14,12},{16,14},{18,16},{20... | collective-permute-start | bytes 1544 | tf_op jit(solution)/shard_map/ppermute | solution.py:17
  369.6 11.2 %collective-permute-start.43 = (f32[8,1,2,32]{0,3,2,1:T(8,128)S(1)}, f32[8,1,2,32]{0,3,2,1:T(8,128)S(1)}, u32[]{:S(2)}, u32[]{:S(2)}) collective-permute-start(f32[8,1,2,32]{0,3,2,1:T(8,128)S(1)} %get-tuple-element.137), channel_id=1, source_target_pairs={{0,64},{2,66},{4,68},{6,70},{8,72},{10,74},{12,76},{14,78},{16,80}... | collective-permute-start | bytes 6152 | tf_op jit(solution)/shard_map/ppermute | solution.py:17
  379.5 13.4 %collective-permute-start.42 = (f32[8,1,2,32]{0,3,2,1:T(8,128)S(1)}, f32[8,1,2,32]{0,3,2,1:T(8,128)S(1)}, u32[]{:S(2)}, u32[]{:S(2)}) collective-permute-start(f32[8,1,2,32]{0,3,2,1:T(8,128)S(1)} %get-tuple-element.138), channel_id=1, source_target_pairs={{64,0},{66,2},{68,4},{70,6},{72,8},{74,10},{76,12},{78,14},{80,16}... | collective-permute-start | bytes 6152 | tf_op jit(solution)/shard_map/ppermute | solution.py:17
  394.3 6.3 %collective-permute-start.44 = (f32[8,4,1,32]{3,0,2,1:T(8,128)S(1)}, f32[8,4,1,32]{3,0,2,1:T(8,128)S(1)}, u32[]{:S(2)}, u32[]{:S(2)}) collective-permute-start(f32[8,4,1,32]{3,0,2,1:T(8,128)S(1)} %get-tuple-element.196), channel_id=1, source_target_pairs={{4,0},{6,2},{8,4},{10,6},{12,8},{14,10},{16,12},{18,14},{20,16},{2... | collective-permute-start | bytes 12296 | tf_op jit(solution)/shard_map/ppermute | solution.py:17
  400.7 13.3 %collective-permute-start.46 = (f32[8,4,4,1]{3,0,2,1:T(8,128)S(1)}, f32[8,4,4,1]{3,0,2,1:T(8,128)S(1)}, u32[]{:S(2)}, u32[]{:S(2)}) collective-permute-start(f32[8,4,4,1]{3,0,2,1:T(8,128)S(1)} %get-tuple-element.135), channel_id=1, source_target_pairs={{2,0},{4,2},{6,4},{8,6},{10,8},{12,10},{14,12},{16,14},{18,16},{20... | collective-permute-start | bytes 1544 | tf_op jit(solution)/shard_map/ppermute | solution.py:17
  416.4 7.8 %collective-permute-start.49 = (f32[8,1,4,64]{3,0,2,1:T(8,128)S(1)}, f32[8,1,4,64]{3,0,2,1:T(8,128)S(1)}, u32[]{:S(2)}, u32[]{:S(2)}) collective-permute-start(f32[8,1,4,64]{3,0,2,1:T(8,128)S(1)} %get-tuple-element.121), channel_id=1, source_target_pairs={{0,64},{2,66},{4,68},{6,70},{8,72},{10,74},{12,76},{14,78},{16,80}... | collective-permute-start | bytes 24584 | tf_op jit(solution)/shard_map/ppermute | solution.py:17
  422.9 13.2 %collective-permute-start.48 = (f32[8,1,4,64]{3,0,2,1:T(8,128)S(1)}, f32[8,1,4,64]{3,0,2,1:T(8,128)S(1)}, u32[]{:S(2)}, u32[]{:S(2)}) collective-permute-start(f32[8,1,4,64]{3,0,2,1:T(8,128)S(1)} %get-tuple-element.122), channel_id=1, source_target_pairs={{64,0},{66,2},{68,4},{70,6},{72,8},{74,10},{76,12},{78,14},{80,16}... | collective-permute-start | bytes 24584 | tf_op jit(solution)/shard_map/ppermute | solution.py:17
  437.4 6.4 %collective-permute-start.50 = (f32[8,6,1,64]{3,0,2,1:T(8,128)S(1)}, f32[8,6,1,64]{3,0,2,1:T(8,128)S(1)}, u32[]{:S(2)}, u32[]{:S(2)}) collective-permute-start(f32[8,6,1,64]{3,0,2,1:T(8,128)S(1)} %get-tuple-element.110), channel_id=1, source_target_pairs={{4,0},{6,2},{8,4},{10,6},{12,8},{14,10},{16,12},{18,14},{20,16},{2... | collective-permute-start | bytes 36872 | tf_op jit(solution)/shard_map/ppermute | solution.py:17
  443.9 13.0 %collective-permute-start.52 = (f32[8,6,6,1]{3,0,2,1:T(8,128)S(1)}, f32[8,6,6,1]{3,0,2,1:T(8,128)S(1)}, u32[]{:S(2)}, u32[]{:S(2)}) collective-permute-start(f32[8,6,6,1]{3,0,2,1:T(8,128)S(1)} %get-tuple-element.93), channel_id=1, source_target_pairs={{2,0},{4,2},{6,4},{8,6},{10,8},{12,10},{14,12},{16,14},{18,16},{20... | collective-permute-start | bytes 3464 | tf_op jit(solution)/shard_map/ppermute | solution.py:17
  459.2 8.0 %collective-permute-start.55 = (f32[8,1,4,64]{3,0,2,1:T(8,128)S(1)}, f32[8,1,4,64]{3,0,2,1:T(8,128)S(1)}, u32[]{:S(2)}, u32[]{:S(2)}) collective-permute-start(f32[8,1,4,64]{3,0,2,1:T(8,128)S(1)} %get-tuple-element.119), channel_id=1, source_target_pairs={{0,64},{2,66},{4,68},{6,70},{8,72},{10,74},{12,76},{14,78},{16,80}... | collective-permute-start | bytes 24584 | tf_op jit(solution)/shard_map/ppermute | solution.py:17
  465.9 13.2 %collective-permute-start.54 = (f32[8,1,4,64]{3,0,2,1:T(8,128)S(1)}, f32[8,1,4,64]{3,0,2,1:T(8,128)S(1)}, u32[]{:S(2)}, u32[]{:S(2)}) collective-permute-start(f32[8,1,4,64]{3,0,2,1:T(8,128)S(1)} %get-tuple-element.120), channel_id=1, source_target_pairs={{64,0},{66,2},{68,4},{70,6},{72,8},{74,10},{76,12},{78,14},{80,16}... | collective-permute-start | bytes 24584 | tf_op jit(solution)/shard_map/ppermute | solution.py:17
  480.4 6.4 %collective-permute-start.56 = (f32[8,6,1,64]{3,0,2,1:T(8,128)S(1)}, f32[8,6,1,64]{3,0,2,1:T(8,128)S(1)}, u32[]{:S(2)}, u32[]{:S(2)}) collective-permute-start(f32[8,6,1,64]{3,0,2,1:T(8,128)S(1)} %get-tuple-element.106), channel_id=1, source_target_pairs={{4,0},{6,2},{8,4},{10,6},{12,8},{14,10},{16,12},{18,14},{20,16},{2... | collective-permute-start | bytes 36872 | tf_op jit(solution)/shard_map/ppermute | solution.py:17
  486.9 13.3 %collective-permute-start.58 = (f32[8,6,6,1]{3,0,2,1:T(8,128)S(1)}, f32[8,6,6,1]{3,0,2,1:T(8,128)S(1)}, u32[]{:S(2)}, u32[]{:S(2)}) collective-permute-start(f32[8,6,6,1]{3,0,2,1:T(8,128)S(1)} %get-tuple-element.89), channel_id=1, source_target_pairs={{2,0},{4,2},{6,4},{8,6},{10,8},{12,10},{14,12},{16,14},{18,16},{20... | collective-permute-start | bytes 3464 | tf_op jit(solution)/shard_map/ppermute | solution.py:17
  508.5 8.1 %collective-permute-start.61 = (f32[8,1,8,128]{3,2,1,0:T(8,128)S(1)}, f32[8,1,8,128]{3,2,1,0:T(8,128)S(1)}, u32[]{:S(2)}, u32[]{:S(2)}) collective-permute-start(f32[8,1,8,128]{3,2,1,0:T(8,128)S(1)} %get-tuple-element.79), channel_id=1, source_target_pairs={{0,64},{2,66},{4,68},{6,70},{8,72},{10,74},{12,76},{14,78},{16,80}... | collective-permute-start | bytes 98312 | tf_op jit(solution)/shard_map/ppermute | solution.py:17
  515.3 13.4 %collective-permute-start.60 = (f32[8,1,8,128]{3,2,1,0:T(8,128)S(1)}, f32[8,1,8,128]{3,2,1,0:T(8,128)S(1)}, u32[]{:S(2)}, u32[]{:S(2)}) collective-permute-start(f32[8,1,8,128]{3,2,1,0:T(8,128)S(1)} %get-tuple-element.80), channel_id=1, source_target_pairs={{64,0},{66,2},{68,4},{70,6},{72,8},{74,10},{76,12},{78,14},{80,16}... | collective-permute-start | bytes 98312 | tf_op jit(solution)/shard_map/ppermute | solution.py:17
  530.1 6.4 %collective-permute-start.62 = (f32[8,10,1,128]{3,0,2,1:T(8,128)S(1)}, f32[8,10,1,128]{3,0,2,1:T(8,128)S(1)}, u32[]{:S(2)}, u32[]{:S(2)}) collective-permute-start(f32[8,10,1,128]{3,0,2,1:T(8,128)S(1)} %copy.1485), channel_id=1, source_target_pairs={{4,0},{6,2},{8,4},{10,6},{12,8},{14,10},{16,12},{18,14},{20,16},{2... | collective-permute-start | bytes 122888 | tf_op jit(solution)/shard_map/ppermute | solution.py:17
  536.7 19.7 %collective-permute-start.65 = (f32[8,10,10,1]{3,0,2,1:T(8,128)S(1)}, f32[8,10,10,1]{3,0,2,1:T(8,128)S(1)}, u32[]{:S(2)}, u32[]{:S(2)}) collective-permute-start(f32[8,10,10,1]{3,0,2,1:T(8,128)S(1)} %get-tuple-element.50), channel_id=1, source_target_pairs={{0,2},{2,4},{4,6},{6,8},{8,10},{10,12},{12,14},{14,16},{16,18},{18... | collective-permute-start | bytes 9608 | tf_op jit(solution)/shard_map/ppermute | solution.py:17
  547.3 10.8 %collective-permute-start.64 = (f32[8,10,10,1]{3,0,2,1:T(8,128)S(1)}, f32[8,10,10,1]{3,0,2,1:T(8,128)S(1)}, u32[]{:S(2)}, u32[]{:S(2)}) collective-permute-start(f32[8,10,10,1]{3,0,2,1:T(8,128)S(1)} %get-tuple-element.49), channel_id=1, source_target_pairs={{2,0},{4,2},{6,4},{8,6},{10,8},{12,10},{14,12},{16,14},{18,16},{20... | collective-permute-start | bytes 9608 | tf_op jit(solution)/shard_map/ppermute | solution.py:17
  559.5 10.6 %collective-permute-start.67 = (f32[8,1,8,128]{3,2,1,0:T(8,128)S(1)}, f32[8,1,8,128]{3,2,1,0:T(8,128)S(1)}, u32[]{:S(2)}, u32[]{:S(2)}) collective-permute-start(f32[8,1,8,128]{3,2,1,0:T(8,128)S(1)} %get-tuple-element.77), channel_id=1, source_target_pairs={{0,64},{2,66},{4,68},{6,70},{8,72},{10,74},{12,76},{14,78},{16,80}... | collective-permute-start | bytes 98312 | tf_op jit(solution)/shard_map/ppermute | solution.py:17
  568.6 13.4 %collective-permute-start.66 = (f32[8,1,8,128]{3,2,1,0:T(8,128)S(1)}, f32[8,1,8,128]{3,2,1,0:T(8,128)S(1)}, u32[]{:S(2)}, u32[]{:S(2)}) collective-permute-start(f32[8,1,8,128]{3,2,1,0:T(8,128)S(1)} %get-tuple-element.78), channel_id=1, source_target_pairs={{64,0},{66,2},{68,4},{70,6},{72,8},{74,10},{76,12},{78,14},{80,16}... | collective-permute-start | bytes 98312 | tf_op jit(solution)/shard_map/ppermute | solution.py:17
  589.9 15.1 %collective-permute-start.71 = (f32[8,10,10,1]{3,0,2,1:T(8,128)S(1)}, f32[8,10,10,1]{3,0,2,1:T(8,128)S(1)}, u32[]{:S(2)}, u32[]{:S(2)}) collective-permute-start(f32[8,10,10,1]{3,0,2,1:T(8,128)S(1)} %get-tuple-element.48), channel_id=1, source_target_pairs={{0,2},{2,4},{4,6},{6,8},{8,10},{10,12},{12,14},{14,16},{16,18},{18... | collective-permute-start | bytes 9608 | tf_op jit(solution)/shard_map/ppermute | solution.py:17
  595.9 10.8 %collective-permute-start.70 = (f32[8,10,10,1]{3,0,2,1:T(8,128)S(1)}, f32[8,10,10,1]{3,0,2,1:T(8,128)S(1)}, u32[]{:S(2)}, u32[]{:S(2)}) collective-permute-start(f32[8,10,10,1]{3,0,2,1:T(8,128)S(1)} %get-tuple-element.47), channel_id=1, source_target_pairs={{2,0},{4,2},{6,4},{8,6},{10,8},{12,10},{14,12},{16,14},{18,16},{20... | collective-permute-start | bytes 9608 | tf_op jit(solution)/shard_map/ppermute | solution.py:17
  (26 other events, 224.8 us)
where the time goes:
time: 611 us; the launch traced here: 609 us
  starting transfers between devices  309 us (51%)
  waiting for transfers between devices  251 us (41%)
  local copies, waits for them, and re-layouts  19.9 us (3%)
  other arithmetic  19.1 us (3%)
  blocking collectives  7 us (1%)
    ppermute x72, starting transfers between devices, from_behind(): lax.ppermute(value, axis, [(source, source + steps) for source in range(i...  309 us
    ppermute x72, waiting for transfers between devices, from_behind(): lax.ppermute(value, axis, [(source, source + steps) for source in range(i...  251 us
  transfers between devices with their start and end apart: 72, of which 44 were waited for; matrix products, arithmetic and copies ran while one was open for 1% of the time, Pallas kernels for 0%

commit v1 on v0

v1 whole, which is shorter than its diff:
```python
import jax
import jax.numpy as jnp
from jax import lax
from jax.experimental import pallas as pl
from jax.experimental.pallas import tpu as pltpu
from jax.sharding import PartitionSpec as P


OMEGA = 0.7
KEEP = 0.3
FINE, MIDDLE, COARSE = 2.0, 0.5, 0.125
PX, PZ = 8, 2
REACH = 3
F32 = jnp.float32
HIGHEST = lax.Precision.HIGHEST


def place():
    position = lax.axis_index("dom")
    size_y = lax.axis_size("dom") // (PX * PZ)
    return position // (size_y * PZ), position // PZ % size_y, position % PZ


def dom_of(px, py, pz, size_y):
    return (px * size_y + py) * PZ + pz


def iota(shape, dimension):
    return lax.broadcasted_iota(jnp.int32, shape, dimension)


def along_x(planes):
    sublane = iota(planes[0].shape, 0)
    first = jnp.where(sublane == 0, 0.0, pltpu.roll(planes[-1], 1, 0))
    last = jnp.where(sublane == PX - 1, 0.0, pltpu.roll(planes[0], PX - 1, 0))
    below = [first] + planes[:-1]
    above = planes[1:] + [last]
    return [b + a for b, a in zip(below, above)]


def along_z(plane, open_end):
    width = plane.shape[1]
    left, right = pltpu.roll(plane, 1, 1), pltpu.roll(plane, width - 1, 1)
    if not open_end:
        lane = iota(plane.shape, 1)
        left = jnp.where(lane == 0, 0.0, left)
        right = jnp.where(lane == width - 1, 0.0, right)
    return left + right


def stencil(below, here, above, open_end=False):
    across = [a + b for a, b in zip(below, above)]
    wide = [a + (h + h) for a, h in zip(across, here)]
    turned = [e + w for e, w in zip(along_x(here), wide)]
    return [
        along_z(t, open_end) + (x + (a + a)) for t, x, a in zip(turned, along_x(wide), across)
    ]


def each(count, chunk, step):
    whole = count // chunk

    def body(index, carry):
        step(index * chunk, chunk)
        return carry

    if whole == 1:
        step(0, chunk)
    else:
        lax.fori_loop(0, whole, body, 0)
    if count % chunk:
        step(whole * chunk, count % chunk)


def take(ref, row):
    return [ref[row, i] for i in range(ref.shape[1])]


def sweep_row(rows, source, inverse, kinetic, open_end=False):
    total = stencil(*rows, open_end)
    return [
        KEEP * u + v * (s + (kinetic / 6.0) * t)
        for u, s, v, t in zip(rows[1], source, inverse, total)
    ]


def sweep(start, source, inverse, target, kinetic, count, chunk, offsets, open_end=False):
    to, of, at = offsets

    def step(base, rows):
        held = [take(start, base + (of + r - 1)) for r in range(rows + 2)]
        for r in range(rows):
            row = base + (at + r)
            new = sweep_row(held[r : r + 3], take(source, row), take(inverse, row), kinetic, open_end)
            for i, plane in enumerate(new):
                target[base + (to + r), i] = plane

    each(count, chunk, step)


def pooling(rows, columns):
    return jnp.where(iota((rows, columns), 0) // 2 == iota((rows, columns), 1), 0.5, 0.0).astype(F32)


def spreading(rows, columns):
    return jnp.where(iota((rows, columns), 0) == iota((rows, columns), 1) // 2, 1.0, 0.0).astype(F32)


def times(value, matrix):
    return jnp.dot(value, matrix, precision=HIGHEST, preferred_element_type=F32)


def cubes(low, high):
    return [
        0.25 * ((low[2 * i] + low[2 * i + 1]) + (high[2 * i] + high[2 * i + 1]))
        for i in range(len(low) // 2)
    ]


def pack(residual, own, mate, out):
    band = lax.axis_index("band")
    planes = [jnp.where(band == 0, own[i], mate[i]) for i in range(4)]
    planes += [jnp.where(band == 0, mate[i], own[i]) for i in range(4)]
    for c in range(PZ):
        rows = slice(4 * c, 4 * c + 4)
        for p in range(4):
            both = jnp.concatenate([planes[2 * p][rows], planes[2 * p + 1][rows]], axis=0)
            for orbital in range(PX):
                base = (orbital * PZ + c) * 64 + p * 8
                out[base : base + 4] = residual[orbital, 2 * p, rows]
                out[base + 4 : base + 8] = residual[orbital, 2 * p + 1, rows]
                out[base + 32 : base + 40] = both


def down(shifts, own, mate, beside, fine_out, source_out, inverse_out, cut, field, potential, source, inverse, start):
    px, py, c = place()
    size_y = lax.axis_size("dom") // (PX * PZ)
    shift = shifts[px]

    def unpack(blocks):
        for row in range(12):
            ref = blocks[row // 4]
            for i in range(8):
                at = (i // 2) * 8 + (i % 2) * 4 + row % 4
                for half in range(PZ):
                    lanes = slice(128 * half, 128 * half + 128)
                    field[row, i, :, lanes] = ref[pl.ds(half * 64 + at, PX, stride=128), :]
                    if 1 <= row <= 10:
                        potential[row - 1, i, :, lanes] = ref[pl.ds(half * 64 + 32 + at, PX, stride=128), :]

    pl.when(c == 0)(lambda: unpack((beside, own, mate)))
    pl.when(c == 1)(lambda: unpack((mate, own, beside)))

    def first(base, rows):
        for r in range(rows):
            row = base + r
            y = py * 8 + 4 * c + row - 3
            inside = jnp.where((y >= 0) & (y < 8 * size_y), OMEGA, 0.0).astype(F32)
            below, here, above = [take(field, row + d) for d in range(3)]
            for i, (b, h, a, x) in enumerate(zip(below, here, above, along_x(here))):
                s = 0.5 * h + ((b + a) + (x + along_z(h, False))) * (1.0 / 12.0)
                v = inside / (potential[row, i] + (4.0 * FINE + shift))
                source[row, i] = s
                inverse[row, i] = v
                start[row, i] = v * s

    each(10, 2, first)
    sweep(start, source, inverse, fine_out, FINE, 8, 2, (0, 1, 1))

    def keep(base, rows):
        for r in range(rows):
            for i in range(8):
                source_out[base + r, i] = source[base + (r + 2), i]
                inverse_out[base + r, i] = inverse[base + (r + 2), i]

    each(6, 2, keep)
    pool = pooling(256, 128)
    for pair in range(2):
        left = []
        for row in (2 * pair, 2 * pair + 1):
            rows = [take(fine_out, row + d) for d in (1, 2, 3)]
            weight = [v + (4.0 * FINE + shift) for v in take(potential, row + 3)]
            total = stencil(*rows)
            left.append(
                [s + (FINE / 6.0) * t - w * u for s, t, w, u in zip(take(source, row + 3), total, weight, rows[1])]
            )
        mean = cubes(*left) + cubes(take(potential, 2 * pair + 3), take(potential, 2 * pair + 4))
        small = times(jnp.concatenate(mean, axis=0), pool)
        for i in range(8):
            cut[pair, i] = small[8 * i : 8 * i + 8]


def up(shifts, fine, source, inverse, block, around, out, weight1, source1, inverse1, middle, other, source2, inverse2, coarse, coarser, work):
    px, py, c = place()
    size_y = lax.axis_size("dom") // (PX * PZ)
    shift = shifts[px]

    def inside(distance):
        return jnp.where((py + distance >= 0) & (py + distance < size_y), OMEGA, 0.0).astype(F32)

    for row in range(28):
        distance = row // 4 - REACH
        if distance == 0:
            at = lambda i: block[row % 4, i]
        else:
            side, step = (0, -distance - 1) if distance < 0 else (1, distance - 1)
            at = lambda i: around[side, step, row % 4, i]
        for i in range(4):
            s = at(i)
            w = at(4 + i) + (4.0 * MIDDLE + shift)
            v = inside(distance) / w
            source1[row, i] = s
            weight1[row, i] = w
            inverse1[row, i] = v
            other[row, i] = v * s

    sweep(other, source1, inverse1, middle, MIDDLE, 26, 4, (1, 1, 1))

    pool = pooling(128, 128)
    spread = spreading(128, 128)
    lane = iota((8, 128), 1)

    def shrink(base, pairs):
        for pair in range(pairs):
            low = 2 * base + (2 * pair + 2)
            left, weights = [], []
            for row in (low, low + 1):
                rows = [take(middle, row + d) for d in (-1, 0, 1)]
                w = take(weight1, row)
                total = stencil(*rows)
                left.append(
                    [s + (MIDDLE / 6.0) * t - x * u for s, t, x, u in zip(take(source1, row), total, w, rows[1])]
                )
                weights.append(w)
            mean = cubes(*left) + cubes(*weights)
            small = times(jnp.concatenate(mean, axis=0), pool)
            distance = (base + (pair + 1)) // 2 - REACH
            for i in range(2):
                s = small[8 * i : 8 * i + 8]
                w = small[16 + 8 * i : 24 + 8 * i] + (4.0 * COARSE - 4.0 * MIDDLE)
                v = jnp.where(lane < 64, inside(distance) / jnp.where(lane < 64, w, 1.0), 0.0)
                source2[base + pair, i] = s
                inverse2[base + pair, i] = v
                coarse[base + pair, i] = v * s

    each(12, 4, shrink)
    sweep(coarse, source2, inverse2, coarser, COARSE, 10, 10, (1, 1, 1), True)
    sweep(coarser, source2, inverse2, coarse, COARSE, 8, 8, (2, 2, 2), True)
    sweep(coarse, source2, inverse2, coarser, COARSE, 6, 6, (3, 3, 3), True)

    for row in range(3, 9):
        wide = times(jnp.concatenate(take(coarser, row), axis=0), spread)
        for fine_row in (2 * row + 2, 2 * row + 3):
            for i in range(4):
                other[fine_row, i] = middle[fine_row, i] + wide[8 * (i // 2) : 8 * (i // 2) + 8]

    sweep(other, source1, inverse1, middle, MIDDLE, 8, 4, (10, 10, 10))
    sweep(middle, source1, inverse1, other, MIDDLE, 6, 6, (11, 11, 11))

    spread = spreading(128, 256)
    for row in range(4):
        wide = times(jnp.concatenate(take(other, 11 + 2 * c + row), axis=0), spread)
        for fine_row in (2 * row, 2 * row + 1):
            for i in range(8):
                work[fine_row, i] = fine[fine_row, i] + wide[8 * (i // 2) : 8 * (i // 2) + 8]

    final = work.at[8:14]
    sweep(work, source, inverse, final, FINE, 6, 2, (0, 1, 0))
    for row in range(4):
        new = sweep_row(
            [take(final, row + d) for d in range(3)], take(source, row + 1), take(inverse, row + 1), FINE
        )
        for i, plane in enumerate(new):
            at = (i // 2) * 8 + (i % 2) * 4 + row
            for half in range(PZ):
                out[pl.ds(half * 32 + at, PX, stride=64), :] = plane[:, 128 * half : 128 * half + 128]


def unpack(blocks, out):
    for orbital in range(PX):
        for c in range(PZ):
            for i in range(8):
                base = (orbital * PZ + c) * 32 + (i // 2) * 8 + (i % 2) * 4
                out[orbital, i, 4 * c : 4 * c + 4] = blocks[base : base + 4]


def call(kernel, outs, scratch=(), smem=False):
    shapes = [jax.ShapeDtypeStruct(shape, F32) for shape in outs]
    specs = [pl.BlockSpec(memory_space=pltpu.VMEM)] * len(outs)

    def run(*args):
        given = [pl.BlockSpec(memory_space=pltpu.VMEM)] * len(args)
        if smem:
            given[0] = pl.BlockSpec(memory_space=pltpu.SMEM)
        return pl.pallas_call(
            kernel,
            out_shape=shapes,
            in_specs=given,
            out_specs=specs,
            scratch_shapes=[pltpu.VMEM(shape, F32) for shape in scratch],
            compiler_params=pltpu.CompilerParams(vmem_limit_bytes=40 * 1024 * 1024),
        )(*args)

    return run


def body(residual, potential, shifts):
    size_y = lax.axis_size("dom") // (PX * PZ)
    blocks = [(px, py, c) for px in range(PX) for py in range(size_y) for c in range(PZ)]
    lines = [
        [dom_of(px, py, c, size_y) for px in range(PX) for c in range(PZ)] for py in range(size_y)
    ]
    cores = [
        [dom_of(px, py, c, size_y) for c in range(PZ)] for px in range(PX) for py in range(size_y)
    ]

    def pairs(target):
        found = [((px, py, c), target(px, py, c)) for px, py, c in blocks]
        return [
            (dom_of(*a, size_y), dom_of(*b, size_y)) for a, b in found if 0 <= b[1] < size_y
        ]

    def swap_lines(value):
        return lax.all_to_all(value, "dom", 0, 0, axis_index_groups=lines, tiled=True)

    mate_planes = lax.ppermute(potential, "band", [(0, 1), (1, 0)])
    (packed,) = call(pack, [(1024, 128)])(residual, potential, mate_planes)
    own = swap_lines(packed)
    beside = lax.ppermute(
        own, "dom", pairs(lambda px, py, c: (px, py - 1, 1) if c == 0 else (px, py + 1, 0))
    )
    mate = lax.ppermute(own, "dom", pairs(lambda px, py, c: (px, py, 1 - c)))
    fine, source, inverse, cut = call(
        down,
        [(8, 8, 8, 256), (6, 8, 8, 256), (6, 8, 8, 256), (2, 8, 8, 128)],
        [(12, 8, 8, 256)] + [(10, 8, 8, 256)] * 4,
        smem=True,
    )(shifts, own, mate, beside)
    block = lax.all_gather(cut, "dom", axis_index_groups=cores, axis=0, tiled=True)
    sent = [
        lax.ppermute(
            block,
            "dom",
            pairs(lambda px, py, c, k=k: (px, py + k, 0) if c == 0 else (px, py - k, 1)),
        )
        for k in range(1, REACH + 1)
    ]
    around = lax.all_gather(jnp.stack(sent), "dom", axis_index_groups=cores, axis=0)
    (final,) = call(
        up,
        [(512, 128)],
        [(28, 4, 8, 128)] * 5 + [(12, 2, 8, 128)] * 4 + [(14, 8, 8, 256)],
        smem=True,
    )(shifts, fine, source, inverse, block, around)
    (correction,) = call(unpack, [(8, 8, 8, 128)])(swap_lines(final))
    return correction


def solution(mesh):
    return jax.shard_map(
        body,
        mesh=mesh,
        in_specs=(P("band", "dom", None, None), P(("dom", "band"), None, None), P("band")),
        out_specs=P("band", "dom", None, None),
        check_vma=False,
    )
```

time: 611 us -> 133 us (0.22)
  the two profiles are of different devices: /device:TPU:1 before, /device:TPU:32 now
where the time goes in v1:
time: 133 us; the launch traced here: 132 us
  blocking collectives  88.9 us (67%)
  starting transfers between devices  19.9 us (15%)
  waiting for transfers between devices  12.6 us (9%)
  Pallas kernels  9.05 us (7%)
  local copies, waits for them, and re-layouts  1.67 us (1%)
    all_to_all x2, blocking collectives, swap_lines(): lax.all_to_all(value, 'dom', 0, 0, axis_index_groups=lines, tiled=True)  80.2 us
    ppermute x3, starting transfers between devices, body(): lax.ppermute(block, 'dom', pairs(lambda px, py, c, k=k: (px, py + k, 0) i...  9.21 us
    pallas_call x4, Pallas kernels, run(): pl.pallas_call(kernel, out_shape=shapes, in_specs=given, out_specs=specs,...  9.05 us
    all_gather x1, blocking collectives, body(): lax.all_gather(cut, 'dom', axis_index_groups=cores, axis=0, tiled=True)  6.24 us
    ppermute x1, waiting for transfers between devices, body(): lax.ppermute(own, 'dom', pairs(lambda px, py, c: (px, py - 1, 1) if c ==...  5.86 us
    ppermute x1, starting transfers between devices, body(): mate = lax.ppermute(own, 'dom', pairs(lambda px, py, c: (px, py, 1 - c)))  5.21 us
    ppermute x3, waiting for transfers between devices, body(): lax.ppermute(block, 'dom', pairs(lambda px, py, c, k=k: (px, py + k, 0) i...  4.42 us
    ppermute x1, starting transfers between devices, body(): mate_planes = lax.ppermute(potential, 'band', [(0, 1), (1, 0)])  3.47 us
  transfers between devices with their start and end apart: 6, of which 4 were waited for; matrix products, arithmetic and copies ran while one was open for 0% of the time, Pallas kernels for 0%

profile of v1, /device:TPU:32, one launch (start us, length us, event | category | flops | bytes accessed | tf_op | source)
XLA Modules:
  0.0 132.3 jit_solution(14661734619120620975)
XLA Ops:
  0.0 3.5 %collective-permute-start = (f32[4,8,128]{2,1,0:T(8,128)}, f32[4,8,128]{2,1,0:T(8,128)S(1)}, u32[]{:S(2)}, u32[]{:S(2)}) collective-permute-start(f32[4,8,128]{2,1,0:T(8,128)} %own.1), channel_id=1, source_target_pairs={{0,1},{1,0},{2,3},{3,2},{4,5},{5,4},{6,7},{7,6},{8,9},{9,8},{10,11... | collective-permute-start | bytes 49160 | tf_op jit(solution)/shard_map/ppermute | solution.py:326
  3.5 2.4 %collective-permute-done.mate = f32[4,8,128]{2,1,0:T(8,128)S(1)} collective-permute-done((f32[4,8,128]{2,1,0:T(8,128)}, f32[4,8,128]{2,1,0:T(8,128)S(1)}, u32[]{:S(2)}, u32[]{:S(2)}) %collective-permute-start) | collective-permute-done | bytes 16416 | tf_op jit(solution)/shard_map/ppermute | solution.py:326
  5.8 0.0 copy-start
  5.8 0.9 copy-done
  6.8 0.0 copy-start.1
  6.8 0.7 copy-done.1
  7.5 0.1 shard_map.37
  7.6 53.0 %all_to_all.22 = f32[16,64,128]{2,1,0:T(8,128)S(1)} all-to-all(f32[16,64,128]{2,1,0:T(8,128)S(1)} %bitcast.12), channel_id=1, replica_groups={{0,2,64,66,128,130,192,194,256,258,320,322,384,386,448,450},{4,6,68,70,..., dimensions={0} | all-to-all | bytes 1048576 | tf_op jit(solution)/shard_map/all_to_all | solution.py:324
  60.6 0.0 copy-start.2
  60.6 2.0 %collective-permute-start.2 = (f32[1024,128]{1,0:T(8,128)S(1)}, f32[1024,128]{1,0:T(8,128)S(1)}, u32[]{:S(2)}, u32[]{:S(2)}) collective-permute-start(f32[1024,128]{1,0:T(8,128)S(1)} %bitcast.9), channel_id=1, source_target_pairs={{2,4},{4,2},{6,8},{8,6},{10,12},{12,10},{14,16},{16,14},{18,20},{2... | collective-permute-start | bytes 1572872 | tf_op jit(solution)/shard_map/ppermute | solution.py:329
  62.6 5.2 %collective-permute-start.1 = (f32[1024,128]{1,0:T(8,128)S(1)}, f32[1024,128]{1,0:T(8,128)S(1)}, u32[]{:S(2)}, u32[]{:S(2)}) collective-permute-start(f32[1024,128]{1,0:T(8,128)S(1)} %bitcast.10), channel_id=1, source_target_pairs={{0,2},{2,0},{4,6},{6,4},{8,10},{10,8},{12,14},{14,12},{16,18},{18,... | collective-permute-start | bytes 1572872 | tf_op jit(solution)/shard_map/ppermute | solution.py:332
  67.8 5.9 %collective-permute-done.2.beside = f32[1024,128]{1,0:T(8,128)S(1)} collective-permute-done((f32[1024,128]{1,0:T(8,128)S(1)}, f32[1024,128]{1,0:T(8,128)S(1)}, u32[]{:S(2)}, u32[]{:S(2)}) %collective-permute-start.2) | collective-permute-done | bytes 524320 | tf_op jit(solution)/shard_map/ppermute | solution.py:329
  73.7 0.0 collective-permute-done.1.mate
  73.7 0.0 copy-done.2
  73.7 3.2 %shard_map.38 = (f32[8,8,8,256]{3,2,1,0:T(8,128)S(1)}, f32[6,8,8,256]{3,2,1,0:T(8,128)S(1)}, f32[6,8,8,256]{3,2,1,0:T(8,128)S(1)}, f32[2,8,8,128]{3,2,1,0:T(8,128)S(1)}) custom-call(f32[8]{0:T(128)S(1)} %copy-done.2, f32[1024,128]{1,0:T(8,128)S(1)} %bitcast.11, f32[1024,128]{1,0:T(8,128)S(1)} %collective-permute-done.1.mate, ...), custom_call_target="tpu_custom_call" | custom-call | tf_op jit(solution)/shard_map/pallas_call | solution.py:295
  76.9 6.2 %all_gather.9.block = f32[4,8,8,128]{3,2,1,0:T(8,128)S(1)} all-gather(f32[2,8,8,128]{3,2,1,0:T(8,128)S(1)} %get-tuple-element.12), channel_id=1, replica_groups={{0,2},{4,6},{8,10},{12,14},{16,18},{20,22},{24,26},{28,30},{32,34},{36,..., dimensions={0}, use_global_device_ids=true | all-gather | bytes 196608 | tf_op jit(solution)/shard_map/all_gather | solution.py:339
  83.1 1.3 collective-permute-start.5
  84.4 3.1 %collective-permute-start.4 = (f32[4,8,8,128]{3,2,1,0:T(8,128)S(1)}, f32[4,8,8,128]{3,2,1,0:T(8,128)S(1)}, u32[]{:S(2)}, u32[]{:S(2)}) collective-permute-start(f32[4,8,8,128]{3,2,1,0:T(8,128)S(1)} %all_gather.9.block), channel_id=1, source_target_pairs={{0,8},{4,12},{8,16},{10,2},{12,20},{14,6},{16,24},{18,10},{20,28},... | collective-permute-start | bytes 393224 | tf_op jit(solution)/shard_map/ppermute | solution.py:341
  87.5 4.8 %collective-permute-start.3 = (f32[4,8,8,128]{3,2,1,0:T(8,128)S(1)}, f32[4,8,8,128]{3,2,1,0:T(8,128)S(1)}, u32[]{:S(2)}, u32[]{:S(2)}) collective-permute-start(f32[4,8,8,128]{3,2,1,0:T(8,128)S(1)} %all_gather.9.block), channel_id=1, source_target_pairs={{0,4},{4,8},{6,2},{8,12},{10,6},{12,16},{14,10},{16,20},{18,14},{2... | collective-permute-start | bytes 393224 | tf_op jit(solution)/shard_map/ppermute | solution.py:341
  92.4 0.0 collective-permute-done.5
  92.4 2.2 %collective-permute-done.4 = f32[4,8,8,128]{3,2,1,0:T(8,128)S(1)} collective-permute-done((f32[4,8,8,128]{3,2,1,0:T(8,128)S(1)}, f32[4,8,8,128]{3,2,1,0:T(8,128)S(1)}, u32[]{:S(2)}, u32[]{:S(2)}) %collective-permute-start.4) | collective-permute-done | bytes 131104 | tf_op jit(solution)/shard_map/ppermute | solution.py:341
  94.6 2.2 %collective-permute-done.3 = f32[4,8,8,128]{3,2,1,0:T(8,128)S(1)} collective-permute-done((f32[4,8,8,128]{3,2,1,0:T(8,128)S(1)}, f32[4,8,8,128]{3,2,1,0:T(8,128)S(1)}, u32[]{:S(2)}, u32[]{:S(2)}) %collective-permute-start.3) | collective-permute-done | bytes 131104 | tf_op jit(solution)/shard_map/ppermute | solution.py:341
  96.8 2.4 %all-gather = f32[6,4,8,8,128]{4,3,2,1,0:T(8,128)S(1)} all-gather(f32[3,4,8,8,128]{4,3,2,1,0:T(8,128)S(1)} %pad_maximum_fusion), channel_id=2, replica_groups={{0,2},{4,6},{8,10},{12,14},{16,18},{20,22},{24,26},{28,30},{32,34},{36,..., dimensions={0}, use_global_device_ids=true | all-gather | bytes 1179648 | tf_op jit(solution)/shard_map/all_gather | solution.py:348
  99.2 5.0 %shard_map.39 = f32[512,128]{1,0:T(8,128)S(1)} custom-call(f32[8]{0:T(128)S(1)} %copy-done.2, f32[8,8,8,256]{3,2,1,0:T(8,128)S(1)} %get-tuple-element.9.fine, f32[6,8,8,256]{3,2,1,0:T(8,128)S(1)} %get-tuple-element.10.source, f32[6,8,8,256]{3,2,1,0:T(8,128)S(1)} %get-tuple-element.11.inverse, f32[4,8,8,128]{3,2,1,0:T(8,128)S(1)} %all_gather.9.block, ...), custom_call_target="tpu_custom_call" | custom-call | tf_op jit(solution)/shard_map/pallas_call | solution.py:295
  104.2 27.3 %all_to_all.23 = f32[16,32,128]{2,1,0:T(8,128)S(1)} all-to-all(f32[16,32,128]{2,1,0:T(8,128)S(1)} %bitcast.14), channel_id=1, replica_groups={{0,2,64,66,128,130,192,194,256,258,320,322,384,386,448,450},{4,6,68,70,..., dimensions={0} | all-to-all | bytes 524288 | tf_op jit(solution)/shard_map/all_to_all | solution.py:324
  131.5 0.7 shard_map.40
  (1 shorter events, 0.0 us)
Async XLA Ops:
  0.0 5.8 %collective-permute-start = (f32[4,8,128]{2,1,0:T(8,128)}, f32[4,8,128]{2,1,0:T(8,128)S(1)}, u32[]{:S(2)}, u32[]{:S(2)}) collective-permute-start(f32[4,8,128]{2,1,0:T(8,128)} %own.1), channel_id=1, source_target_pairs={{0,1},{1,0},{2,3},{3,2},{4,5},{5,4},{6,7},{7,6},{8,9},{9,8},{10,11... | collective-permute-start | bytes 49160 | tf_op jit(solution)/shard_map/ppermute | solution.py:326
  5.8 1.0 copy-start
  6.8 0.7 copy-start.1
  60.6 13.1 %copy-start.2 = (f32[8]{0:T(128)S(1)}, f32[8]{0:T(128)}, u32[]{:S(2)}) copy-start(f32[8]{0:T(128)} %shifts.3) | copy-start | bytes 100
  60.6 13.1 %collective-permute-start.2 = (f32[1024,128]{1,0:T(8,128)S(1)}, f32[1024,128]{1,0:T(8,128)S(1)}, u32[]{:S(2)}, u32[]{:S(2)}) collective-permute-start(f32[1024,128]{1,0:T(8,128)S(1)} %bitcast.9), channel_id=1, source_target_pairs={{2,4},{4,2},{6,8},{8,6},{10,12},{12,10},{14,16},{16,14},{18,20},{2... | collective-permute-start | bytes 1572872 | tf_op jit(solution)/shard_map/ppermute | solution.py:329
  62.6 11.1 %collective-permute-start.1 = (f32[1024,128]{1,0:T(8,128)S(1)}, f32[1024,128]{1,0:T(8,128)S(1)}, u32[]{:S(2)}, u32[]{:S(2)}) collective-permute-start(f32[1024,128]{1,0:T(8,128)S(1)} %bitcast.10), channel_id=1, source_target_pairs={{0,2},{2,0},{4,6},{6,4},{8,10},{10,8},{12,14},{14,12},{16,18},{18,... | collective-permute-start | bytes 1572872 | tf_op jit(solution)/shard_map/ppermute | solution.py:332
  83.1 9.2 %collective-permute-start.5 = (f32[4,8,8,128]{3,2,1,0:T(8,128)S(1)}, f32[4,8,8,128]{3,2,1,0:T(8,128)S(1)}, u32[]{:S(2)}, u32[]{:S(2)}) collective-permute-start(f32[4,8,8,128]{3,2,1,0:T(8,128)S(1)} %all_gather.9.block), channel_id=1, source_target_pairs={{0,12},{4,16},{8,20},{12,24},{14,2},{16,28},{18,6},{20,32},{22,10}... | collective-permute-start | bytes 393224 | tf_op jit(solution)/shard_map/ppermute | solution.py:341
  84.4 10.2 %collective-permute-start.4 = (f32[4,8,8,128]{3,2,1,0:T(8,128)S(1)}, f32[4,8,8,128]{3,2,1,0:T(8,128)S(1)}, u32[]{:S(2)}, u32[]{:S(2)}) collective-permute-start(f32[4,8,8,128]{3,2,1,0:T(8,128)S(1)} %all_gather.9.block), channel_id=1, source_target_pairs={{0,8},{4,12},{8,16},{10,2},{12,20},{14,6},{16,24},{18,10},{20,28},... | collective-permute-start | bytes 393224 | tf_op jit(solution)/shard_map/ppermute | solution.py:341
  87.5 9.3 %collective-permute-start.3 = (f32[4,8,8,128]{3,2,1,0:T(8,128)S(1)}, f32[4,8,8,128]{3,2,1,0:T(8,128)S(1)}, u32[]{:S(2)}, u32[]{:S(2)}) collective-permute-start(f32[4,8,8,128]{3,2,1,0:T(8,128)S(1)} %all_gather.9.block), channel_id=1, source_target_pairs={{0,4},{4,8},{6,2},{8,12},{10,6},{12,16},{14,10},{16,20},{18,14},{2... | collective-permute-start | bytes 393224 | tf_op jit(solution)/shard_map/ppermute | solution.py:341

commit v2 on v1

--- a/solution.py
+++ b/solution.py
@@ -117,39 +117,41 @@
     ]
 
 
-def pack(residual, own, mate, out):
-    band = lax.axis_index("band")
-    planes = [jnp.where(band == 0, own[i], mate[i]) for i in range(4)]
-    planes += [jnp.where(band == 0, mate[i], own[i]) for i in range(4)]
+def pack(residual, potential, out):
     for c in range(PZ):
         rows = slice(4 * c, 4 * c + 4)
-        for p in range(4):
-            both = jnp.concatenate([planes[2 * p][rows], planes[2 * p + 1][rows]], axis=0)
-            for orbital in range(PX):
-                base = (orbital * PZ + c) * 64 + p * 8
-                out[base : base + 4] = residual[orbital, 2 * p, rows]
-                out[base + 4 : base + 8] = residual[orbital, 2 * p + 1, rows]
-                out[base + 32 : base + 40] = both
-
-
-def down(shifts, own, mate, beside, fine_out, source_out, inverse_out, cut, field, potential, source, inverse, start):
+        for orbital in range(PX):
+            base = (orbital * PZ + c) * 48
+            for i in range(8):
+                out[base + 4 * i : base + 4 * i + 4] = residual[orbital, i, rows]
+            for i in range(4):
+                out[base + 32 + 4 * i : base + 36 + 4 * i] = potential[i, rows]
+
+
+def down(shifts, own, mate, beside, own_half, mate_half, beside_half, fine_out, source_out, inverse_out, cut, field, potential, source, inverse, start):
     px, py, c = place()
     size_y = lax.axis_size("dom") // (PX * PZ)
     shift = shifts[px]
 
-    def unpack(blocks):
+    band = lax.axis_index("band")
+
+    def unpack(blocks, halves):
         for row in range(12):
-            ref = blocks[row // 4]
-            for i in range(8):
-                at = (i // 2) * 8 + (i % 2) * 4 + row % 4
-                for half in range(PZ):
-                    lanes = slice(128 * half, 128 * half + 128)
-                    field[row, i, :, lanes] = ref[pl.ds(half * 64 + at, PX, stride=128), :]
-                    if 1 <= row <= 10:
-                        potential[row - 1, i, :, lanes] = ref[pl.ds(half * 64 + 32 + at, PX, stride=128), :]
-
-    pl.when(c == 0)(lambda: unpack((beside, own, mate)))
-    pl.when(c == 1)(lambda: unpack((mate, own, beside)))
+            block, other_half = blocks[row // 4], halves[row // 4]
+            for half in range(PZ):
+                lanes = slice(128 * half, 128 * half + 128)
+                for i in range(8):
+                    at = 48 * half + 4 * i + row % 4
+                    field[row, i, :, lanes] = block[pl.ds(at, PX, stride=96), :]
+                if 1 <= row <= 10:
+                    for i in range(4):
+                        at = 48 * half + 32 + 4 * i + row % 4
+                        potential[row - 1, 4 * band + i, :, lanes] = block[pl.ds(at, PX, stride=96), :]
+                        at = 16 * half + 4 * i + row % 4
+                        potential[row - 1, 4 * (1 - band) + i, :, lanes] = other_half[pl.ds(at, PX, stride=32), :]
+
+    pl.when(c == 0)(lambda: unpack((beside, own, mate), (beside_half, own_half, mate_half)))
+    pl.when(c == 1)(lambda: unpack((mate, own, beside), (mate_half, own_half, beside_half)))
 
     def first(base, rows):
         for r in range(rows):
@@ -314,28 +316,35 @@
         [dom_of(px, py, c, size_y) for c in range(PZ)] for px in range(PX) for py in range(size_y)
     ]
 
-    def pairs(target):
+    def pairs(target, bands=False):
         found = [((px, py, c), target(px, py, c)) for px, py, c in blocks]
-        return [
-            (dom_of(*a, size_y), dom_of(*b, size_y)) for a, b in found if 0 <= b[1] < size_y
-        ]
+        found = [(dom_of(*a, size_y), dom_of(*b, size_y)) for a, b in found if 0 <= b[1] < size_y]
+        return [(2 * a + n, 2 * b + 1 - n) for a, b in found for n in range(2)] if bands else found
 
     def swap_lines(value):
         return lax.all_to_all(value, "dom", 0, 0, axis_index_groups=lines, tiled=True)
 
-    mate_planes = lax.ppermute(potential, "band", [(0, 1), (1, 0)])
-    (packed,) = call(pack, [(1024, 128)])(residual, potential, mate_planes)
+    def to_beside(px, py, c):
+        return (px, py - 1, 1) if c == 0 else (px, py + 1, 0)
+
+    def to_mate(px, py, c):
+        return (px, py, 1 - c)
+
+    (packed,) = call(pack, [(768, 128)])(residual, potential)
     own = swap_lines(packed)
-    beside = lax.ppermute(
-        own, "dom", pairs(lambda px, py, c: (px, py - 1, 1) if c == 0 else (px, py + 1, 0))
-    )
-    mate = lax.ppermute(own, "dom", pairs(lambda px, py, c: (px, py, 1 - c)))
+    half = own.reshape(16, 48, 128)[:, 32:].reshape(256, 128)
+    both = ("dom", "band")
+    beside = lax.ppermute(own, "dom", pairs(to_beside))
+    beside_half = lax.ppermute(half, both, pairs(to_beside, True))
+    mate = lax.ppermute(own, "dom", pairs(to_mate))
+    own_half = lax.ppermute(half, "band", [(0, 1), (1, 0)])
+    mate_half = lax.ppermute(half, both, pairs(to_mate, True))
     fine, source, inverse, cut = call(
         down,
         [(8, 8, 8, 256), (6, 8, 8, 256), (6, 8, 8, 256), (2, 8, 8, 128)],
         [(12, 8, 8, 256)] + [(10, 8, 8, 256)] * 4,
         smem=True,
-    )(shifts, own, mate, beside)
+    )(shifts, own, mate, beside, own_half, mate_half, beside_half)
     block = lax.all_gather(cut, "dom", axis_index_groups=cores, axis=0, tiled=True)
     sent = [
         lax.ppermute(

time: 133 us -> 126 us (0.947)
  blocking collectives: 88.9 us -> 79.7 us
  starting transfers between devices: 19.9 us -> 22.7 us
    all_to_all x2, blocking collectives: 80.2 us -> 75.4 us  [swap_lines(): lax.all_to_all(value, 'dom', 0, 0, axis_index_groups=lines, tiled=True)]
    all_gather x1, blocking collectives: 6.24 us -> 1.91 us  [body(): lax.all_gather(cut, 'dom', axis_index_groups=cores, axis=0, tiled=True)]
    ppermute x3 -> x5, starting transfers between devices: 10.7 us -> 14.5 us  [the longest x1 5.21 us: body(): mate = lax.ppermute(own, 'dom', pairs(to_mate))]
    ppermute x3 -> x5, waiting for transfers between devices: 8.22 us -> 6.34 us  [the longest x1 2.61 us: body(): mate_half = lax.ppermute(half, both, pairs(to_mate, True))]
    ppermute x3, waiting for transfers between devices: 4.42 us -> 6.06 us  [body(): lax.ppermute(block, 'dom', pairs(lambda px, py, c, k=k: (px, py + k, 0) i...]
  transfers between devices with their start and end apart: 6 -> 8, of which waited for: 4 -> 5; matrix products, arithmetic and copies ran while one was open for 0% -> 0% of each run, Pallas kernels for 0% -> 0%
where the time goes in v2:
time: 126 us
  blocking collectives  79.7 us (63%)
  starting transfers between devices  22.7 us (18%)
  waiting for transfers between devices  12.4 us (10%)
  Pallas kernels  9.05 us (7%)
  local copies, waits for them, and re-layouts  1.68 us (1%)
    all_to_all x2, blocking collectives, swap_lines(): lax.all_to_all(value, 'dom', 0, 0, axis_index_groups=lines, tiled=True)  75.4 us
    pallas_call x4, Pallas kernels, run(): pl.pallas_call(kernel, out_shape=shapes, in_specs=given, out_specs=specs,...  9.05 us
    ppermute x3, starting transfers between devices, body(): lax.ppermute(block, 'dom', pairs(lambda px, py, c, k=k: (px, py + k, 0) i...  8.16 us
    ppermute x3, waiting for transfers between devices, body(): lax.ppermute(block, 'dom', pairs(lambda px, py, c, k=k: (px, py + k, 0) i...  6.06 us
    ppermute x1, starting transfers between devices, body(): mate = lax.ppermute(own, 'dom', pairs(to_mate))  5.21 us
    ppermute x1, starting transfers between devices, body(): beside_half = lax.ppermute(half, both, pairs(to_beside, True))  3.48 us
    ppermute x1, waiting for transfers between devices, body(): mate_half = lax.ppermute(half, both, pairs(to_mate, True))  2.61 us
  transfers between devices with their start and end apart: 8, of which 5 were waited for; matrix products, arithmetic and copies ran while one was open for 0% of the time, Pallas kernels for 0%

profile of v2, /device:TPU:32, one launch (start us, length us, event | category | flops | bytes accessed | tf_op | source)
XLA Modules:
  0.0 125.6 jit_solution(15856928223790560032)
XLA Ops:
  0.0 0.0 copy-start
  0.0 0.9 copy-done
  1.0 0.0 copy-start.1
  1.0 0.7 copy-done.1
  1.7 0.1 shard_map.37
  1.7 47.4 %all_to_all.22 = f32[16,48,128]{2,1,0:T(8,128)S(1)} all-to-all(f32[16,48,128]{2,1,0:T(8,128)S(1)} %bitcast.13), channel_id=1, replica_groups={{0,2,64,66,128,130,192,194,256,258,320,322,384,386,448,450},{4,6,68,70,..., dimensions={0} | all-to-all | bytes 786432 | tf_op jit(solution)/shard_map/all_to_all | solution.py:325
  49.1 1.9 %collective-permute-start.1 = (f32[768,128]{1,0:T(8,128)S(1)}, f32[768,128]{1,0:T(8,128)S(1)}, u32[]{:S(2)}, u32[]{:S(2)}) collective-permute-start(f32[768,128]{1,0:T(8,128)S(1)} %bitcast.10), channel_id=1, source_target_pairs={{2,4},{4,2},{6,8},{8,6},{10,12},{12,10},{14,16},{16,14},{18,20},{2... | collective-permute-start | bytes 1179656 | tf_op jit(solution)/shard_map/ppermute | solution.py:337
  51.0 5.2 %collective-permute-start = (f32[768,128]{1,0:T(8,128)S(1)}, f32[768,128]{1,0:T(8,128)S(1)}, u32[]{:S(2)}, u32[]{:S(2)}) collective-permute-start(f32[768,128]{1,0:T(8,128)S(1)} %bitcast.11), channel_id=1, source_target_pairs={{0,2},{2,0},{4,6},{6,4},{8,10},{10,8},{12,14},{14,12},{16,18},{18,... | collective-permute-start | bytes 1179656 | tf_op jit(solution)/shard_map/ppermute | solution.py:339
  56.2 0.0 copy-start.2
  56.3 3.5 %collective-permute-start.4 = (f32[256,128]{1,0:T(8,128)S(1)}, f32[256,128]{1,0:T(8,128)S(1)}, u32[]{:S(2)}, u32[]{:S(2)}) collective-permute-start(f32[256,128]{1,0:T(8,128)S(1)} %bitcast.16), channel_id=1, source_target_pairs={{2,5},{3,4},{4,3},{5,2},{6,9},{7,8},{8,7},{9,6},{10,13},{11,12},{1... | collective-permute-start | bytes 393224 | tf_op jit(solution)/shard_map/ppermute | solution.py:338
  59.7 1.9 %collective-permute-start.3 = (f32[256,128]{1,0:T(8,128)S(1)}, f32[256,128]{1,0:T(8,128)S(1)}, u32[]{:S(2)}, u32[]{:S(2)}) collective-permute-start(f32[256,128]{1,0:T(8,128)S(1)} %bitcast.17), channel_id=1, source_target_pairs={{0,3},{1,2},{2,1},{3,0},{4,7},{5,6},{6,5},{7,4},{8,11},{9,10},{10,... | collective-permute-start | bytes 393224 | tf_op jit(solution)/shard_map/ppermute | solution.py:341
  61.7 2.0 %collective-permute-start.2 = (f32[256,128]{1,0:T(8,128)S(1)}, f32[256,128]{1,0:T(8,128)S(1)}, u32[]{:S(2)}, u32[]{:S(2)}) collective-permute-start(f32[256,128]{1,0:T(8,128)S(1)} %bitcast.18), channel_id=1, source_target_pairs={{0,1},{1,0},{2,3},{3,2},{4,5},{5,4},{6,7},{7,6},{8,9},{9,8},{10,11... | collective-permute-start | bytes 393224 | tf_op jit(solution)/shard_map/ppermute | solution.py:340
  63.7 2.0 %collective-permute-done.4.beside_half = f32[256,128]{1,0:T(8,128)S(1)} collective-permute-done((f32[256,128]{1,0:T(8,128)S(1)}, f32[256,128]{1,0:T(8,128)S(1)}, u32[]{:S(2)}, u32[]{:S(2)}) %collective-permute-start.4) | collective-permute-done | bytes 131104 | tf_op jit(solution)/shard_map/ppermute | solution.py:338
  65.7 2.6 %collective-permute-done.3.mate_half = f32[256,128]{1,0:T(8,128)S(1)} collective-permute-done((f32[256,128]{1,0:T(8,128)S(1)}, f32[256,128]{1,0:T(8,128)S(1)}, u32[]{:S(2)}, u32[]{:S(2)}) %collective-permute-start.3) | collective-permute-done | bytes 131104 | tf_op jit(solution)/shard_map/ppermute | solution.py:341
  68.3 1.7 %collective-permute-done.2.own_half = f32[256,128]{1,0:T(8,128)S(1)} collective-permute-done((f32[256,128]{1,0:T(8,128)S(1)}, f32[256,128]{1,0:T(8,128)S(1)}, u32[]{:S(2)}, u32[]{:S(2)}) %collective-permute-start.2) | collective-permute-done | bytes 131104 | tf_op jit(solution)/shard_map/ppermute | solution.py:340
  70.0 0.0 collective-permute-done.1.beside
  70.0 0.0 collective-permute-done.mate
  70.0 0.0 copy-done.2
  70.0 3.2 %shard_map.38 = (f32[8,8,8,256]{3,2,1,0:T(8,128)S(1)}, f32[6,8,8,256]{3,2,1,0:T(8,128)S(1)}, f32[6,8,8,256]{3,2,1,0:T(8,128)S(1)}, f32[2,8,8,128]{3,2,1,0:T(8,128)S(1)}) custom-call(f32[8]{0:T(128)S(1)} %copy-done.2, f32[768,128]{1,0:T(8,128)S(1)} %bitcast.12, f32[768,128]{1,0:T(8,128)S(1)} %collective-permute-done.mate, ...), custom_call_target="tpu_custom_call" | custom-call | tf_op jit(solution)/shard_map/pallas_call | solution.py:297
  73.2 1.9 %all_gather.9.block = f32[4,8,8,128]{3,2,1,0:T(8,128)S(1)} all-gather(f32[2,8,8,128]{3,2,1,0:T(8,128)S(1)} %get-tuple-element.12), channel_id=1, replica_groups={{0,2},{4,6},{8,10},{12,14},{16,18},{20,22},{24,26},{28,30},{32,34},{36,..., dimensions={0}, use_global_device_ids=true | all-gather | bytes 196608 | tf_op jit(solution)/shard_map/all_gather | solution.py:348
  75.1 2.6 %collective-permute-start.7 = (f32[4,8,8,128]{3,2,1,0:T(8,128)S(1)}, f32[4,8,8,128]{3,2,1,0:T(8,128)S(1)}, u32[]{:S(2)}, u32[]{:S(2)}) collective-permute-start(f32[4,8,8,128]{3,2,1,0:T(8,128)S(1)} %all_gather.9.block), channel_id=1, source_target_pairs={{0,12},{4,16},{8,20},{12,24},{14,2},{16,28},{18,6},{20,32},{22,10}... | collective-permute-start | bytes 393224 | tf_op jit(solution)/shard_map/ppermute | solution.py:350
  77.8 2.3 %collective-permute-start.6 = (f32[4,8,8,128]{3,2,1,0:T(8,128)S(1)}, f32[4,8,8,128]{3,2,1,0:T(8,128)S(1)}, u32[]{:S(2)}, u32[]{:S(2)}) collective-permute-start(f32[4,8,8,128]{3,2,1,0:T(8,128)S(1)} %all_gather.9.block), channel_id=1, source_target_pairs={{0,8},{4,12},{8,16},{10,2},{12,20},{14,6},{16,24},{18,10},{20,28},... | collective-permute-start | bytes 393224 | tf_op jit(solution)/shard_map/ppermute | solution.py:350
  80.1 3.2 %collective-permute-start.5 = (f32[4,8,8,128]{3,2,1,0:T(8,128)S(1)}, f32[4,8,8,128]{3,2,1,0:T(8,128)S(1)}, u32[]{:S(2)}, u32[]{:S(2)}) collective-permute-start(f32[4,8,8,128]{3,2,1,0:T(8,128)S(1)} %all_gather.9.block), channel_id=1, source_target_pairs={{0,4},{4,8},{6,2},{8,12},{10,6},{12,16},{14,10},{16,20},{18,14},{2... | collective-permute-start | bytes 393224 | tf_op jit(solution)/shard_map/ppermute | solution.py:350
  83.3 0.0 collective-permute-done.7
  83.3 1.7 %collective-permute-done.6 = f32[4,8,8,128]{3,2,1,0:T(8,128)S(1)} collective-permute-done((f32[4,8,8,128]{3,2,1,0:T(8,128)S(1)}, f32[4,8,8,128]{3,2,1,0:T(8,128)S(1)}, u32[]{:S(2)}, u32[]{:S(2)}) %collective-permute-start.6) | collective-permute-done | bytes 131104 | tf_op jit(solution)/shard_map/ppermute | solution.py:350
  85.0 4.4 %collective-permute-done.5 = f32[4,8,8,128]{3,2,1,0:T(8,128)S(1)} collective-permute-done((f32[4,8,8,128]{3,2,1,0:T(8,128)S(1)}, f32[4,8,8,128]{3,2,1,0:T(8,128)S(1)}, u32[]{:S(2)}, u32[]{:S(2)}) %collective-permute-start.5) | collective-permute-done | bytes 131104 | tf_op jit(solution)/shard_map/ppermute | solution.py:350
  89.4 2.4 %all-gather = f32[6,4,8,8,128]{4,3,2,1,0:T(8,128)S(1)} all-gather(f32[3,4,8,8,128]{4,3,2,1,0:T(8,128)S(1)} %pad_maximum_fusion), channel_id=2, replica_groups={{0,2},{4,6},{8,10},{12,14},{16,18},{20,22},{24,26},{28,30},{32,34},{36,..., dimensions={0}, use_global_device_ids=true | all-gather | bytes 1179648 | tf_op jit(solution)/shard_map/all_gather | solution.py:357
  91.8 5.0 %shard_map.39 = f32[512,128]{1,0:T(8,128)S(1)} custom-call(f32[8]{0:T(128)S(1)} %copy-done.2, f32[8,8,8,256]{3,2,1,0:T(8,128)S(1)} %get-tuple-element.9.fine, f32[6,8,8,256]{3,2,1,0:T(8,128)S(1)} %get-tuple-element.10.source, f32[6,8,8,256]{3,2,1,0:T(8,128)S(1)} %get-tuple-element.11.inverse, f32[4,8,8,128]{3,2,1,0:T(8,128)S(1)} %all_gather.9.block, ...), custom_call_target="tpu_custom_call" | custom-call | tf_op jit(solution)/shard_map/pallas_call | solution.py:297
  96.8 28.0 %all_to_all.23 = f32[16,32,128]{2,1,0:T(8,128)S(1)} all-to-all(f32[16,32,128]{2,1,0:T(8,128)S(1)} %bitcast.15), channel_id=1, replica_groups={{0,2,64,66,128,130,192,194,256,258,320,322,384,386,448,450},{4,6,68,70,..., dimensions={0} | all-to-all | bytes 524288 | tf_op jit(solution)/shard_map/all_to_all | solution.py:325
  124.9 0.7 shard_map.40
  (2 shorter events, 0.0 us)
Async XLA Ops:
  0.0 0.9 copy-start
  1.0 0.7 copy-start.1
  49.1 20.9 %collective-permute-start.1 = (f32[768,128]{1,0:T(8,128)S(1)}, f32[768,128]{1,0:T(8,128)S(1)}, u32[]{:S(2)}, u32[]{:S(2)}) collective-permute-start(f32[768,128]{1,0:T(8,128)S(1)} %bitcast.10), channel_id=1, source_target_pairs={{2,4},{4,2},{6,8},{8,6},{10,12},{12,10},{14,16},{16,14},{18,20},{2... | collective-permute-start | bytes 1179656 | tf_op jit(solution)/shard_map/ppermute | solution.py:337
  51.0 19.0 %collective-permute-start = (f32[768,128]{1,0:T(8,128)S(1)}, f32[768,128]{1,0:T(8,128)S(1)}, u32[]{:S(2)}, u32[]{:S(2)}) collective-permute-start(f32[768,128]{1,0:T(8,128)S(1)} %bitcast.11), channel_id=1, source_target_pairs={{0,2},{2,0},{4,6},{6,4},{8,10},{10,8},{12,14},{14,12},{16,18},{18,... | collective-permute-start | bytes 1179656 | tf_op jit(solution)/shard_map/ppermute | solution.py:339
  56.2 13.8 %copy-start.2 = (f32[8]{0:T(128)S(1)}, f32[8]{0:T(128)}, u32[]{:S(2)}) copy-start(f32[8]{0:T(128)} %shifts.3) | copy-start | bytes 100
  56.3 9.4 %collective-permute-start.4 = (f32[256,128]{1,0:T(8,128)S(1)}, f32[256,128]{1,0:T(8,128)S(1)}, u32[]{:S(2)}, u32[]{:S(2)}) collective-permute-start(f32[256,128]{1,0:T(8,128)S(1)} %bitcast.16), channel_id=1, source_target_pairs={{2,5},{3,4},{4,3},{5,2},{6,9},{7,8},{8,7},{9,6},{10,13},{11,12},{1... | collective-permute-start | bytes 393224 | tf_op jit(solution)/shard_map/ppermute | solution.py:338
  59.7 8.5 %collective-permute-start.3 = (f32[256,128]{1,0:T(8,128)S(1)}, f32[256,128]{1,0:T(8,128)S(1)}, u32[]{:S(2)}, u32[]{:S(2)}) collective-permute-start(f32[256,128]{1,0:T(8,128)S(1)} %bitcast.17), channel_id=1, source_target_pairs={{0,3},{1,2},{2,1},{3,0},{4,7},{5,6},{6,5},{7,4},{8,11},{9,10},{10,... | collective-permute-start | bytes 393224 | tf_op jit(solution)/shard_map/ppermute | solution.py:341
  61.7 8.3 %collective-permute-start.2 = (f32[256,128]{1,0:T(8,128)S(1)}, f32[256,128]{1,0:T(8,128)S(1)}, u32[]{:S(2)}, u32[]{:S(2)}) collective-permute-start(f32[256,128]{1,0:T(8,128)S(1)} %bitcast.18), channel_id=1, source_target_pairs={{0,1},{1,0},{2,3},{3,2},{4,5},{5,4},{6,7},{7,6},{8,9},{9,8},{10,11... | collective-permute-start | bytes 393224 | tf_op jit(solution)/shard_map/ppermute | solution.py:340
  75.1 8.2 %collective-permute-start.7 = (f32[4,8,8,128]{3,2,1,0:T(8,128)S(1)}, f32[4,8,8,128]{3,2,1,0:T(8,128)S(1)}, u32[]{:S(2)}, u32[]{:S(2)}) collective-permute-start(f32[4,8,8,128]{3,2,1,0:T(8,128)S(1)} %all_gather.9.block), channel_id=1, source_target_pairs={{0,12},{4,16},{8,20},{12,24},{14,2},{16,28},{18,6},{20,32},{22,10}... | collective-permute-start | bytes 393224 | tf_op jit(solution)/shard_map/ppermute | solution.py:350
  77.8 7.2 %collective-permute-start.6 = (f32[4,8,8,128]{3,2,1,0:T(8,128)S(1)}, f32[4,8,8,128]{3,2,1,0:T(8,128)S(1)}, u32[]{:S(2)}, u32[]{:S(2)}) collective-permute-start(f32[4,8,8,128]{3,2,1,0:T(8,128)S(1)} %all_gather.9.block), channel_id=1, source_target_pairs={{0,8},{4,12},{8,16},{10,2},{12,20},{14,6},{16,24},{18,10},{20,28},... | collective-permute-start | bytes 393224 | tf_op jit(solution)/shard_map/ppermute | solution.py:350
  80.1 9.3 %collective-permute-start.5 = (f32[4,8,8,128]{3,2,1,0:T(8,128)S(1)}, f32[4,8,8,128]{3,2,1,0:T(8,128)S(1)}, u32[]{:S(2)}, u32[]{:S(2)}) collective-permute-start(f32[4,8,8,128]{3,2,1,0:T(8,128)S(1)} %all_gather.9.block), channel_id=1, source_target_pairs={{0,4},{4,8},{6,2},{8,12},{10,6},{12,16},{14,10},{16,20},{18,14},{2... | collective-permute-start | bytes 393224 | tf_op jit(solution)/shard_map/ppermute | solution.py:350

commit v3 on v2

--- a/solution.py
+++ b/solution.py
@@ -128,7 +128,7 @@
                 out[base + 32 + 4 * i : base + 36 + 4 * i] = potential[i, rows]
 
 
-def down(shifts, own, mate, beside, own_half, mate_half, beside_half, fine_out, source_out, inverse_out, cut, field, potential, source, inverse, start):
+def down(shifts, cores, beside, cores_half, beside_half, fine_out, source_out, inverse_out, cut, field, potential, source, inverse, start):
     px, py, c = place()
     size_y = lax.axis_size("dom") // (PX * PZ)
     shift = shifts[px]
@@ -150,8 +150,10 @@
                         at = 16 * half + 4 * i + row % 4
                         potential[row - 1, 4 * (1 - band) + i, :, lanes] = other_half[pl.ds(at, PX, stride=32), :]
 
-    pl.when(c == 0)(lambda: unpack((beside, own, mate), (beside_half, own_half, mate_half)))
-    pl.when(c == 1)(lambda: unpack((mate, own, beside), (mate_half, own_half, beside_half)))
+    here = (cores.at[0], cores.at[1])
+    here_half = (cores_half.at[0], cores_half.at[1])
+    pl.when(c == 0)(lambda: unpack((beside, *here), (beside_half, *here_half)))
+    pl.when(c == 1)(lambda: unpack((*here, beside), (*here_half, beside_half)))
 
     def first(base, rows):
         for r in range(rows):
@@ -327,24 +329,21 @@
     def to_beside(px, py, c):
         return (px, py - 1, 1) if c == 0 else (px, py + 1, 0)
 
-    def to_mate(px, py, c):
-        return (px, py, 1 - c)
-
     (packed,) = call(pack, [(768, 128)])(residual, potential)
     own = swap_lines(packed)
     half = own.reshape(16, 48, 128)[:, 32:].reshape(256, 128)
     both = ("dom", "band")
+    own_half = lax.ppermute(half, "band", [(0, 1), (1, 0)])
     beside = lax.ppermute(own, "dom", pairs(to_beside))
     beside_half = lax.ppermute(half, both, pairs(to_beside, True))
-    mate = lax.ppermute(own, "dom", pairs(to_mate))
-    own_half = lax.ppermute(half, "band", [(0, 1), (1, 0)])
-    mate_half = lax.ppermute(half, both, pairs(to_mate, True))
+    of_cores = lax.all_gather(own, "dom", axis_index_groups=cores, axis=0)
+    of_cores_half = lax.all_gather(own_half, "dom", axis_index_groups=cores, axis=0)
     fine, source, inverse, cut = call(
         down,
         [(8, 8, 8, 256), (6, 8, 8, 256), (6, 8, 8, 256), (2, 8, 8, 128)],
         [(12, 8, 8, 256)] + [(10, 8, 8, 256)] * 4,
         smem=True,
-    )(shifts, own, mate, beside, own_half, mate_half, beside_half)
+    )(shifts, of_cores, beside, of_cores_half, beside_half)
     block = lax.all_gather(cut, "dom", axis_index_groups=cores, axis=0, tiled=True)
     sent = [
         lax.ppermute(

time: 126 us -> 126 us (level)
  blocking collectives: 79.7 us -> 85.4 us
  starting transfers between devices: 22.7 us -> 18 us
  waiting for transfers between devices: 12.4 us -> 10.6 us
    ppermute x2 -> x0, starting transfers between devices: 7.13 us -> none  [the longest x1 5.21 us: body(): mate = lax.ppermute(own, 'dom', pairs(to_mate))]
    all_gather x0 -> x2, blocking collectives: none -> 5.71 us  [the longest x1 3.34 us: body(): lax.all_gather(own_half, 'dom', axis_index_groups=cores, axis=0)]
    ppermute x1, starting transfers between devices: 3.48 us -> 6.76 us  [body(): beside_half = lax.ppermute(half, both, pairs(to_beside, True))]
    ppermute x2 -> x0, waiting for transfers between devices: 2.62 us -> none  [the longest x1 2.61 us: body(): mate_half = lax.ppermute(half, both, pairs(to_mate, True))]
    ppermute x1, waiting for transfers between devices: 1.73 us -> 4.09 us  [body(): own_half = lax.ppermute(half, 'band', [(0, 1), (1, 0)])]
    ppermute x1, waiting for transfers between devices: 2 us -> 0.01 us  [body(): beside_half = lax.ppermute(half, both, pairs(to_beside, True))]
  transfers between devices with their start and end apart: 8 -> 6, of which waited for: 5 -> 3; matrix products, arithmetic and copies ran while one was open for 0% -> 0% of each run, Pallas kernels for 0% -> 0%
where the time goes in v3:
time: 126 us; the launch traced here: 125 us
  blocking collectives  85.4 us (68%)
  starting transfers between devices  18 us (14%)
  waiting for transfers between devices  10.6 us (8%)
  Pallas kernels  9.05 us (7%)
  local copies, waits for them, and re-layouts  2.33 us (2%)
    all_to_all x2, blocking collectives, swap_lines(): lax.all_to_all(value, 'dom', 0, 0, axis_index_groups=lines, tiled=True)  75.4 us
    pallas_call x4, Pallas kernels, run(): pl.pallas_call(kernel, out_shape=shapes, in_specs=given, out_specs=specs,...  9.05 us
    ppermute x3, starting transfers between devices, body(): lax.ppermute(block, 'dom', pairs(lambda px, py, c, k=k: (px, py + k, 0) i...  7.38 us
    ppermute x1, starting transfers between devices, body(): beside_half = lax.ppermute(half, both, pairs(to_beside, True))  6.76 us
    ppermute x3, waiting for transfers between devices, body(): lax.ppermute(block, 'dom', pairs(lambda px, py, c, k=k: (px, py + k, 0) i...  6.47 us
    ppermute x1, waiting for transfers between devices, body(): own_half = lax.ppermute(half, 'band', [(0, 1), (1, 0)])  4.09 us
    all_gather x1, blocking collectives, body(): lax.all_gather(own_half, 'dom', axis_index_groups=cores, axis=0)  3.34 us
  transfers between devices with their start and end apart: 6, of which 3 were waited for; matrix products, arithmetic and copies ran while one was open for 0% of the time, Pallas kernels for 0%

profile of v3, /device:TPU:32, one launch (start us, length us, event | category | flops | bytes accessed | tf_op | source)
XLA Modules:
  0.0 125.4 jit_solution(3579741566147485361)
XLA Ops:
  0.0 0.0 copy-start
  0.0 0.9 copy-done
  1.0 0.0 copy-start.1
  1.0 0.7 copy-done.1
  1.7 0.1 shard_map.37
  1.7 47.4 %all_to_all.23 = f32[16,48,128]{2,1,0:T(8,128)S(1)} all-to-all(f32[16,48,128]{2,1,0:T(8,128)S(1)} %bitcast.12), channel_id=1, replica_groups={{0,2,64,66,128,130,192,194,256,258,320,322,384,386,448,450},{4,6,68,70,..., dimensions={0} | all-to-all | bytes 786432 | tf_op jit(solution)/shard_map/all_to_all | solution.py:327
  49.1 1.9 %collective-permute-start = (f32[768,128]{1,0:T(8,128)S(1)}, f32[768,128]{1,0:T(8,128)S(1)}, u32[]{:S(2)}, u32[]{:S(2)}) collective-permute-start(f32[768,128]{1,0:T(8,128)S(1)} %bitcast.16), channel_id=1, source_target_pairs={{2,4},{4,2},{6,8},{8,6},{10,12},{12,10},{14,16},{16,14},{18,20},{2... | collective-permute-start | bytes 1179656 | tf_op jit(solution)/shard_map/ppermute | solution.py:337
  51.0 6.8 %collective-permute-start.2 = (f32[256,128]{1,0:T(8,128)S(1)}, f32[256,128]{1,0:T(8,128)S(1)}, u32[]{:S(2)}, u32[]{:S(2)}) collective-permute-start(f32[256,128]{1,0:T(8,128)S(1)} %bitcast.18), channel_id=1, source_target_pairs={{2,5},{3,4},{4,3},{5,2},{6,9},{7,8},{8,7},{9,6},{10,13},{11,12},{1... | collective-permute-start | bytes 393224 | tf_op jit(solution)/shard_map/ppermute | solution.py:338
  57.8 1.9 %collective-permute-start.1 = (f32[256,128]{1,0:T(8,128)S(1)}, f32[256,128]{1,0:T(8,128)S(1)}, u32[]{:S(2)}, u32[]{:S(2)}) collective-permute-start(f32[256,128]{1,0:T(8,128)S(1)} %bitcast.19), channel_id=1, source_target_pairs={{0,1},{1,0},{2,3},{3,2},{4,5},{5,4},{6,7},{7,6},{8,9},{9,8},{10,11... | collective-permute-start | bytes 393224 | tf_op jit(solution)/shard_map/ppermute | solution.py:336
  59.7 2.4 %all_gather.22.cores = f32[2,768,128]{2,1,0:T(8,128)S(1)} all-gather(f32[1,768,128]{2,1,0:T(8,128)S(1)} %bitcast.17), channel_id=1, replica_groups={{0,2},{4,6},{8,10},{12,14},{16,18},{20,22},{24,26},{28,30},{32,34},{36,..., dimensions={0}, use_global_device_ids=true | all-gather | bytes 1179648 | tf_op jit(solution)/shard_map/all_gather | solution.py:339
  62.1 4.1 %collective-permute-done.1 = f32[256,128]{1,0:T(8,128)S(1)} collective-permute-done((f32[256,128]{1,0:T(8,128)S(1)}, f32[256,128]{1,0:T(8,128)S(1)}, u32[]{:S(2)}, u32[]{:S(2)}) %collective-permute-start.1) | collective-permute-done | bytes 131104 | tf_op jit(solution)/shard_map/ppermute | solution.py:336
  66.2 3.3 %all-gather = f32[512,128]{1,0:T(8,128)S(1)} all-gather(f32[256,128]{1,0:T(8,128)S(1)} %collective-permute-done.1), channel_id=2, replica_groups={{0,2},{4,6},{8,10},{12,14},{16,18},{20,22},{24,26},{28,30},{32,34},{36,..., dimensions={0}, use_global_device_ids=true | all-gather | bytes 393216 | tf_op jit(solution)/shard_map/all_gather | solution.py:340
  69.5 0.0 copy-start.2
  69.5 0.0 collective-permute-done.2.beside_half
  69.5 0.0 collective-permute-done.beside
  69.5 0.6 copy-done.2
  70.2 3.2 %shard_map.38 = (f32[8,8,8,256]{3,2,1,0:T(8,128)S(1)}, f32[6,8,8,256]{3,2,1,0:T(8,128)S(1)}, f32[6,8,8,256]{3,2,1,0:T(8,128)S(1)}, f32[2,8,8,128]{3,2,1,0:T(8,128)S(1)}) custom-call(f32[8]{0:T(128)S(1)} %copy-done.2, f32[2,768,128]{2,1,0:T(8,128)S(1)} %all_gather.22.cores, f32[768,128]{1,0:T(8,128)S(1)} %collective-permute-done.beside, ...), custom_call_target="tpu_custom_call" | custom-call | tf_op jit(solution)/shard_map/pallas_call | solution.py:299
  73.4 1.9 %all_gather.25.block = f32[4,8,8,128]{3,2,1,0:T(8,128)S(1)} all-gather(f32[2,8,8,128]{3,2,1,0:T(8,128)S(1)} %get-tuple-element.12), channel_id=1, replica_groups={{0,2},{4,6},{8,10},{12,14},{16,18},{20,22},{24,26},{28,30},{32,34},{36,..., dimensions={0}, use_global_device_ids=true | all-gather | bytes 196608 | tf_op jit(solution)/shard_map/all_gather | solution.py:347
  75.3 1.3 %collective-permute-start.5 = (f32[4,8,8,128]{3,2,1,0:T(8,128)S(1)}, f32[4,8,8,128]{3,2,1,0:T(8,128)S(1)}, u32[]{:S(2)}, u32[]{:S(2)}) collective-permute-start(f32[4,8,8,128]{3,2,1,0:T(8,128)S(1)} %all_gather.25.block), channel_id=1, source_target_pairs={{0,12},{4,16},{8,20},{12,24},{14,2},{16,28},{18,6},{20,32},{22,10}... | collective-permute-start | bytes 393224 | tf_op jit(solution)/shard_map/ppermute | solution.py:349
  76.6 3.3 %collective-permute-start.4 = (f32[4,8,8,128]{3,2,1,0:T(8,128)S(1)}, f32[4,8,8,128]{3,2,1,0:T(8,128)S(1)}, u32[]{:S(2)}, u32[]{:S(2)}) collective-permute-start(f32[4,8,8,128]{3,2,1,0:T(8,128)S(1)} %all_gather.25.block), channel_id=1, source_target_pairs={{0,8},{4,12},{8,16},{10,2},{12,20},{14,6},{16,24},{18,10},{20,28},... | collective-permute-start | bytes 393224 | tf_op jit(solution)/shard_map/ppermute | solution.py:349
  79.9 2.8 %collective-permute-start.3 = (f32[4,8,8,128]{3,2,1,0:T(8,128)S(1)}, f32[4,8,8,128]{3,2,1,0:T(8,128)S(1)}, u32[]{:S(2)}, u32[]{:S(2)}) collective-permute-start(f32[4,8,8,128]{3,2,1,0:T(8,128)S(1)} %all_gather.25.block), channel_id=1, source_target_pairs={{0,4},{4,8},{6,2},{8,12},{10,6},{12,16},{14,10},{16,20},{18,14},{2... | collective-permute-start | bytes 393224 | tf_op jit(solution)/shard_map/ppermute | solution.py:349
  82.7 0.0 collective-permute-done.5
  82.7 2.2 %collective-permute-done.4 = f32[4,8,8,128]{3,2,1,0:T(8,128)S(1)} collective-permute-done((f32[4,8,8,128]{3,2,1,0:T(8,128)S(1)}, f32[4,8,8,128]{3,2,1,0:T(8,128)S(1)}, u32[]{:S(2)}, u32[]{:S(2)}) %collective-permute-start.4) | collective-permute-done | bytes 131104 | tf_op jit(solution)/shard_map/ppermute | solution.py:349
  84.9 4.3 %collective-permute-done.3 = f32[4,8,8,128]{3,2,1,0:T(8,128)S(1)} collective-permute-done((f32[4,8,8,128]{3,2,1,0:T(8,128)S(1)}, f32[4,8,8,128]{3,2,1,0:T(8,128)S(1)}, u32[]{:S(2)}, u32[]{:S(2)}) %collective-permute-start.3) | collective-permute-done | bytes 131104 | tf_op jit(solution)/shard_map/ppermute | solution.py:349
  89.2 2.4 %all-gather.1 = f32[6,4,8,8,128]{4,3,2,1,0:T(8,128)S(1)} all-gather(f32[3,4,8,8,128]{4,3,2,1,0:T(8,128)S(1)} %pad_maximum_fusion), channel_id=3, replica_groups={{0,2},{4,6},{8,10},{12,14},{16,18},{20,22},{24,26},{28,30},{32,34},{36,..., dimensions={0}, use_global_device_ids=true | all-gather | bytes 1179648 | tf_op jit(solution)/shard_map/all_gather | solution.py:356
  91.6 5.0 %shard_map.39 = f32[512,128]{1,0:T(8,128)S(1)} custom-call(f32[8]{0:T(128)S(1)} %copy-done.2, f32[8,8,8,256]{3,2,1,0:T(8,128)S(1)} %get-tuple-element.9.fine, f32[6,8,8,256]{3,2,1,0:T(8,128)S(1)} %get-tuple-element.10.source, f32[6,8,8,256]{3,2,1,0:T(8,128)S(1)} %get-tuple-element.11.inverse, f32[4,8,8,128]{3,2,1,0:T(8,128)S(1)} %all_gather.25.block, ...), custom_call_target="tpu_custom_call" | custom-call | tf_op jit(solution)/shard_map/pallas_call | solution.py:299
  96.7 28.0 %all_to_all.24 = f32[16,32,128]{2,1,0:T(8,128)S(1)} all-to-all(f32[16,32,128]{2,1,0:T(8,128)S(1)} %bitcast.15), channel_id=1, replica_groups={{0,2,64,66,128,130,192,194,256,258,320,322,384,386,448,450},{4,6,68,70,..., dimensions={0} | all-to-all | bytes 524288 | tf_op jit(solution)/shard_map/all_to_all | solution.py:327
  124.7 0.7 shard_map.40
  (2 shorter events, 0.0 us)
Async XLA Ops:
  0.0 0.9 copy-start
  1.0 0.7 copy-start.1
  49.1 20.4 %collective-permute-start = (f32[768,128]{1,0:T(8,128)S(1)}, f32[768,128]{1,0:T(8,128)S(1)}, u32[]{:S(2)}, u32[]{:S(2)}) collective-permute-start(f32[768,128]{1,0:T(8,128)S(1)} %bitcast.16), channel_id=1, source_target_pairs={{2,4},{4,2},{6,8},{8,6},{10,12},{12,10},{14,16},{16,14},{18,20},{2... | collective-permute-start | bytes 1179656 | tf_op jit(solution)/shard_map/ppermute | solution.py:337
  51.0 18.5 %collective-permute-start.2 = (f32[256,128]{1,0:T(8,128)S(1)}, f32[256,128]{1,0:T(8,128)S(1)}, u32[]{:S(2)}, u32[]{:S(2)}) collective-permute-start(f32[256,128]{1,0:T(8,128)S(1)} %bitcast.18), channel_id=1, source_target_pairs={{2,5},{3,4},{4,3},{5,2},{6,9},{7,8},{8,7},{9,6},{10,13},{11,12},{1... | collective-permute-start | bytes 393224 | tf_op jit(solution)/shard_map/ppermute | solution.py:338
  57.8 8.4 %collective-permute-start.1 = (f32[256,128]{1,0:T(8,128)S(1)}, f32[256,128]{1,0:T(8,128)S(1)}, u32[]{:S(2)}, u32[]{:S(2)}) collective-permute-start(f32[256,128]{1,0:T(8,128)S(1)} %bitcast.19), channel_id=1, source_target_pairs={{0,1},{1,0},{2,3},{3,2},{4,5},{5,4},{6,7},{7,6},{8,9},{9,8},{10,11... | collective-permute-start | bytes 393224 | tf_op jit(solution)/shard_map/ppermute | solution.py:336
  69.5 0.7 copy-start.2
  75.3 7.4 %collective-permute-start.5 = (f32[4,8,8,128]{3,2,1,0:T(8,128)S(1)}, f32[4,8,8,128]{3,2,1,0:T(8,128)S(1)}, u32[]{:S(2)}, u32[]{:S(2)}) collective-permute-start(f32[4,8,8,128]{3,2,1,0:T(8,128)S(1)} %all_gather.25.block), channel_id=1, source_target_pairs={{0,12},{4,16},{8,20},{12,24},{14,2},{16,28},{18,6},{20,32},{22,10}... | collective-permute-start | bytes 393224 | tf_op jit(solution)/shard_map/ppermute | solution.py:349
  76.6 8.3 %collective-permute-start.4 = (f32[4,8,8,128]{3,2,1,0:T(8,128)S(1)}, f32[4,8,8,128]{3,2,1,0:T(8,128)S(1)}, u32[]{:S(2)}, u32[]{:S(2)}) collective-permute-start(f32[4,8,8,128]{3,2,1,0:T(8,128)S(1)} %all_gather.25.block), channel_id=1, source_target_pairs={{0,8},{4,12},{8,16},{10,2},{12,20},{14,6},{16,24},{18,10},{20,28},... | collective-permute-start | bytes 393224 | tf_op jit(solution)/shard_map/ppermute | solution.py:349
  79.9 9.3 %collective-permute-start.3 = (f32[4,8,8,128]{3,2,1,0:T(8,128)S(1)}, f32[4,8,8,128]{3,2,1,0:T(8,128)S(1)}, u32[]{:S(2)}, u32[]{:S(2)}) collective-permute-start(f32[4,8,8,128]{3,2,1,0:T(8,128)S(1)} %all_gather.25.block), channel_id=1, source_target_pairs={{0,4},{4,8},{6,2},{8,12},{10,6},{12,16},{14,10},{16,20},{18,14},{2... | collective-permute-start | bytes 393224 | tf_op jit(solution)/shard_map/ppermute | solution.py:349

commit v4 on v3

--- a/solution.py
+++ b/solution.py
@@ -58,18 +58,8 @@
 
 
 def each(count, chunk, step):
-    whole = count // chunk
-
-    def body(index, carry):
-        step(index * chunk, chunk)
-        return carry
-
-    if whole == 1:
-        step(0, chunk)
-    else:
-        lax.fori_loop(0, whole, body, 0)
-    if count % chunk:
-        step(whole * chunk, count % chunk)
+    for base in range(0, count, chunk):
+        step(base, min(chunk, count - base))
 
 
 def take(ref, row):
@@ -117,22 +107,30 @@
     ]
 
 
-def pack(residual, potential, out):
+def pack(residual, potential, shifts, out, shift, held, planes, numbers, arrived):
+    copies = [
+        pltpu.make_async_copy(source, target, arrived.at[i])
+        for i, (source, target) in enumerate([(residual, held), (potential, planes), (shifts, numbers)])
+    ]
+    for copy in copies:
+        copy.start()
+    for copy in copies:
+        copy.wait()
+    shift[...] = jnp.full((8, 128), numbers[place()[0]], F32)
     for c in range(PZ):
         rows = slice(4 * c, 4 * c + 4)
         for orbital in range(PX):
             base = (orbital * PZ + c) * 48
             for i in range(8):
-                out[base + 4 * i : base + 4 * i + 4] = residual[orbital, i, rows]
+                out[base + 4 * i : base + 4 * i + 4] = held[orbital, i, rows]
             for i in range(4):
-                out[base + 32 + 4 * i : base + 36 + 4 * i] = potential[i, rows]
-
-
-def down(shifts, cores, beside, cores_half, beside_half, fine_out, source_out, inverse_out, cut, field, potential, source, inverse, start):
+                out[base + 32 + 4 * i : base + 36 + 4 * i] = planes[i, rows]
+
+
+def down(shifts, cores, beside, cores_half, beside_half, fine_out, source, inverse, cut, field, potential, start):
     px, py, c = place()
     size_y = lax.axis_size("dom") // (PX * PZ)
-    shift = shifts[px]
-
+    shift = jnp.concatenate([shifts[...]] * 2, axis=1)
     band = lax.axis_index("band")
 
     def unpack(blocks, halves):
@@ -171,14 +169,8 @@
     each(10, 2, first)
     sweep(start, source, inverse, fine_out, FINE, 8, 2, (0, 1, 1))
 
-    def keep(base, rows):
-        for r in range(rows):
-            for i in range(8):
-                source_out[base + r, i] = source[base + (r + 2), i]
-                inverse_out[base + r, i] = inverse[base + (r + 2), i]
-
-    each(6, 2, keep)
     pool = pooling(256, 128)
+    means = []
     for pair in range(2):
         left = []
         for row in (2 * pair, 2 * pair + 1):
@@ -188,16 +180,17 @@
             left.append(
                 [s + (FINE / 6.0) * t - w * u for s, t, w, u in zip(take(source, row + 3), total, weight, rows[1])]
             )
-        mean = cubes(*left) + cubes(take(potential, 2 * pair + 3), take(potential, 2 * pair + 4))
-        small = times(jnp.concatenate(mean, axis=0), pool)
+        means += cubes(*left) + cubes(take(potential, 2 * pair + 3), take(potential, 2 * pair + 4))
+    small = times(jnp.concatenate(means, axis=0), pool)
+    for pair in range(2):
         for i in range(8):
-            cut[pair, i] = small[8 * i : 8 * i + 8]
+            cut[pair, i] = small[64 * pair + 8 * i : 64 * pair + 8 * i + 8]
 
 
 def up(shifts, fine, source, inverse, block, around, out, weight1, source1, inverse1, middle, other, source2, inverse2, coarse, coarser, work):
     px, py, c = place()
     size_y = lax.axis_size("dom") // (PX * PZ)
-    shift = shifts[px]
+    shift = shifts[...]
 
     def inside(distance):
         return jnp.where((py + distance >= 0) & (py + distance < size_y), OMEGA, 0.0).astype(F32)
@@ -224,55 +217,53 @@
     spread = spreading(128, 128)
     lane = iota((8, 128), 1)
 
-    def shrink(base, pairs):
-        for pair in range(pairs):
-            low = 2 * base + (2 * pair + 2)
-            left, weights = [], []
-            for row in (low, low + 1):
-                rows = [take(middle, row + d) for d in (-1, 0, 1)]
-                w = take(weight1, row)
-                total = stencil(*rows)
-                left.append(
-                    [s + (MIDDLE / 6.0) * t - x * u for s, t, x, u in zip(take(source1, row), total, w, rows[1])]
-                )
-                weights.append(w)
-            mean = cubes(*left) + cubes(*weights)
-            small = times(jnp.concatenate(mean, axis=0), pool)
-            distance = (base + (pair + 1)) // 2 - REACH
-            for i in range(2):
-                s = small[8 * i : 8 * i + 8]
-                w = small[16 + 8 * i : 24 + 8 * i] + (4.0 * COARSE - 4.0 * MIDDLE)
-                v = jnp.where(lane < 64, inside(distance) / jnp.where(lane < 64, w, 1.0), 0.0)
-                source2[base + pair, i] = s
-                inverse2[base + pair, i] = v
-                coarse[base + pair, i] = v * s
-
-    each(12, 4, shrink)
+    means = []
+    for pair in range(12):
+        left, weights = [], []
+        for row in (2 * pair + 2, 2 * pair + 3):
+            rows = [take(middle, row + d) for d in (-1, 0, 1)]
+            w = take(weight1, row)
+            total = stencil(*rows)
+            left.append(
+                [s + (MIDDLE / 6.0) * t - x * u for s, t, x, u in zip(take(source1, row), total, w, rows[1])]
+            )
+            weights.append(w)
+        means += cubes(*left) + cubes(*weights)
+    small = times(jnp.concatenate(means, axis=0), pool)
+    for pair in range(12):
+        for i in range(2):
+            s = small[32 * pair + 8 * i : 32 * pair + 8 * i + 8]
+            w = small[32 * pair + 8 * i + 16 : 32 * pair + 8 * i + 24] + (4.0 * COARSE - 4.0 * MIDDLE)
+            v = jnp.where(lane < 64, inside((pair + 1) // 2 - REACH) / jnp.where(lane < 64, w, 1.0), 0.0)
+            source2[pair, i] = s
+            inverse2[pair, i] = v
+            coarse[pair, i] = v * s
+
     sweep(coarse, source2, inverse2, coarser, COARSE, 10, 10, (1, 1, 1), True)
     sweep(coarser, source2, inverse2, coarse, COARSE, 8, 8, (2, 2, 2), True)
     sweep(coarse, source2, inverse2, coarser, COARSE, 6, 6, (3, 3, 3), True)
 
-    for row in range(3, 9):
-        wide = times(jnp.concatenate(take(coarser, row), axis=0), spread)
-        for fine_row in (2 * row + 2, 2 * row + 3):
-            for i in range(4):
-                other[fine_row, i] = middle[fine_row, i] + wide[8 * (i // 2) : 8 * (i // 2) + 8]
+    wide = times(jnp.concatenate([p for row in range(3, 9) for p in take(coarser, row)], axis=0), spread)
+    for row in range(8, 20):
+        for i in range(4):
+            at = 16 * (row // 2 - 4) + 8 * (i // 2)
+            other[row, i] = middle[row, i] + wide[at : at + 8]
 
     sweep(other, source1, inverse1, middle, MIDDLE, 8, 4, (10, 10, 10))
     sweep(middle, source1, inverse1, other, MIDDLE, 6, 6, (11, 11, 11))
 
     spread = spreading(128, 256)
-    for row in range(4):
-        wide = times(jnp.concatenate(take(other, 11 + 2 * c + row), axis=0), spread)
-        for fine_row in (2 * row, 2 * row + 1):
-            for i in range(8):
-                work[fine_row, i] = fine[fine_row, i] + wide[8 * (i // 2) : 8 * (i // 2) + 8]
+    wide = times(jnp.concatenate([p for row in range(4) for p in take(other, 11 + 2 * c + row)], axis=0), spread)
+    for row in range(8):
+        for i in range(8):
+            at = 32 * (row // 2) + 8 * (i // 2)
+            work[row, i] = fine[row, i] + wide[at : at + 8]
 
     final = work.at[8:14]
-    sweep(work, source, inverse, final, FINE, 6, 2, (0, 1, 0))
+    sweep(work, source, inverse, final, FINE, 6, 2, (0, 1, 2))
     for row in range(4):
         new = sweep_row(
-            [take(final, row + d) for d in range(3)], take(source, row + 1), take(inverse, row + 1), FINE
+            [take(final, row + d) for d in range(3)], take(source, row + 3), take(inverse, row + 3), FINE
         )
         for i, plane in enumerate(new):
             at = (i // 2) * 8 + (i % 2) * 4 + row
@@ -288,24 +279,36 @@
                 out[orbital, i, 4 * c : 4 * c + 4] = blocks[base : base + 4]
 
 
-def call(kernel, outs, scratch=(), smem=False):
-    shapes = [jax.ShapeDtypeStruct(shape, F32) for shape in outs]
-    specs = [pl.BlockSpec(memory_space=pltpu.VMEM)] * len(outs)
+def call(kernel, outs, scratch=(), anywhere=False, others=()):
+    vmem = pl.BlockSpec(memory_space=pltpu.VMEM)
 
     def run(*args):
-        given = [pl.BlockSpec(memory_space=pltpu.VMEM)] * len(args)
-        if smem:
-            given[0] = pl.BlockSpec(memory_space=pltpu.SMEM)
         return pl.pallas_call(
             kernel,
-            out_shape=shapes,
-            in_specs=given,
-            out_specs=specs,
-            scratch_shapes=[pltpu.VMEM(shape, F32) for shape in scratch],
+            out_shape=[jax.ShapeDtypeStruct(shape, F32) for shape in outs],
+            in_specs=[pl.BlockSpec(memory_space=pl.ANY) if anywhere else vmem] * len(args),
+            out_specs=[vmem] * len(outs),
+            scratch_shapes=[pltpu.VMEM(shape, F32) for shape in scratch] + list(others),
             compiler_params=pltpu.CompilerParams(vmem_limit_bytes=40 * 1024 * 1024),
         )(*args)
 
     return run
+
+
+def run_down(*args):
+    return call(
+        down,
+        [(8, 8, 8, 256), (10, 8, 8, 256), (10, 8, 8, 256), (2, 8, 8, 128)],
+        [(12, 8, 8, 256)] + [(10, 8, 8, 256)] * 2,
+    )(*args)
+
+
+def run_up(*args):
+    return call(
+        up,
+        [(512, 128)],
+        [(28, 4, 8, 128)] * 5 + [(12, 2, 8, 128)] * 4 + [(14, 8, 8, 256)],
+    )(*args)[0]
 
 
 def body(residual, potential, shifts):
@@ -329,7 +332,13 @@
     def to_beside(px, py, c):
         return (px, py - 1, 1) if c == 0 else (px, py + 1, 0)
 
-    (packed,) = call(pack, [(768, 128)])(residual, potential)
+    packed, shift = call(
+        pack,
+        [(768, 128), (8, 128)],
+        [(8, 8, 8, 128), (4, 8, 128)],
+        anywhere=True,
+        others=[pltpu.SMEM((8,), F32), pltpu.SemaphoreType.DMA((3,))],
+    )(residual, potential, shifts)
     own = swap_lines(packed)
     half = own.reshape(16, 48, 128)[:, 32:].reshape(256, 128)
     both = ("dom", "band")
@@ -338,12 +347,7 @@
     beside_half = lax.ppermute(half, both, pairs(to_beside, True))
     of_cores = lax.all_gather(own, "dom", axis_index_groups=cores, axis=0)
     of_cores_half = lax.all_gather(own_half, "dom", axis_index_groups=cores, axis=0)
-    fine, source, inverse, cut = call(
-        down,
-        [(8, 8, 8, 256), (6, 8, 8, 256), (6, 8, 8, 256), (2, 8, 8, 128)],
-        [(12, 8, 8, 256)] + [(10, 8, 8, 256)] * 4,
-        smem=True,
-    )(shifts, of_cores, beside, of_cores_half, beside_half)
+    fine, source, inverse, cut = run_down(shift, of_cores, beside, of_cores_half, beside_half)
     block = lax.all_gather(cut, "dom", axis_index_groups=cores, axis=0, tiled=True)
     sent = [
         lax.ppermute(
@@ -354,12 +358,7 @@
         for k in range(1, REACH + 1)
     ]
     around = lax.all_gather(jnp.stack(sent), "dom", axis_index_groups=cores, axis=0)
-    (final,) = call(
-        up,
-        [(512, 128)],
-        [(28, 4, 8, 128)] * 5 + [(12, 2, 8, 128)] * 4 + [(14, 8, 8, 256)],
-        smem=True,
-    )(shifts, fine, source, inverse, block, around)
+    final = run_up(shift, fine, source, inverse, block, around)
     (correction,) = call(unpack, [(8, 8, 8, 128)])(swap_lines(final))
     return correction
 

time: 126 us -> 123 us (0.976)
  Pallas kernels: 9.05 us -> 6.19 us
    pallas_call x4, Pallas kernels: 9.05 us -> 6.19 us  [run(): pl.pallas_call(kernel, out_shape=[jax.ShapeDtypeStruct(shape, F32) for sh...]
where the time goes in v4:
time: 123 us
  blocking collectives  85.4 us (69%)
  starting transfers between devices  18 us (15%)
  waiting for transfers between devices  10.6 us (9%)
  Pallas kernels  6.19 us (5%)
  local copies, waits for them, and re-layouts  2.33 us (2%)
    all_to_all x2, blocking collectives, swap_lines(): lax.all_to_all(value, 'dom', 0, 0, axis_index_groups=lines, tiled=True)  75.4 us
    ppermute x3, starting transfers between devices, body(): lax.ppermute(block, 'dom', pairs(lambda px, py, c, k=k: (px, py + k, 0) i...  7.38 us
    ppermute x1, starting transfers between devices, body(): beside_half = lax.ppermute(half, both, pairs(to_beside, True))  6.76 us
    ppermute x3, waiting for transfers between devices, body(): lax.ppermute(block, 'dom', pairs(lambda px, py, c, k=k: (px, py + k, 0) i...  6.47 us
    pallas_call x4, Pallas kernels, run(): pl.pallas_call(kernel, out_shape=[jax.ShapeDtypeStruct(shape, F32) for sh...  6.19 us
    ppermute x1, waiting for transfers between devices, body(): own_half = lax.ppermute(half, 'band', [(0, 1), (1, 0)])  4.09 us
    all_gather x1, blocking collectives, body(): lax.all_gather(own_half, 'dom', axis_index_groups=cores, axis=0)  3.34 us
  transfers between devices with their start and end apart: 6, of which 3 were waited for; matrix products, arithmetic and copies ran while one was open for 0% of the time, Pallas kernels for 0%

profile of v4, /device:TPU:32, one launch (start us, length us, event | category | flops | bytes accessed | tf_op | source)
XLA Modules:
  0.0 122.6 jit_solution(16281276550581917061)
XLA Ops:
  0.0 0.0 copy-start
  0.0 0.9 copy-done
  1.0 0.0 copy-start.1
  1.0 0.7 copy-done.1
  1.7 0.0 copy-start.2
  1.7 0.7 copy-done.2
  2.3 0.7 shard_map.37
  3.0 47.4 %all_to_all.23 = f32[16,48,128]{2,1,0:T(8,128)S(1)} all-to-all(f32[16,48,128]{2,1,0:T(8,128)S(1)} %bitcast.15), channel_id=1, replica_groups={{0,2,64,66,128,130,192,194,256,258,320,322,384,386,448,450},{4,6,68,70,..., dimensions={0} | all-to-all | bytes 786432 | tf_op jit(solution)/shard_map/all_to_all | solution.py:330
  50.4 1.9 %collective-permute-start = (f32[768,128]{1,0:T(8,128)S(1)}, f32[768,128]{1,0:T(8,128)S(1)}, u32[]{:S(2)}, u32[]{:S(2)}) collective-permute-start(f32[768,128]{1,0:T(8,128)S(1)} %bitcast.16), channel_id=1, source_target_pairs={{2,4},{4,2},{6,8},{8,6},{10,12},{12,10},{14,16},{16,14},{18,20},{2... | collective-permute-start | bytes 1179656 | tf_op jit(solution)/shard_map/ppermute | solution.py:346
  52.3 6.8 %collective-permute-start.2 = (f32[256,128]{1,0:T(8,128)S(1)}, f32[256,128]{1,0:T(8,128)S(1)}, u32[]{:S(2)}, u32[]{:S(2)}) collective-permute-start(f32[256,128]{1,0:T(8,128)S(1)} %bitcast.18), channel_id=1, source_target_pairs={{2,5},{3,4},{4,3},{5,2},{6,9},{7,8},{8,7},{9,6},{10,13},{11,12},{1... | collective-permute-start | bytes 393224 | tf_op jit(solution)/shard_map/ppermute | solution.py:347
  59.1 1.9 %collective-permute-start.1 = (f32[256,128]{1,0:T(8,128)S(1)}, f32[256,128]{1,0:T(8,128)S(1)}, u32[]{:S(2)}, u32[]{:S(2)}) collective-permute-start(f32[256,128]{1,0:T(8,128)S(1)} %bitcast.19), channel_id=1, source_target_pairs={{0,1},{1,0},{2,3},{3,2},{4,5},{5,4},{6,7},{7,6},{8,9},{9,8},{10,11... | collective-permute-start | bytes 393224 | tf_op jit(solution)/shard_map/ppermute | solution.py:345
  61.0 2.4 %all_gather.22.cores = f32[2,768,128]{2,1,0:T(8,128)S(1)} all-gather(f32[1,768,128]{2,1,0:T(8,128)S(1)} %bitcast.17), channel_id=1, replica_groups={{0,2},{4,6},{8,10},{12,14},{16,18},{20,22},{24,26},{28,30},{32,34},{36,..., dimensions={0}, use_global_device_ids=true | all-gather | bytes 1179648 | tf_op jit(solution)/shard_map/all_gather | solution.py:348
  63.4 4.1 %collective-permute-done.1 = f32[256,128]{1,0:T(8,128)S(1)} collective-permute-done((f32[256,128]{1,0:T(8,128)S(1)}, f32[256,128]{1,0:T(8,128)S(1)}, u32[]{:S(2)}, u32[]{:S(2)}) %collective-permute-start.1) | collective-permute-done | bytes 131104 | tf_op jit(solution)/shard_map/ppermute | solution.py:345
  67.5 3.3 %all-gather = f32[512,128]{1,0:T(8,128)S(1)} all-gather(f32[256,128]{1,0:T(8,128)S(1)} %collective-permute-done.1), channel_id=2, replica_groups={{0,2},{4,6},{8,10},{12,14},{16,18},{20,22},{24,26},{28,30},{32,34},{36,..., dimensions={0}, use_global_device_ids=true | all-gather | bytes 393216 | tf_op jit(solution)/shard_map/all_gather | solution.py:349
  70.8 0.0 collective-permute-done.2.beside_half
  70.8 0.0 collective-permute-done.beside
  70.8 2.1 %shard_map.38 = (f32[8,8,8,256]{3,2,1,0:T(8,128)S(1)}, f32[10,8,8,256]{3,2,1,0:T(8,128)S(1)}, f32[10,8,8,256]{3,2,1,0:T(8,128)S(1)}, f32[2,8,8,128]{3,2,1,0:T(8,128)S(1)}) custom-call(f32[8,128]{1,0:T(8,128)S(1)} %get-tuple-element.11.shifts, f32[2,768,128]{2,1,0:T(8,128)S(1)} %all_gather.22.cores, f32[768,128]{1,0:T(8,128)S(1)} %collective-permute-done.beside, ...), custom_call_target="tpu_custom_call" | custom-call | tf_op jit(solution)/shard_map/pallas_call | solution.py:286
  72.9 1.9 %all_gather.25.block = f32[4,8,8,128]{3,2,1,0:T(8,128)S(1)} all-gather(f32[2,8,8,128]{3,2,1,0:T(8,128)S(1)} %get-tuple-element.16), channel_id=1, replica_groups={{0,2},{4,6},{8,10},{12,14},{16,18},{20,22},{24,26},{28,30},{32,34},{36,..., dimensions={0}, use_global_device_ids=true | all-gather | bytes 196608 | tf_op jit(solution)/shard_map/all_gather | solution.py:351
  74.8 1.3 %collective-permute-start.5 = (f32[4,8,8,128]{3,2,1,0:T(8,128)S(1)}, f32[4,8,8,128]{3,2,1,0:T(8,128)S(1)}, u32[]{:S(2)}, u32[]{:S(2)}) collective-permute-start(f32[4,8,8,128]{3,2,1,0:T(8,128)S(1)} %all_gather.25.block), channel_id=1, source_target_pairs={{0,12},{4,16},{8,20},{12,24},{14,2},{16,28},{18,6},{20,32},{22,10}... | collective-permute-start | bytes 393224 | tf_op jit(solution)/shard_map/ppermute | solution.py:353
  76.1 3.3 %collective-permute-start.4 = (f32[4,8,8,128]{3,2,1,0:T(8,128)S(1)}, f32[4,8,8,128]{3,2,1,0:T(8,128)S(1)}, u32[]{:S(2)}, u32[]{:S(2)}) collective-permute-start(f32[4,8,8,128]{3,2,1,0:T(8,128)S(1)} %all_gather.25.block), channel_id=1, source_target_pairs={{0,8},{4,12},{8,16},{10,2},{12,20},{14,6},{16,24},{18,10},{20,28},... | collective-permute-start | bytes 393224 | tf_op jit(solution)/shard_map/ppermute | solution.py:353
  79.5 2.8 %collective-permute-start.3 = (f32[4,8,8,128]{3,2,1,0:T(8,128)S(1)}, f32[4,8,8,128]{3,2,1,0:T(8,128)S(1)}, u32[]{:S(2)}, u32[]{:S(2)}) collective-permute-start(f32[4,8,8,128]{3,2,1,0:T(8,128)S(1)} %all_gather.25.block), channel_id=1, source_target_pairs={{0,4},{4,8},{6,2},{8,12},{10,6},{12,16},{14,10},{16,20},{18,14},{2... | collective-permute-start | bytes 393224 | tf_op jit(solution)/shard_map/ppermute | solution.py:353
  82.2 0.0 collective-permute-done.5
  82.3 2.2 %collective-permute-done.4 = f32[4,8,8,128]{3,2,1,0:T(8,128)S(1)} collective-permute-done((f32[4,8,8,128]{3,2,1,0:T(8,128)S(1)}, f32[4,8,8,128]{3,2,1,0:T(8,128)S(1)}, u32[]{:S(2)}, u32[]{:S(2)}) %collective-permute-start.4) | collective-permute-done | bytes 131104 | tf_op jit(solution)/shard_map/ppermute | solution.py:353
  84.4 4.3 %collective-permute-done.3 = f32[4,8,8,128]{3,2,1,0:T(8,128)S(1)} collective-permute-done((f32[4,8,8,128]{3,2,1,0:T(8,128)S(1)}, f32[4,8,8,128]{3,2,1,0:T(8,128)S(1)}, u32[]{:S(2)}, u32[]{:S(2)}) %collective-permute-start.3) | collective-permute-done | bytes 131104 | tf_op jit(solution)/shard_map/ppermute | solution.py:353
  88.8 2.4 %all-gather.1 = f32[6,4,8,8,128]{4,3,2,1,0:T(8,128)S(1)} all-gather(f32[3,4,8,8,128]{4,3,2,1,0:T(8,128)S(1)} %pad_maximum_fusion), channel_id=3, replica_groups={{0,2},{4,6},{8,10},{12,14},{16,18},{20,22},{24,26},{28,30},{32,34},{36,..., dimensions={0}, use_global_device_ids=true | all-gather | bytes 1179648 | tf_op jit(solution)/shard_map/all_gather | solution.py:360
  91.1 2.7 %shard_map.39 = f32[512,128]{1,0:T(8,128)S(1)} custom-call(f32[8,128]{1,0:T(8,128)S(1)} %get-tuple-element.11.shifts, f32[8,8,8,256]{3,2,1,0:T(8,128)S(1)} %get-tuple-element.13.fine, f32[10,8,8,256]{3,2,1,0:T(8,128)S(1)} %get-tuple-element.14.source, f32[10,8,8,256]{3,2,1,0:T(8,128)S(1)} %get-tuple-element.15.inverse, ...), custom_call_target="tpu_custom_call" | custom-call | tf_op jit(solution)/shard_map/pallas_call | solution.py:286
  93.8 28.0 %all_to_all.24 = f32[16,32,128]{2,1,0:T(8,128)S(1)} all-to-all(f32[16,32,128]{2,1,0:T(8,128)S(1)} %bitcast.12), channel_id=1, replica_groups={{0,2,64,66,128,130,192,194,256,258,320,322,384,386,448,450},{4,6,68,70,..., dimensions={0} | all-to-all | bytes 524288 | tf_op jit(solution)/shard_map/all_to_all | solution.py:330
  121.8 0.7 shard_map.40
  (2 shorter events, 0.0 us)
Async XLA Ops:
  0.0 0.9 copy-start
  1.0 0.7 copy-start.1
  1.7 0.7 copy-start.2
  50.4 20.4 %collective-permute-start = (f32[768,128]{1,0:T(8,128)S(1)}, f32[768,128]{1,0:T(8,128)S(1)}, u32[]{:S(2)}, u32[]{:S(2)}) collective-permute-start(f32[768,128]{1,0:T(8,128)S(1)} %bitcast.16), channel_id=1, source_target_pairs={{2,4},{4,2},{6,8},{8,6},{10,12},{12,10},{14,16},{16,14},{18,20},{2... | collective-permute-start | bytes 1179656 | tf_op jit(solution)/shard_map/ppermute | solution.py:346
  52.3 18.5 %collective-permute-start.2 = (f32[256,128]{1,0:T(8,128)S(1)}, f32[256,128]{1,0:T(8,128)S(1)}, u32[]{:S(2)}, u32[]{:S(2)}) collective-permute-start(f32[256,128]{1,0:T(8,128)S(1)} %bitcast.18), channel_id=1, source_target_pairs={{2,5},{3,4},{4,3},{5,2},{6,9},{7,8},{8,7},{9,6},{10,13},{11,12},{1... | collective-permute-start | bytes 393224 | tf_op jit(solution)/shard_map/ppermute | solution.py:347
  59.1 8.4 %collective-permute-start.1 = (f32[256,128]{1,0:T(8,128)S(1)}, f32[256,128]{1,0:T(8,128)S(1)}, u32[]{:S(2)}, u32[]{:S(2)}) collective-permute-start(f32[256,128]{1,0:T(8,128)S(1)} %bitcast.19), channel_id=1, source_target_pairs={{0,1},{1,0},{2,3},{3,2},{4,5},{5,4},{6,7},{7,6},{8,9},{9,8},{10,11... | collective-permute-start | bytes 393224 | tf_op jit(solution)/shard_map/ppermute | solution.py:345
  74.8 7.4 %collective-permute-start.5 = (f32[4,8,8,128]{3,2,1,0:T(8,128)S(1)}, f32[4,8,8,128]{3,2,1,0:T(8,128)S(1)}, u32[]{:S(2)}, u32[]{:S(2)}) collective-permute-start(f32[4,8,8,128]{3,2,1,0:T(8,128)S(1)} %all_gather.25.block), channel_id=1, source_target_pairs={{0,12},{4,16},{8,20},{12,24},{14,2},{16,28},{18,6},{20,32},{22,10}... | collective-permute-start | bytes 393224 | tf_op jit(solution)/shard_map/ppermute | solution.py:353
  76.1 8.3 %collective-permute-start.4 = (f32[4,8,8,128]{3,2,1,0:T(8,128)S(1)}, f32[4,8,8,128]{3,2,1,0:T(8,128)S(1)}, u32[]{:S(2)}, u32[]{:S(2)}) collective-permute-start(f32[4,8,8,128]{3,2,1,0:T(8,128)S(1)} %all_gather.25.block), channel_id=1, source_target_pairs={{0,8},{4,12},{8,16},{10,2},{12,20},{14,6},{16,24},{18,10},{20,28},... | collective-permute-start | bytes 393224 | tf_op jit(solution)/shard_map/ppermute | solution.py:353
  79.5 9.3 %collective-permute-start.3 = (f32[4,8,8,128]{3,2,1,0:T(8,128)S(1)}, f32[4,8,8,128]{3,2,1,0:T(8,128)S(1)}, u32[]{:S(2)}, u32[]{:S(2)}) collective-permute-start(f32[4,8,8,128]{3,2,1,0:T(8,128)S(1)} %all_gather.25.block), channel_id=1, source_target_pairs={{0,4},{4,8},{6,2},{8,12},{10,6},{12,16},{14,10},{16,20},{18,14},{2... | collective-permute-start | bytes 393224 | tf_op jit(solution)/shard_map/ppermute | solution.py:353

commit v5 on v4

--- a/solution.py
+++ b/solution.py
@@ -286,10 +286,10 @@
         return pl.pallas_call(
             kernel,
             out_shape=[jax.ShapeDtypeStruct(shape, F32) for shape in outs],
-            in_specs=[pl.BlockSpec(memory_space=pl.ANY) if anywhere else vmem] * len(args),
+            in_specs=[pl.BlockSpec(memory_space=pltpu.HBM) if anywhere else vmem] * len(args),
             out_specs=[vmem] * len(outs),
             scratch_shapes=[pltpu.VMEM(shape, F32) for shape in scratch] + list(others),
-            compiler_params=pltpu.CompilerParams(vmem_limit_bytes=40 * 1024 * 1024),
+            compiler_params=pltpu.CompilerParams(vmem_limit_bytes=(56 if anywhere else 40) * 1024 * 1024),
         )(*args)
 
     return run
@@ -321,10 +321,9 @@
         [dom_of(px, py, c, size_y) for c in range(PZ)] for px in range(PX) for py in range(size_y)
     ]
 
-    def pairs(target, bands=False):
+    def pairs(target):
         found = [((px, py, c), target(px, py, c)) for px, py, c in blocks]
-        found = [(dom_of(*a, size_y), dom_of(*b, size_y)) for a, b in found if 0 <= b[1] < size_y]
-        return [(2 * a + n, 2 * b + 1 - n) for a, b in found for n in range(2)] if bands else found
+        return [(dom_of(*a, size_y), dom_of(*b, size_y)) for a, b in found if 0 <= b[1] < size_y]
 
     def swap_lines(value):
         return lax.all_to_all(value, "dom", 0, 0, axis_index_groups=lines, tiled=True)
@@ -341,10 +340,9 @@
     )(residual, potential, shifts)
     own = swap_lines(packed)
     half = own.reshape(16, 48, 128)[:, 32:].reshape(256, 128)
-    both = ("dom", "band")
+    beside = lax.ppermute(own, "dom", pairs(to_beside))
     own_half = lax.ppermute(half, "band", [(0, 1), (1, 0)])
-    beside = lax.ppermute(own, "dom", pairs(to_beside))
-    beside_half = lax.ppermute(half, both, pairs(to_beside, True))
+    beside_half = lax.ppermute(own_half, "dom", pairs(to_beside))
     of_cores = lax.all_gather(own, "dom", axis_index_groups=cores, axis=0)
     of_cores_half = lax.all_gather(own_half, "dom", axis_index_groups=cores, axis=0)
     fine, source, inverse, cut = run_down(shift, of_cores, beside, of_cores_half, beside_half)
@@ -355,9 +353,9 @@
             "dom",
             pairs(lambda px, py, c, k=k: (px, py + k, 0) if c == 0 else (px, py - k, 1)),
         )
-        for k in range(1, REACH + 1)
-    ]
-    around = lax.all_gather(jnp.stack(sent), "dom", axis_index_groups=cores, axis=0)
+        for k in range(REACH, 0, -1)
+    ]
+    around = lax.all_gather(jnp.stack(sent[::-1]), "dom", axis_index_groups=cores, axis=0)
     final = run_up(shift, fine, source, inverse, block, around)
     (correction,) = call(unpack, [(8, 8, 8, 128)])(swap_lines(final))
     return correction

time: 123 us -> 123 us (level)
  waiting for transfers between devices: 10.6 us -> 7.57 us
  blocking collectives: 85.4 us -> 88.4 us
  local copies, waits for them, and re-layouts: 2.33 us -> 0.01 us
    all_gather x1, blocking collectives: 1.92 us -> 5.94 us  [body(): lax.all_gather(cut, 'dom', axis_index_groups=cores, axis=0, tiled=True)]
    ppermute x1, waiting for transfers between devices: 4.09 us -> 1.44 us  [body(): own_half = lax.ppermute(half, 'band', [(0, 1), (1, 0)])]
    unnamed x6 -> x2, local copies, waits for them, and re-layouts: 2.32 us -> 0.01 us
    ppermute x1, starting transfers between devices: 6.76 us -> 4.61 us  [body(): beside_half = lax.ppermute(own_half, 'dom', pairs(to_beside))]
    ppermute x3, starting transfers between devices: 7.38 us -> 9.21 us  [body(): lax.ppermute(block, 'dom', pairs(lambda px, py, c, k=k: (px, py + k, 0) i...]
    ppermute x1, starting transfers between devices: 1.92 us -> 3.48 us  [body(): own_half = lax.ppermute(half, 'band', [(0, 1), (1, 0)])]
  transfers between devices with their start and end apart: 6 -> 6, of which waited for: 3 -> 4; matrix products, arithmetic and copies ran while one was open for 0% -> 0% of each run, Pallas kernels for 0% -> 0%
where the time goes in v5:
time: 123 us
  blocking collectives  88.4 us (72%)
  starting transfers between devices  19.2 us (16%)
  waiting for transfers between devices  7.57 us (6%)
  Pallas kernels  7.32 us (6%)
    all_to_all x2, blocking collectives, swap_lines(): lax.all_to_all(value, 'dom', 0, 0, axis_index_groups=lines, tiled=True)  75.4 us
    ppermute x3, starting transfers between devices, body(): lax.ppermute(block, 'dom', pairs(lambda px, py, c, k=k: (px, py + k, 0) i...  9.21 us
    pallas_call x4, Pallas kernels, run(): pl.pallas_call(kernel, out_shape=[jax.ShapeDtypeStruct(shape, F32) for sh...  7.32 us
    all_gather x1, blocking collectives, body(): lax.all_gather(cut, 'dom', axis_index_groups=cores, axis=0, tiled=True)  5.94 us
    ppermute x3, waiting for transfers between devices, body(): lax.ppermute(block, 'dom', pairs(lambda px, py, c, k=k: (px, py + k, 0) i...  5.83 us
    ppermute x1, starting transfers between devices, body(): beside_half = lax.ppermute(own_half, 'dom', pairs(to_beside))  4.61 us
    ppermute x1, starting transfers between devices, body(): own_half = lax.ppermute(half, 'band', [(0, 1), (1, 0)])  3.48 us
    all_gather x1, blocking collectives, body(): of_cores = lax.all_gather(own, 'dom', axis_index_groups=cores, axis=0)  2.59 us
  transfers between devices with their start and end apart: 6, of which 4 were waited for; matrix products, arithmetic and copies ran while one was open for 0% of the time, Pallas kernels for 0%

profile of v5, /device:TPU:32, one launch (start us, length us, event | category | flops | bytes accessed | tf_op | source)
XLA Modules:
  0.0 122.6 jit_solution(18206391048805958190)
XLA Ops:
  0.0 1.8 %shard_map.37 = (f32[768,128]{1,0:T(8,128)}, f32[8,128]{1,0:T(8,128)}) custom-call(f32[8,8,8,128]{3,2,1,0:T(8,128)} %residual.1, f32[4,8,128]{2,1,0:T(8,128)} %potential.1, f32[8]{0:T(128)} %shifts.1), custom_call_target="tpu_custom_call" | custom-call | tf_op jit(solution)/shard_map/pallas_call | solution.py:286
  1.8 47.6 %all_to_all.23 = f32[16,48,128]{2,1,0:T(8,128)S(1)} all-to-all(f32[16,48,128]{2,1,0:T(8,128)} %bitcast.17), channel_id=1, replica_groups={{0,2,64,66,128,130,192,194,256,258,320,322,384,386,448,450},{4,6,68,70,..., dimensions={0} | all-to-all | bytes 786432 | tf_op jit(solution)/shard_map/all_to_all | solution.py:329
  49.4 3.5 %collective-permute-start.1 = (f32[256,128]{1,0:T(8,128)S(1)}, f32[256,128]{1,0:T(8,128)S(1)}, u32[]{:S(2)}, u32[]{:S(2)}) collective-permute-start(f32[256,128]{1,0:T(8,128)S(1)} %bitcast.18), channel_id=1, source_target_pairs={{0,1},{1,0},{2,3},{3,2},{4,5},{5,4},{6,7},{7,6},{8,9},{9,8},{10,11... | collective-permute-start | bytes 393224 | tf_op jit(solution)/shard_map/ppermute | solution.py:344
  52.9 1.9 %collective-permute-start = (f32[768,128]{1,0:T(8,128)S(1)}, f32[768,128]{1,0:T(8,128)S(1)}, u32[]{:S(2)}, u32[]{:S(2)}) collective-permute-start(f32[768,128]{1,0:T(8,128)S(1)} %bitcast.15), channel_id=1, source_target_pairs={{2,4},{4,2},{6,8},{8,6},{10,12},{12,10},{14,16},{16,14},{18,20},{2... | collective-permute-start | bytes 1179656 | tf_op jit(solution)/shard_map/ppermute | solution.py:343
  54.8 1.4 %collective-permute-done.1 = f32[256,128]{1,0:T(8,128)S(1)} collective-permute-done((f32[256,128]{1,0:T(8,128)S(1)}, f32[256,128]{1,0:T(8,128)S(1)}, u32[]{:S(2)}, u32[]{:S(2)}) %collective-permute-start.1) | collective-permute-done | bytes 131104 | tf_op jit(solution)/shard_map/ppermute | solution.py:344
  56.3 4.6 %collective-permute-start.2 = (f32[256,128]{1,0:T(8,128)S(1)}, f32[256,128]{1,0:T(8,128)S(1)}, u32[]{:S(2)}, u32[]{:S(2)}) collective-permute-start(f32[256,128]{1,0:T(8,128)S(1)} %collective-permute-done.1), channel_id=1, source_target_pairs={{2,4},{4,2},{6,8},{8,6},{10,12},{12,10},{14,16},{16,14},{18,20},{2... | collective-permute-start | bytes 393224 | tf_op jit(solution)/shard_map/ppermute | solution.py:345
  60.9 2.6 %all_gather.22.cores = f32[2,768,128]{2,1,0:T(8,128)S(1)} all-gather(f32[1,768,128]{2,1,0:T(8,128)S(1)} %bitcast.16), channel_id=1, replica_groups={{0,2},{4,6},{8,10},{12,14},{16,18},{20,22},{24,26},{28,30},{32,34},{36,..., dimensions={0}, use_global_device_ids=true | all-gather | bytes 1179648 | tf_op jit(solution)/shard_map/all_gather | solution.py:346
  63.5 0.0 copy-start
  63.5 2.1 %all-gather = f32[512,128]{1,0:T(8,128)S(1)} all-gather(f32[256,128]{1,0:T(8,128)S(1)} %collective-permute-done.1), channel_id=2, replica_groups={{0,2},{4,6},{8,10},{12,14},{16,18},{20,22},{24,26},{28,30},{32,34},{36,..., dimensions={0}, use_global_device_ids=true | all-gather | bytes 393216 | tf_op jit(solution)/shard_map/all_gather | solution.py:347
  65.6 0.3 collective-permute-done.2.beside_half
  65.9 0.0 collective-permute-done.beside
  65.9 0.0 copy-done
  65.9 2.1 %shard_map.38 = (f32[8,8,8,256]{3,2,1,0:T(8,128)S(1)}, f32[10,8,8,256]{3,2,1,0:T(8,128)S(1)}, f32[10,8,8,256]{3,2,1,0:T(8,128)S(1)}, f32[2,8,8,128]{3,2,1,0:T(8,128)S(1)}) custom-call(f32[8,128]{1,0:T(8,128)S(1)} %copy-done, f32[2,768,128]{2,1,0:T(8,128)S(1)} %all_gather.22.cores, f32[768,128]{1,0:T(8,128)S(1)} %collective-permute-done.beside, ...), custom_call_target="tpu_custom_call" | custom-call | tf_op jit(solution)/shard_map/pallas_call | solution.py:286
  68.0 5.9 %all_gather.25.block = f32[4,8,8,128]{3,2,1,0:T(8,128)S(1)} all-gather(f32[2,8,8,128]{3,2,1,0:T(8,128)S(1)} %get-tuple-element.16), channel_id=1, replica_groups={{0,2},{4,6},{8,10},{12,14},{16,18},{20,22},{24,26},{28,30},{32,34},{36,..., dimensions={0}, use_global_device_ids=true | all-gather | bytes 196608 | tf_op jit(solution)/shard_map/all_gather | solution.py:349
  73.9 1.3 %collective-permute-start.5 = (f32[4,8,8,128]{3,2,1,0:T(8,128)S(1)}, f32[4,8,8,128]{3,2,1,0:T(8,128)S(1)}, u32[]{:S(2)}, u32[]{:S(2)}) collective-permute-start(f32[4,8,8,128]{3,2,1,0:T(8,128)S(1)} %all_gather.25.block), channel_id=1, source_target_pairs={{0,12},{4,16},{8,20},{12,24},{14,2},{16,28},{18,6},{20,32},{22,10}... | collective-permute-start | bytes 393224 | tf_op jit(solution)/shard_map/ppermute | solution.py:351
  75.2 4.5 %collective-permute-start.4 = (f32[4,8,8,128]{3,2,1,0:T(8,128)S(1)}, f32[4,8,8,128]{3,2,1,0:T(8,128)S(1)}, u32[]{:S(2)}, u32[]{:S(2)}) collective-permute-start(f32[4,8,8,128]{3,2,1,0:T(8,128)S(1)} %all_gather.25.block), channel_id=1, source_target_pairs={{0,8},{4,12},{8,16},{10,2},{12,20},{14,6},{16,24},{18,10},{20,28},... | collective-permute-start | bytes 393224 | tf_op jit(solution)/shard_map/ppermute | solution.py:351
  79.8 3.4 %collective-permute-start.3 = (f32[4,8,8,128]{3,2,1,0:T(8,128)S(1)}, f32[4,8,8,128]{3,2,1,0:T(8,128)S(1)}, u32[]{:S(2)}, u32[]{:S(2)}) collective-permute-start(f32[4,8,8,128]{3,2,1,0:T(8,128)S(1)} %all_gather.25.block), channel_id=1, source_target_pairs={{0,4},{4,8},{6,2},{8,12},{10,6},{12,16},{14,10},{16,20},{18,14},{2... | collective-permute-start | bytes 393224 | tf_op jit(solution)/shard_map/ppermute | solution.py:351
  83.2 0.0 collective-permute-done.5
  83.2 2.2 %collective-permute-done.4 = f32[4,8,8,128]{3,2,1,0:T(8,128)S(1)} collective-permute-done((f32[4,8,8,128]{3,2,1,0:T(8,128)S(1)}, f32[4,8,8,128]{3,2,1,0:T(8,128)S(1)}, u32[]{:S(2)}, u32[]{:S(2)}) %collective-permute-start.4) | collective-permute-done | bytes 131104 | tf_op jit(solution)/shard_map/ppermute | solution.py:351
  85.4 3.6 %collective-permute-done.3 = f32[4,8,8,128]{3,2,1,0:T(8,128)S(1)} collective-permute-done((f32[4,8,8,128]{3,2,1,0:T(8,128)S(1)}, f32[4,8,8,128]{3,2,1,0:T(8,128)S(1)}, u32[]{:S(2)}, u32[]{:S(2)}) %collective-permute-start.3) | collective-permute-done | bytes 131104 | tf_op jit(solution)/shard_map/ppermute | solution.py:351
  89.1 2.4 %all-gather.1 = f32[6,4,8,8,128]{4,3,2,1,0:T(8,128)S(1)} all-gather(f32[3,4,8,8,128]{4,3,2,1,0:T(8,128)S(1)} %pad_maximum_fusion), channel_id=3, replica_groups={{0,2},{4,6},{8,10},{12,14},{16,18},{20,22},{24,26},{28,30},{32,34},{36,..., dimensions={0}, use_global_device_ids=true | all-gather | bytes 1179648 | tf_op jit(solution)/shard_map/all_gather | solution.py:358
  91.4 2.7 %shard_map.39 = f32[512,128]{1,0:T(8,128)S(1)} custom-call(f32[8,128]{1,0:T(8,128)S(1)} %copy-done, f32[8,8,8,256]{3,2,1,0:T(8,128)S(1)} %get-tuple-element.13.fine, f32[10,8,8,256]{3,2,1,0:T(8,128)S(1)} %get-tuple-element.14.source, f32[10,8,8,256]{3,2,1,0:T(8,128)S(1)} %get-tuple-element.15.inverse, f32[4,8,8,128]{3,2,1,0:T(8,128)S(1)} %all_gather.25.block, ...), custom_call_target="tpu_custom_call" | custom-call | tf_op jit(solution)/shard_map/pallas_call | solution.py:286
  94.1 27.8 %all_to_all.24 = f32[16,32,128]{2,1,0:T(8,128)S(1)} all-to-all(f32[16,32,128]{2,1,0:T(8,128)S(1)} %bitcast.12), channel_id=1, replica_groups={{0,2,64,66,128,130,192,194,256,258,320,322,384,386,448,450},{4,6,68,70,..., dimensions={0} | all-to-all | bytes 524288 | tf_op jit(solution)/shard_map/all_to_all | solution.py:329
  121.9 0.7 shard_map.40
  (2 shorter events, 0.0 us)
Async XLA Ops:
  49.4 6.9 %collective-permute-start.1 = (f32[256,128]{1,0:T(8,128)S(1)}, f32[256,128]{1,0:T(8,128)S(1)}, u32[]{:S(2)}, u32[]{:S(2)}) collective-permute-start(f32[256,128]{1,0:T(8,128)S(1)} %bitcast.18), channel_id=1, source_target_pairs={{0,1},{1,0},{2,3},{3,2},{4,5},{5,4},{6,7},{7,6},{8,9},{9,8},{10,11... | collective-permute-start | bytes 393224 | tf_op jit(solution)/shard_map/ppermute | solution.py:344
  52.9 13.0 %collective-permute-start = (f32[768,128]{1,0:T(8,128)S(1)}, f32[768,128]{1,0:T(8,128)S(1)}, u32[]{:S(2)}, u32[]{:S(2)}) collective-permute-start(f32[768,128]{1,0:T(8,128)S(1)} %bitcast.15), channel_id=1, source_target_pairs={{2,4},{4,2},{6,8},{8,6},{10,12},{12,10},{14,16},{16,14},{18,20},{2... | collective-permute-start | bytes 1179656 | tf_op jit(solution)/shard_map/ppermute | solution.py:343
  56.3 9.6 %collective-permute-start.2 = (f32[256,128]{1,0:T(8,128)S(1)}, f32[256,128]{1,0:T(8,128)S(1)}, u32[]{:S(2)}, u32[]{:S(2)}) collective-permute-start(f32[256,128]{1,0:T(8,128)S(1)} %collective-permute-done.1), channel_id=1, source_target_pairs={{2,4},{4,2},{6,8},{8,6},{10,12},{12,10},{14,16},{16,14},{18,20},{2... | collective-permute-start | bytes 393224 | tf_op jit(solution)/shard_map/ppermute | solution.py:345
  63.5 2.4 %copy-start = (f32[8,128]{1,0:T(8,128)S(1)}, f32[8,128]{1,0:T(8,128)}, u32[]{:S(2)}) copy-start(f32[8,128]{1,0:T(8,128)} %get-tuple-element.11.shifts) | copy-start | bytes 12292
  73.9 9.2 %collective-permute-start.5 = (f32[4,8,8,128]{3,2,1,0:T(8,128)S(1)}, f32[4,8,8,128]{3,2,1,0:T(8,128)S(1)}, u32[]{:S(2)}, u32[]{:S(2)}) collective-permute-start(f32[4,8,8,128]{3,2,1,0:T(8,128)S(1)} %all_gather.25.block), channel_id=1, source_target_pairs={{0,12},{4,16},{8,20},{12,24},{14,2},{16,28},{18,6},{20,32},{22,10}... | collective-permute-start | bytes 393224 | tf_op jit(solution)/shard_map/ppermute | solution.py:351
  75.2 10.2 %collective-permute-start.4 = (f32[4,8,8,128]{3,2,1,0:T(8,128)S(1)}, f32[4,8,8,128]{3,2,1,0:T(8,128)S(1)}, u32[]{:S(2)}, u32[]{:S(2)}) collective-permute-start(f32[4,8,8,128]{3,2,1,0:T(8,128)S(1)} %all_gather.25.block), channel_id=1, source_target_pairs={{0,8},{4,12},{8,16},{10,2},{12,20},{14,6},{16,24},{18,10},{20,28},... | collective-permute-start | bytes 393224 | tf_op jit(solution)/shard_map/ppermute | solution.py:351
  79.8 9.3 %collective-permute-start.3 = (f32[4,8,8,128]{3,2,1,0:T(8,128)S(1)}, f32[4,8,8,128]{3,2,1,0:T(8,128)S(1)}, u32[]{:S(2)}, u32[]{:S(2)}) collective-permute-start(f32[4,8,8,128]{3,2,1,0:T(8,128)S(1)} %all_gather.25.block), channel_id=1, source_target_pairs={{0,4},{4,8},{6,2},{8,12},{10,6},{12,16},{14,10},{16,20},{18,14},{2... | collective-permute-start | bytes 393224 | tf_op jit(solution)/shard_map/ppermute | solution.py:351

commit v6 on v4

--- a/solution.py
+++ b/solution.py
@@ -109,22 +109,29 @@
 
 def pack(residual, potential, shifts, out, shift, held, planes, numbers, arrived):
     copies = [
-        pltpu.make_async_copy(source, target, arrived.at[i])
-        for i, (source, target) in enumerate([(residual, held), (potential, planes), (shifts, numbers)])
+        pltpu.make_async_copy(potential, planes, arrived.at[PX]),
+        pltpu.make_async_copy(shifts, numbers, arrived.at[PX + 1]),
+    ]
+    copies += [
+        pltpu.make_async_copy(residual.at[i], held.at[i], arrived.at[i]) for i in range(PX)
     ]
     for copy in copies:
         copy.start()
-    for copy in copies:
-        copy.wait()
+    copies[0].wait()
+    for c in range(PZ):
+        for i in range(4):
+            both = planes[i, 4 * c : 4 * c + 4]
+            for orbital in range(PX):
+                base = (orbital * PZ + c) * 48 + 32 + 4 * i
+                out[base : base + 4] = both
+    copies[1].wait()
     shift[...] = jnp.full((8, 128), numbers[place()[0]], F32)
-    for c in range(PZ):
-        rows = slice(4 * c, 4 * c + 4)
-        for orbital in range(PX):
+    for orbital in range(PX):
+        copies[2 + orbital].wait()
+        for c in range(PZ):
             base = (orbital * PZ + c) * 48
             for i in range(8):
-                out[base + 4 * i : base + 4 * i + 4] = held[orbital, i, rows]
-            for i in range(4):
-                out[base + 32 + 4 * i : base + 36 + 4 * i] = planes[i, rows]
+                out[base + 4 * i : base + 4 * i + 4] = held[orbital, i, 4 * c : 4 * c + 4]
 
 
 def down(shifts, cores, beside, cores_half, beside_half, fine_out, source, inverse, cut, field, potential, start):
@@ -285,7 +292,7 @@
     def run(*args):
         return pl.pallas_call(
             kernel,
-            out_shape=[jax.ShapeDtypeStruct(shape, F32) for shape in outs],
+            out_shape=[(pltpu.VMEM if anywhere else jax.ShapeDtypeStruct)(shape, F32) for shape in outs],
             in_specs=[pl.BlockSpec(memory_space=pl.ANY) if anywhere else vmem] * len(args),
             out_specs=[vmem] * len(outs),
             scratch_shapes=[pltpu.VMEM(shape, F32) for shape in scratch] + list(others),
@@ -337,8 +344,8 @@
         [(768, 128), (8, 128)],
         [(8, 8, 8, 128), (4, 8, 128)],
         anywhere=True,
-        others=[pltpu.SMEM((8,), F32), pltpu.SemaphoreType.DMA((3,))],
-    )(residual, potential, shifts)
+        others=[pltpu.SMEM((8,), F32), pltpu.SemaphoreType.DMA((PX + 2,))],
+    )(*[pltpu.with_memory_space_constraint(x, pltpu.HBM) for x in (residual, potential, shifts)])
     own = swap_lines(packed)
     half = own.reshape(16, 48, 128)[:, 32:].reshape(256, 128)
     both = ("dom", "band")

time: 123 us -> 121 us (0.984)
  local copies, waits for them, and re-layouts: 2.33 us -> 0.01 us
    unnamed x6 -> x0, local copies, waits for them, and re-layouts: 2.32 us -> none
where the time goes in v6:
time: 121 us
  blocking collectives  85.4 us (71%)
  starting transfers between devices  18 us (15%)
  waiting for transfers between devices  10.6 us (9%)
  Pallas kernels  6.51 us (5%)
    all_to_all x2, blocking collectives, swap_lines(): lax.all_to_all(value, 'dom', 0, 0, axis_index_groups=lines, tiled=True)  75.4 us
    ppermute x3, starting transfers between devices, body(): lax.ppermute(block, 'dom', pairs(lambda px, py, c, k=k: (px, py + k, 0) i...  7.38 us
    ppermute x1, starting transfers between devices, body(): beside_half = lax.ppermute(half, both, pairs(to_beside, True))  6.76 us
    pallas_call x4, Pallas kernels, run(): pl.pallas_call(kernel, out_shape=[(pltpu.VMEM if anywhere else jax.ShapeD...  6.51 us
    ppermute x3, waiting for transfers between devices, body(): lax.ppermute(block, 'dom', pairs(lambda px, py, c, k=k: (px, py + k, 0) i...  6.47 us
    ppermute x1, waiting for transfers between devices, body(): own_half = lax.ppermute(half, 'band', [(0, 1), (1, 0)])  4.09 us
    all_gather x1, blocking collectives, body(): lax.all_gather(own_half, 'dom', axis_index_groups=cores, axis=0)  3.34 us
  transfers between devices with their start and end apart: 6, of which 3 were waited for; matrix products, arithmetic and copies ran while one was open for 0% of the time, Pallas kernels for 0%

profile of v6, /device:TPU:32, one launch (start us, length us, event | category | flops | bytes accessed | tf_op | source)
XLA Modules:
  0.0 120.6 jit_solution(12210445397572858661)
XLA Ops:
  0.0 1.0 shard_map.37
  1.0 47.4 %all_to_all.23 = f32[16,48,128]{2,1,0:T(8,128)S(1)} all-to-all(f32[16,48,128]{2,1,0:T(8,128)S(1)} %bitcast.15), channel_id=1, replica_groups={{0,2,64,66,128,130,192,194,256,258,320,322,384,386,448,450},{4,6,68,70,..., dimensions={0} | all-to-all | bytes 786432 | tf_op jit(solution)/shard_map/all_to_all | solution.py:337
  48.4 1.9 %collective-permute-start = (f32[768,128]{1,0:T(8,128)S(1)}, f32[768,128]{1,0:T(8,128)S(1)}, u32[]{:S(2)}, u32[]{:S(2)}) collective-permute-start(f32[768,128]{1,0:T(8,128)S(1)} %bitcast.16), channel_id=1, source_target_pairs={{2,4},{4,2},{6,8},{8,6},{10,12},{12,10},{14,16},{16,14},{18,20},{2... | collective-permute-start | bytes 1179656 | tf_op jit(solution)/shard_map/ppermute | solution.py:353
  50.3 6.8 %collective-permute-start.2 = (f32[256,128]{1,0:T(8,128)S(1)}, f32[256,128]{1,0:T(8,128)S(1)}, u32[]{:S(2)}, u32[]{:S(2)}) collective-permute-start(f32[256,128]{1,0:T(8,128)S(1)} %bitcast.18), channel_id=1, source_target_pairs={{2,5},{3,4},{4,3},{5,2},{6,9},{7,8},{8,7},{9,6},{10,13},{11,12},{1... | collective-permute-start | bytes 393224 | tf_op jit(solution)/shard_map/ppermute | solution.py:354
  57.1 1.9 %collective-permute-start.1 = (f32[256,128]{1,0:T(8,128)S(1)}, f32[256,128]{1,0:T(8,128)S(1)}, u32[]{:S(2)}, u32[]{:S(2)}) collective-permute-start(f32[256,128]{1,0:T(8,128)S(1)} %bitcast.19), channel_id=1, source_target_pairs={{0,1},{1,0},{2,3},{3,2},{4,5},{5,4},{6,7},{7,6},{8,9},{9,8},{10,11... | collective-permute-start | bytes 393224 | tf_op jit(solution)/shard_map/ppermute | solution.py:352
  59.0 2.4 %all_gather.22.cores = f32[2,768,128]{2,1,0:T(8,128)S(1)} all-gather(f32[1,768,128]{2,1,0:T(8,128)S(1)} %bitcast.17), channel_id=1, replica_groups={{0,2},{4,6},{8,10},{12,14},{16,18},{20,22},{24,26},{28,30},{32,34},{36,..., dimensions={0}, use_global_device_ids=true | all-gather | bytes 1179648 | tf_op jit(solution)/shard_map/all_gather | solution.py:355
  61.4 4.1 %collective-permute-done.1 = f32[256,128]{1,0:T(8,128)S(1)} collective-permute-done((f32[256,128]{1,0:T(8,128)S(1)}, f32[256,128]{1,0:T(8,128)S(1)}, u32[]{:S(2)}, u32[]{:S(2)}) %collective-permute-start.1) | collective-permute-done | bytes 131104 | tf_op jit(solution)/shard_map/ppermute | solution.py:352
  65.4 3.3 %all-gather = f32[512,128]{1,0:T(8,128)S(1)} all-gather(f32[256,128]{1,0:T(8,128)S(1)} %collective-permute-done.1), channel_id=2, replica_groups={{0,2},{4,6},{8,10},{12,14},{16,18},{20,22},{24,26},{28,30},{32,34},{36,..., dimensions={0}, use_global_device_ids=true | all-gather | bytes 393216 | tf_op jit(solution)/shard_map/all_gather | solution.py:356
  68.8 0.0 collective-permute-done.2.beside_half
  68.8 0.0 collective-permute-done.beside
  68.8 2.1 %shard_map.38 = (f32[8,8,8,256]{3,2,1,0:T(8,128)S(1)}, f32[10,8,8,256]{3,2,1,0:T(8,128)S(1)}, f32[10,8,8,256]{3,2,1,0:T(8,128)S(1)}, f32[2,8,8,128]{3,2,1,0:T(8,128)S(1)}) custom-call(f32[8,128]{1,0:T(8,128)S(1)} %get-tuple-element.11.shifts, f32[2,768,128]{2,1,0:T(8,128)S(1)} %all_gather.22.cores, f32[768,128]{1,0:T(8,128)S(1)} %collective-permute-done.beside, ...), custom_call_target="tpu_custom_call" | custom-call | tf_op jit(solution)/shard_map/pallas_call | solution.py:293
  70.9 1.9 %all_gather.25.block = f32[4,8,8,128]{3,2,1,0:T(8,128)S(1)} all-gather(f32[2,8,8,128]{3,2,1,0:T(8,128)S(1)} %get-tuple-element.16), channel_id=1, replica_groups={{0,2},{4,6},{8,10},{12,14},{16,18},{20,22},{24,26},{28,30},{32,34},{36,..., dimensions={0}, use_global_device_ids=true | all-gather | bytes 196608 | tf_op jit(solution)/shard_map/all_gather | solution.py:358
  72.8 1.3 %collective-permute-start.5 = (f32[4,8,8,128]{3,2,1,0:T(8,128)S(1)}, f32[4,8,8,128]{3,2,1,0:T(8,128)S(1)}, u32[]{:S(2)}, u32[]{:S(2)}) collective-permute-start(f32[4,8,8,128]{3,2,1,0:T(8,128)S(1)} %all_gather.25.block), channel_id=1, source_target_pairs={{0,12},{4,16},{8,20},{12,24},{14,2},{16,28},{18,6},{20,32},{22,10}... | collective-permute-start | bytes 393224 | tf_op jit(solution)/shard_map/ppermute | solution.py:360
  74.1 3.3 %collective-permute-start.4 = (f32[4,8,8,128]{3,2,1,0:T(8,128)S(1)}, f32[4,8,8,128]{3,2,1,0:T(8,128)S(1)}, u32[]{:S(2)}, u32[]{:S(2)}) collective-permute-start(f32[4,8,8,128]{3,2,1,0:T(8,128)S(1)} %all_gather.25.block), channel_id=1, source_target_pairs={{0,8},{4,12},{8,16},{10,2},{12,20},{14,6},{16,24},{18,10},{20,28},... | collective-permute-start | bytes 393224 | tf_op jit(solution)/shard_map/ppermute | solution.py:360
  77.5 2.8 %collective-permute-start.3 = (f32[4,8,8,128]{3,2,1,0:T(8,128)S(1)}, f32[4,8,8,128]{3,2,1,0:T(8,128)S(1)}, u32[]{:S(2)}, u32[]{:S(2)}) collective-permute-start(f32[4,8,8,128]{3,2,1,0:T(8,128)S(1)} %all_gather.25.block), channel_id=1, source_target_pairs={{0,4},{4,8},{6,2},{8,12},{10,6},{12,16},{14,10},{16,20},{18,14},{2... | collective-permute-start | bytes 393224 | tf_op jit(solution)/shard_map/ppermute | solution.py:360
  80.2 0.0 collective-permute-done.5
  80.2 2.2 %collective-permute-done.4 = f32[4,8,8,128]{3,2,1,0:T(8,128)S(1)} collective-permute-done((f32[4,8,8,128]{3,2,1,0:T(8,128)S(1)}, f32[4,8,8,128]{3,2,1,0:T(8,128)S(1)}, u32[]{:S(2)}, u32[]{:S(2)}) %collective-permute-start.4) | collective-permute-done | bytes 131104 | tf_op jit(solution)/shard_map/ppermute | solution.py:360
  82.4 4.3 %collective-permute-done.3 = f32[4,8,8,128]{3,2,1,0:T(8,128)S(1)} collective-permute-done((f32[4,8,8,128]{3,2,1,0:T(8,128)S(1)}, f32[4,8,8,128]{3,2,1,0:T(8,128)S(1)}, u32[]{:S(2)}, u32[]{:S(2)}) %collective-permute-start.3) | collective-permute-done | bytes 131104 | tf_op jit(solution)/shard_map/ppermute | solution.py:360
  86.8 2.4 %all-gather.1 = f32[6,4,8,8,128]{4,3,2,1,0:T(8,128)S(1)} all-gather(f32[3,4,8,8,128]{4,3,2,1,0:T(8,128)S(1)} %pad_maximum_fusion), channel_id=3, replica_groups={{0,2},{4,6},{8,10},{12,14},{16,18},{20,22},{24,26},{28,30},{32,34},{36,..., dimensions={0}, use_global_device_ids=true | all-gather | bytes 1179648 | tf_op jit(solution)/shard_map/all_gather | solution.py:367
  89.1 2.7 %shard_map.39 = f32[512,128]{1,0:T(8,128)S(1)} custom-call(f32[8,128]{1,0:T(8,128)S(1)} %get-tuple-element.11.shifts, f32[8,8,8,256]{3,2,1,0:T(8,128)S(1)} %get-tuple-element.13.fine, f32[10,8,8,256]{3,2,1,0:T(8,128)S(1)} %get-tuple-element.14.source, f32[10,8,8,256]{3,2,1,0:T(8,128)S(1)} %get-tuple-element.15.inverse, ...), custom_call_target="tpu_custom_call" | custom-call | tf_op jit(solution)/shard_map/pallas_call | solution.py:293
  91.8 28.0 %all_to_all.24 = f32[16,32,128]{2,1,0:T(8,128)S(1)} all-to-all(f32[16,32,128]{2,1,0:T(8,128)S(1)} %bitcast.12), channel_id=1, replica_groups={{0,2,64,66,128,130,192,194,256,258,320,322,384,386,448,450},{4,6,68,70,..., dimensions={0} | all-to-all | bytes 524288 | tf_op jit(solution)/shard_map/all_to_all | solution.py:337
  119.8 0.7 shard_map.40
  (2 shorter events, 0.0 us)
Async XLA Ops:
  48.4 20.4 %collective-permute-start = (f32[768,128]{1,0:T(8,128)S(1)}, f32[768,128]{1,0:T(8,128)S(1)}, u32[]{:S(2)}, u32[]{:S(2)}) collective-permute-start(f32[768,128]{1,0:T(8,128)S(1)} %bitcast.16), channel_id=1, source_target_pairs={{2,4},{4,2},{6,8},{8,6},{10,12},{12,10},{14,16},{16,14},{18,20},{2... | collective-permute-start | bytes 1179656 | tf_op jit(solution)/shard_map/ppermute | solution.py:353
  50.3 18.5 %collective-permute-start.2 = (f32[256,128]{1,0:T(8,128)S(1)}, f32[256,128]{1,0:T(8,128)S(1)}, u32[]{:S(2)}, u32[]{:S(2)}) collective-permute-start(f32[256,128]{1,0:T(8,128)S(1)} %bitcast.18), channel_id=1, source_target_pairs={{2,5},{3,4},{4,3},{5,2},{6,9},{7,8},{8,7},{9,6},{10,13},{11,12},{1... | collective-permute-start | bytes 393224 | tf_op jit(solution)/shard_map/ppermute | solution.py:354
  57.1 8.4 %collective-permute-start.1 = (f32[256,128]{1,0:T(8,128)S(1)}, f32[256,128]{1,0:T(8,128)S(1)}, u32[]{:S(2)}, u32[]{:S(2)}) collective-permute-start(f32[256,128]{1,0:T(8,128)S(1)} %bitcast.19), channel_id=1, source_target_pairs={{0,1},{1,0},{2,3},{3,2},{4,5},{5,4},{6,7},{7,6},{8,9},{9,8},{10,11... | collective-permute-start | bytes 393224 | tf_op jit(solution)/shard_map/ppermute | solution.py:352
  72.8 7.4 %collective-permute-start.5 = (f32[4,8,8,128]{3,2,1,0:T(8,128)S(1)}, f32[4,8,8,128]{3,2,1,0:T(8,128)S(1)}, u32[]{:S(2)}, u32[]{:S(2)}) collective-permute-start(f32[4,8,8,128]{3,2,1,0:T(8,128)S(1)} %all_gather.25.block), channel_id=1, source_target_pairs={{0,12},{4,16},{8,20},{12,24},{14,2},{16,28},{18,6},{20,32},{22,10}... | collective-permute-start | bytes 393224 | tf_op jit(solution)/shard_map/ppermute | solution.py:360
  74.1 8.3 %collective-permute-start.4 = (f32[4,8,8,128]{3,2,1,0:T(8,128)S(1)}, f32[4,8,8,128]{3,2,1,0:T(8,128)S(1)}, u32[]{:S(2)}, u32[]{:S(2)}) collective-permute-start(f32[4,8,8,128]{3,2,1,0:T(8,128)S(1)} %all_gather.25.block), channel_id=1, source_target_pairs={{0,8},{4,12},{8,16},{10,2},{12,20},{14,6},{16,24},{18,10},{20,28},... | collective-permute-start | bytes 393224 | tf_op jit(solution)/shard_map/ppermute | solution.py:360
  77.5 9.3 %collective-permute-start.3 = (f32[4,8,8,128]{3,2,1,0:T(8,128)S(1)}, f32[4,8,8,128]{3,2,1,0:T(8,128)S(1)}, u32[]{:S(2)}, u32[]{:S(2)}) collective-permute-start(f32[4,8,8,128]{3,2,1,0:T(8,128)S(1)} %all_gather.25.block), channel_id=1, source_target_pairs={{0,4},{4,8},{6,2},{8,12},{10,6},{12,16},{14,10},{16,20},{18,14},{2... | collective-permute-start | bytes 393224 | tf_op jit(solution)/shard_map/ppermute | solution.py:360

commit v7 on v6

--- a/solution.py
+++ b/solution.py
@@ -132,6 +132,17 @@
             base = (orbital * PZ + c) * 48
             for i in range(8):
                 out[base + 4 * i : base + 4 * i + 4] = held[orbital, i, 4 * c : 4 * c + 4]
+
+
+def cut_out(slab, out):
+    for piece in range(16):
+        out[16 * piece : 16 * piece + 16] = slab[48 * piece + 32 : 48 * piece + 48]
+
+
+def cut_own(slabs, out):
+    _, _, c = place()
+    for piece in range(16):
+        out[16 * piece : 16 * piece + 16] = slabs[c, 48 * piece + 32 : 48 * piece + 48]
 
 
 def down(shifts, cores, beside, cores_half, beside_half, fine_out, source, inverse, cut, field, potential, start):
@@ -351,6 +362,7 @@
     both = ("dom", "band")
     own_half = lax.ppermute(half, "band", [(0, 1), (1, 0)])
     beside = lax.ppermute(own, "dom", pairs(to_beside))
+    (half,) = call(cut_out, [(256, 128)])(own)
     beside_half = lax.ppermute(half, both, pairs(to_beside, True))
     of_cores = lax.all_gather(own, "dom", axis_index_groups=cores, axis=0)
     of_cores_half = lax.all_gather(own_half, "dom", axis_index_groups=cores, axis=0)

time: 121 us -> 120 us (level)
  waiting for transfers between devices: 10.6 us -> 6.89 us
  blocking collectives: 85.4 us -> 87.1 us
    ppermute x1, waiting for transfers between devices: 4.09 us -> 1.19 us  [body(): own_half = lax.ppermute(half, 'band', [(0, 1), (1, 0)])]
    all_gather x1, blocking collectives: 3.34 us -> 5.23 us  [body(): lax.all_gather(own_half, 'dom', axis_index_groups=cores, axis=0)]
    ppermute x1, starting transfers between devices: 6.76 us -> 5.2 us  [body(): beside_half = lax.ppermute(half, both, pairs(to_beside, True))]
    ppermute x1, starting transfers between devices: 1.92 us -> 3.48 us  [body(): own_half = lax.ppermute(half, 'band', [(0, 1), (1, 0)])]
    pallas_call x4 -> x5, Pallas kernels: 6.51 us -> 6.52 us  [run(): pl.pallas_call(kernel, out_shape=[(pltpu.VMEM if anywhere else jax.ShapeD...]
where the time goes in v7:
time: 120 us; the launch traced here: 119 us
  blocking collectives  87.1 us (73%)
  starting transfers between devices  18.5 us (15%)
  waiting for transfers between devices  6.89 us (6%)
  Pallas kernels  6.52 us (5%)
    all_to_all x2, blocking collectives, swap_lines(): lax.all_to_all(value, 'dom', 0, 0, axis_index_groups=lines, tiled=True)  75.2 us
    ppermute x3, starting transfers between devices, body(): lax.ppermute(block, 'dom', pairs(lambda px, py, c, k=k: (px, py + k, 0) i...  7.92 us
    pallas_call x5, Pallas kernels, run(): pl.pallas_call(kernel, out_shape=[(pltpu.VMEM if anywhere else jax.ShapeD...  6.52 us
    ppermute x3, waiting for transfers between devices, body(): lax.ppermute(block, 'dom', pairs(lambda px, py, c, k=k: (px, py + k, 0) i...  5.7 us
    all_gather x1, blocking collectives, body(): lax.all_gather(own_half, 'dom', axis_index_groups=cores, axis=0)  5.23 us
    ppermute x1, starting transfers between devices, body(): beside_half = lax.ppermute(half, both, pairs(to_beside, True))  5.2 us
    ppermute x1, starting transfers between devices, body(): own_half = lax.ppermute(half, 'band', [(0, 1), (1, 0)])  3.48 us
  transfers between devices with their start and end apart: 6, of which 3 were waited for; matrix products, arithmetic and copies ran while one was open for 0% of the time, Pallas kernels for 0%

profile of v7, /device:TPU:32, one launch (start us, length us, event | category | flops | bytes accessed | tf_op | source)
XLA Modules:
  0.0 119.2 jit_solution(4118440472934254465)
XLA Ops:
  0.0 1.0 shard_map.37
  1.0 47.4 %all_to_all.22 = f32[16,48,128]{2,1,0:T(8,128)S(1)} all-to-all(f32[16,48,128]{2,1,0:T(8,128)S(1)} %bitcast.18), channel_id=1, replica_groups={{0,2,64,66,128,130,192,194,256,258,320,322,384,386,448,450},{4,6,68,70,..., dimensions={0} | all-to-all | bytes 786432 | tf_op jit(solution)/shard_map/all_to_all | solution.py:348
  48.4 1.9 %collective-permute-start = (f32[768,128]{1,0:T(8,128)S(1)}, f32[768,128]{1,0:T(8,128)S(1)}, u32[]{:S(2)}, u32[]{:S(2)}) collective-permute-start(f32[768,128]{1,0:T(8,128)S(1)} %bitcast.11), channel_id=1, source_target_pairs={{2,4},{4,2},{6,8},{8,6},{10,12},{12,10},{14,16},{16,14},{18,20},{2... | collective-permute-start | bytes 1179656 | tf_op jit(solution)/shard_map/ppermute | solution.py:364
  50.3 3.5 %collective-permute-start.1 = (f32[256,128]{1,0:T(8,128)S(1)}, f32[256,128]{1,0:T(8,128)S(1)}, u32[]{:S(2)}, u32[]{:S(2)}) collective-permute-start(f32[256,128]{1,0:T(8,128)S(1)} %bitcast.19), channel_id=1, source_target_pairs={{0,1},{1,0},{2,3},{3,2},{4,5},{5,4},{6,7},{7,6},{8,9},{9,8},{10,11... | collective-permute-start | bytes 393224 | tf_op jit(solution)/shard_map/ppermute | solution.py:363
  53.8 5.2 %collective-permute-start.2 = (f32[256,128]{1,0:T(8,128)S(1)}, f32[256,128]{1,0:T(8,128)S(1)}, u32[]{:S(2)}, u32[]{:S(2)}) collective-permute-start(f32[256,128]{1,0:T(8,128)S(1)} %shard_map.38), channel_id=1, source_target_pairs={{2,5},{3,4},{4,3},{5,2},{6,9},{7,8},{8,7},{9,6},{10,13},{11,12},{1... | collective-permute-start | bytes 393224 | tf_op jit(solution)/shard_map/ppermute | solution.py:366
  59.0 2.4 %all_gather.22.cores = f32[2,768,128]{2,1,0:T(8,128)S(1)} all-gather(f32[1,768,128]{2,1,0:T(8,128)S(1)} %bitcast.13), channel_id=1, replica_groups={{0,2},{4,6},{8,10},{12,14},{16,18},{20,22},{24,26},{28,30},{32,34},{36,..., dimensions={0}, use_global_device_ids=true | all-gather | bytes 1179648 | tf_op jit(solution)/shard_map/all_gather | solution.py:367
  61.4 1.2 collective-permute-done.1
  62.6 5.2 %all-gather = f32[512,128]{1,0:T(8,128)S(1)} all-gather(f32[256,128]{1,0:T(8,128)S(1)} %collective-permute-done.1), channel_id=2, replica_groups={{0,2},{4,6},{8,10},{12,14},{16,18},{20,22},{24,26},{28,30},{32,34},{36,..., dimensions={0}, use_global_device_ids=true | all-gather | bytes 393216 | tf_op jit(solution)/shard_map/all_gather | solution.py:368
  67.8 0.0 collective-permute-done.2.beside_half
  67.8 0.0 collective-permute-done.beside
  67.8 2.1 %shard_map.39 = (f32[8,8,8,256]{3,2,1,0:T(8,128)S(1)}, f32[10,8,8,256]{3,2,1,0:T(8,128)S(1)}, f32[10,8,8,256]{3,2,1,0:T(8,128)S(1)}, f32[2,8,8,128]{3,2,1,0:T(8,128)S(1)}) custom-call(f32[8,128]{1,0:T(8,128)S(1)} %get-tuple-element.11.shifts, f32[2,768,128]{2,1,0:T(8,128)S(1)} %all_gather.22.cores, f32[768,128]{1,0:T(8,128)S(1)} %collective-permute-done.beside, ...), custom_call_target="tpu_custom_call" | custom-call | tf_op jit(solution)/shard_map/pallas_call | solution.py:304
  69.9 1.9 %all_gather.25.block = f32[4,8,8,128]{3,2,1,0:T(8,128)S(1)} all-gather(f32[2,8,8,128]{3,2,1,0:T(8,128)S(1)} %get-tuple-element.16), channel_id=1, replica_groups={{0,2},{4,6},{8,10},{12,14},{16,18},{20,22},{24,26},{28,30},{32,34},{36,..., dimensions={0}, use_global_device_ids=true | all-gather | bytes 196608 | tf_op jit(solution)/shard_map/all_gather | solution.py:370
  71.8 1.3 %collective-permute-start.5 = (f32[4,8,8,128]{3,2,1,0:T(8,128)S(1)}, f32[4,8,8,128]{3,2,1,0:T(8,128)S(1)}, u32[]{:S(2)}, u32[]{:S(2)}) collective-permute-start(f32[4,8,8,128]{3,2,1,0:T(8,128)S(1)} %all_gather.25.block), channel_id=1, source_target_pairs={{0,12},{4,16},{8,20},{12,24},{14,2},{16,28},{18,6},{20,32},{22,10}... | collective-permute-start | bytes 393224 | tf_op jit(solution)/shard_map/ppermute | solution.py:372
  73.1 3.1 %collective-permute-start.4 = (f32[4,8,8,128]{3,2,1,0:T(8,128)S(1)}, f32[4,8,8,128]{3,2,1,0:T(8,128)S(1)}, u32[]{:S(2)}, u32[]{:S(2)}) collective-permute-start(f32[4,8,8,128]{3,2,1,0:T(8,128)S(1)} %all_gather.25.block), channel_id=1, source_target_pairs={{0,8},{4,12},{8,16},{10,2},{12,20},{14,6},{16,24},{18,10},{20,28},... | collective-permute-start | bytes 393224 | tf_op jit(solution)/shard_map/ppermute | solution.py:372
  76.2 3.6 %collective-permute-start.3 = (f32[4,8,8,128]{3,2,1,0:T(8,128)S(1)}, f32[4,8,8,128]{3,2,1,0:T(8,128)S(1)}, u32[]{:S(2)}, u32[]{:S(2)}) collective-permute-start(f32[4,8,8,128]{3,2,1,0:T(8,128)S(1)} %all_gather.25.block), channel_id=1, source_target_pairs={{0,4},{4,8},{6,2},{8,12},{10,6},{12,16},{14,10},{16,20},{18,14},{2... | collective-permute-start | bytes 393224 | tf_op jit(solution)/shard_map/ppermute | solution.py:372
  79.8 0.0 collective-permute-done.5
  79.8 2.2 %collective-permute-done.4 = f32[4,8,8,128]{3,2,1,0:T(8,128)S(1)} collective-permute-done((f32[4,8,8,128]{3,2,1,0:T(8,128)S(1)}, f32[4,8,8,128]{3,2,1,0:T(8,128)S(1)}, u32[]{:S(2)}, u32[]{:S(2)}) %collective-permute-start.4) | collective-permute-done | bytes 131104 | tf_op jit(solution)/shard_map/ppermute | solution.py:372
  82.0 3.5 %collective-permute-done.3 = f32[4,8,8,128]{3,2,1,0:T(8,128)S(1)} collective-permute-done((f32[4,8,8,128]{3,2,1,0:T(8,128)S(1)}, f32[4,8,8,128]{3,2,1,0:T(8,128)S(1)}, u32[]{:S(2)}, u32[]{:S(2)}) %collective-permute-start.3) | collective-permute-done | bytes 131104 | tf_op jit(solution)/shard_map/ppermute | solution.py:372
  85.5 2.4 %all-gather.1 = f32[6,4,8,8,128]{4,3,2,1,0:T(8,128)S(1)} all-gather(f32[3,4,8,8,128]{4,3,2,1,0:T(8,128)S(1)} %pad_maximum_fusion), channel_id=3, replica_groups={{0,2},{4,6},{8,10},{12,14},{16,18},{20,22},{24,26},{28,30},{32,34},{36,..., dimensions={0}, use_global_device_ids=true | all-gather | bytes 1179648 | tf_op jit(solution)/shard_map/all_gather | solution.py:379
  87.9 2.7 %shard_map.40 = f32[512,128]{1,0:T(8,128)S(1)} custom-call(f32[8,128]{1,0:T(8,128)S(1)} %get-tuple-element.11.shifts, f32[8,8,8,256]{3,2,1,0:T(8,128)S(1)} %get-tuple-element.13.fine, f32[10,8,8,256]{3,2,1,0:T(8,128)S(1)} %get-tuple-element.14.source, f32[10,8,8,256]{3,2,1,0:T(8,128)S(1)} %get-tuple-element.15.inverse, ...), custom_call_target="tpu_custom_call" | custom-call | tf_op jit(solution)/shard_map/pallas_call | solution.py:304
  90.6 27.9 %all_to_all.23 = f32[16,32,128]{2,1,0:T(8,128)S(1)} all-to-all(f32[16,32,128]{2,1,0:T(8,128)S(1)} %bitcast.15), channel_id=1, replica_groups={{0,2,64,66,128,130,192,194,256,258,320,322,384,386,448,450},{4,6,68,70,..., dimensions={0} | all-to-all | bytes 524288 | tf_op jit(solution)/shard_map/all_to_all | solution.py:348
  118.4 0.7 shard_map.41
  (3 shorter events, 0.0 us)
Async XLA Ops:
  48.4 19.4 %collective-permute-start = (f32[768,128]{1,0:T(8,128)S(1)}, f32[768,128]{1,0:T(8,128)S(1)}, u32[]{:S(2)}, u32[]{:S(2)}) collective-permute-start(f32[768,128]{1,0:T(8,128)S(1)} %bitcast.11), channel_id=1, source_target_pairs={{2,4},{4,2},{6,8},{8,6},{10,12},{12,10},{14,16},{16,14},{18,20},{2... | collective-permute-start | bytes 1179656 | tf_op jit(solution)/shard_map/ppermute | solution.py:364
  50.3 12.3 %collective-permute-start.1 = (f32[256,128]{1,0:T(8,128)S(1)}, f32[256,128]{1,0:T(8,128)S(1)}, u32[]{:S(2)}, u32[]{:S(2)}) collective-permute-start(f32[256,128]{1,0:T(8,128)S(1)} %bitcast.19), channel_id=1, source_target_pairs={{0,1},{1,0},{2,3},{3,2},{4,5},{5,4},{6,7},{7,6},{8,9},{9,8},{10,11... | collective-permute-start | bytes 393224 | tf_op jit(solution)/shard_map/ppermute | solution.py:363
  53.8 14.0 %collective-permute-start.2 = (f32[256,128]{1,0:T(8,128)S(1)}, f32[256,128]{1,0:T(8,128)S(1)}, u32[]{:S(2)}, u32[]{:S(2)}) collective-permute-start(f32[256,128]{1,0:T(8,128)S(1)} %shard_map.38), channel_id=1, source_target_pairs={{2,5},{3,4},{4,3},{5,2},{6,9},{7,8},{8,7},{9,6},{10,13},{11,12},{1... | collective-permute-start | bytes 393224 | tf_op jit(solution)/shard_map/ppermute | solution.py:366
  71.8 8.0 %collective-permute-start.5 = (f32[4,8,8,128]{3,2,1,0:T(8,128)S(1)}, f32[4,8,8,128]{3,2,1,0:T(8,128)S(1)}, u32[]{:S(2)}, u32[]{:S(2)}) collective-permute-start(f32[4,8,8,128]{3,2,1,0:T(8,128)S(1)} %all_gather.25.block), channel_id=1, source_target_pairs={{0,12},{4,16},{8,20},{12,24},{14,2},{16,28},{18,6},{20,32},{22,10}... | collective-permute-start | bytes 393224 | tf_op jit(solution)/shard_map/ppermute | solution.py:372
  73.1 8.8 %collective-permute-start.4 = (f32[4,8,8,128]{3,2,1,0:T(8,128)S(1)}, f32[4,8,8,128]{3,2,1,0:T(8,128)S(1)}, u32[]{:S(2)}, u32[]{:S(2)}) collective-permute-start(f32[4,8,8,128]{3,2,1,0:T(8,128)S(1)} %all_gather.25.block), channel_id=1, source_target_pairs={{0,8},{4,12},{8,16},{10,2},{12,20},{14,6},{16,24},{18,10},{20,28},... | collective-permute-start | bytes 393224 | tf_op jit(solution)/shard_map/ppermute | solution.py:372
  76.2 9.3 %collective-permute-start.3 = (f32[4,8,8,128]{3,2,1,0:T(8,128)S(1)}, f32[4,8,8,128]{3,2,1,0:T(8,128)S(1)}, u32[]{:S(2)}, u32[]{:S(2)}) collective-permute-start(f32[4,8,8,128]{3,2,1,0:T(8,128)S(1)} %all_gather.25.block), channel_id=1, source_target_pairs={{0,4},{4,8},{6,2},{8,12},{10,6},{12,16},{14,10},{16,20},{18,14},{2... | collective-permute-start | bytes 393224 | tf_op jit(solution)/shard_map/ppermute | solution.py:372

commit v8 on v7

--- a/solution.py
+++ b/solution.py
@@ -12,7 +12,7 @@
 PX, PZ = 8, 2
 REACH = 3
 F32 = jnp.float32
-HIGHEST = lax.Precision.HIGHEST
+BF16 = jnp.bfloat16
 
 
 def place():
@@ -97,7 +97,13 @@
 
 
 def times(value, matrix):
-    return jnp.dot(value, matrix, precision=HIGHEST, preferred_element_type=F32)
+    high = value.astype(BF16)
+    rest = value - high.astype(F32)
+    middle = rest.astype(BF16)
+    low = (rest - middle.astype(F32)).astype(BF16)
+    matrix = matrix.astype(BF16)
+    parts = [jnp.dot(part, matrix, preferred_element_type=F32) for part in (high, middle, low)]
+    return parts[0] + (parts[1] + parts[2])
 
 
 def cubes(low, high):
@@ -137,12 +143,6 @@
 def cut_out(slab, out):
     for piece in range(16):
         out[16 * piece : 16 * piece + 16] = slab[48 * piece + 32 : 48 * piece + 48]
-
-
-def cut_own(slabs, out):
-    _, _, c = place()
-    for piece in range(16):
-        out[16 * piece : 16 * piece + 16] = slabs[c, 48 * piece + 32 : 48 * piece + 48]
 
 
 def down(shifts, cores, beside, cores_half, beside_half, fine_out, source, inverse, cut, field, potential, start):
@@ -374,9 +374,9 @@
             "dom",
             pairs(lambda px, py, c, k=k: (px, py + k, 0) if c == 0 else (px, py - k, 1)),
         )
-        for k in range(1, REACH + 1)
-    ]
-    around = lax.all_gather(jnp.stack(sent), "dom", axis_index_groups=cores, axis=0)
+        for k in range(REACH, 0, -1)
+    ]
+    around = lax.all_gather(jnp.stack(sent[::-1]), "dom", axis_index_groups=cores, axis=0)
     final = run_up(shift, fine, source, inverse, block, around)
     (correction,) = call(unpack, [(8, 8, 8, 128)])(swap_lines(final))
     return correction

time: 120 us -> 119 us (level)
  no operation moved by 1% of the time
where the time goes in v8:
time: 119 us
  blocking collectives  87.1 us (73%)
  starting transfers between devices  18.5 us (16%)
  waiting for transfers between devices  6.89 us (6%)
  Pallas kernels  6.18 us (5%)
    all_to_all x2, blocking collectives, swap_lines(): lax.all_to_all(value, 'dom', 0, 0, axis_index_groups=lines, tiled=True)  75.2 us
    ppermute x3, starting transfers between devices, body(): lax.ppermute(block, 'dom', pairs(lambda px, py, c, k=k: (px, py + k, 0) i...  7.92 us
    pallas_call x5, Pallas kernels, run(): pl.pallas_call(kernel, out_shape=[(pltpu.VMEM if anywhere else jax.ShapeD...  6.18 us
    ppermute x3, waiting for transfers between devices, body(): lax.ppermute(block, 'dom', pairs(lambda px, py, c, k=k: (px, py + k, 0) i...  5.7 us
    all_gather x1, blocking collectives, body(): lax.all_gather(own_half, 'dom', axis_index_groups=cores, axis=0)  5.23 us
    ppermute x1, starting transfers between devices, body(): beside_half = lax.ppermute(half, both, pairs(to_beside, True))  5.2 us
    ppermute x1, starting transfers between devices, body(): own_half = lax.ppermute(half, 'band', [(0, 1), (1, 0)])  3.48 us
  transfers between devices with their start and end apart: 6, of which 3 were waited for; matrix products, arithmetic and copies ran while one was open for 0% of the time, Pallas kernels for 0%

profile of v8, /device:TPU:32, one launch (start us, length us, event | category | flops | bytes accessed | tf_op | source)
XLA Modules:
  0.0 118.8 jit_solution(5226296666649696796)
XLA Ops:
  0.0 1.0 shard_map.37
  1.0 47.4 %all_to_all.22 = f32[16,48,128]{2,1,0:T(8,128)S(1)} all-to-all(f32[16,48,128]{2,1,0:T(8,128)S(1)} %bitcast.18), channel_id=1, replica_groups={{0,2,64,66,128,130,192,194,256,258,320,322,384,386,448,450},{4,6,68,70,..., dimensions={0} | all-to-all | bytes 786432 | tf_op jit(solution)/shard_map/all_to_all | solution.py:348
  48.4 1.9 %collective-permute-start = (f32[768,128]{1,0:T(8,128)S(1)}, f32[768,128]{1,0:T(8,128)S(1)}, u32[]{:S(2)}, u32[]{:S(2)}) collective-permute-start(f32[768,128]{1,0:T(8,128)S(1)} %bitcast.11), channel_id=1, source_target_pairs={{2,4},{4,2},{6,8},{8,6},{10,12},{12,10},{14,16},{16,14},{18,20},{2... | collective-permute-start | bytes 1179656 | tf_op jit(solution)/shard_map/ppermute | solution.py:364
  50.3 3.5 %collective-permute-start.1 = (f32[256,128]{1,0:T(8,128)S(1)}, f32[256,128]{1,0:T(8,128)S(1)}, u32[]{:S(2)}, u32[]{:S(2)}) collective-permute-start(f32[256,128]{1,0:T(8,128)S(1)} %bitcast.19), channel_id=1, source_target_pairs={{0,1},{1,0},{2,3},{3,2},{4,5},{5,4},{6,7},{7,6},{8,9},{9,8},{10,11... | collective-permute-start | bytes 393224 | tf_op jit(solution)/shard_map/ppermute | solution.py:363
  53.8 5.2 %collective-permute-start.2 = (f32[256,128]{1,0:T(8,128)S(1)}, f32[256,128]{1,0:T(8,128)S(1)}, u32[]{:S(2)}, u32[]{:S(2)}) collective-permute-start(f32[256,128]{1,0:T(8,128)S(1)} %shard_map.38), channel_id=1, source_target_pairs={{2,5},{3,4},{4,3},{5,2},{6,9},{7,8},{8,7},{9,6},{10,13},{11,12},{1... | collective-permute-start | bytes 393224 | tf_op jit(solution)/shard_map/ppermute | solution.py:366
  59.0 2.4 %all_gather.22.cores = f32[2,768,128]{2,1,0:T(8,128)S(1)} all-gather(f32[1,768,128]{2,1,0:T(8,128)S(1)} %bitcast.13), channel_id=1, replica_groups={{0,2},{4,6},{8,10},{12,14},{16,18},{20,22},{24,26},{28,30},{32,34},{36,..., dimensions={0}, use_global_device_ids=true | all-gather | bytes 1179648 | tf_op jit(solution)/shard_map/all_gather | solution.py:367
  61.4 1.2 collective-permute-done.1
  62.6 5.2 %all-gather = f32[512,128]{1,0:T(8,128)S(1)} all-gather(f32[256,128]{1,0:T(8,128)S(1)} %collective-permute-done.1), channel_id=2, replica_groups={{0,2},{4,6},{8,10},{12,14},{16,18},{20,22},{24,26},{28,30},{32,34},{36,..., dimensions={0}, use_global_device_ids=true | all-gather | bytes 393216 | tf_op jit(solution)/shard_map/all_gather | solution.py:368
  67.8 0.0 collective-permute-done.2.beside_half
  67.8 0.0 collective-permute-done.beside
  67.8 2.1 %shard_map.39 = (f32[8,8,8,256]{3,2,1,0:T(8,128)S(1)}, f32[10,8,8,256]{3,2,1,0:T(8,128)S(1)}, f32[10,8,8,256]{3,2,1,0:T(8,128)S(1)}, f32[2,8,8,128]{3,2,1,0:T(8,128)S(1)}) custom-call(f32[8,128]{1,0:T(8,128)S(1)} %get-tuple-element.11.shifts, f32[2,768,128]{2,1,0:T(8,128)S(1)} %all_gather.22.cores, f32[768,128]{1,0:T(8,128)S(1)} %collective-permute-done.beside, ...), custom_call_target="tpu_custom_call" | custom-call | tf_op jit(solution)/shard_map/pallas_call | solution.py:304
  69.9 1.9 %all_gather.25.block = f32[4,8,8,128]{3,2,1,0:T(8,128)S(1)} all-gather(f32[2,8,8,128]{3,2,1,0:T(8,128)S(1)} %get-tuple-element.16), channel_id=1, replica_groups={{0,2},{4,6},{8,10},{12,14},{16,18},{20,22},{24,26},{28,30},{32,34},{36,..., dimensions={0}, use_global_device_ids=true | all-gather | bytes 196608 | tf_op jit(solution)/shard_map/all_gather | solution.py:370
  71.8 1.3 %collective-permute-start.5 = (f32[4,8,8,128]{3,2,1,0:T(8,128)S(1)}, f32[4,8,8,128]{3,2,1,0:T(8,128)S(1)}, u32[]{:S(2)}, u32[]{:S(2)}) collective-permute-start(f32[4,8,8,128]{3,2,1,0:T(8,128)S(1)} %all_gather.25.block), channel_id=1, source_target_pairs={{0,12},{4,16},{8,20},{12,24},{14,2},{16,28},{18,6},{20,32},{22,10}... | collective-permute-start | bytes 393224 | tf_op jit(solution)/shard_map/ppermute | solution.py:372
  73.1 3.1 %collective-permute-start.4 = (f32[4,8,8,128]{3,2,1,0:T(8,128)S(1)}, f32[4,8,8,128]{3,2,1,0:T(8,128)S(1)}, u32[]{:S(2)}, u32[]{:S(2)}) collective-permute-start(f32[4,8,8,128]{3,2,1,0:T(8,128)S(1)} %all_gather.25.block), channel_id=1, source_target_pairs={{0,8},{4,12},{8,16},{10,2},{12,20},{14,6},{16,24},{18,10},{20,28},... | collective-permute-start | bytes 393224 | tf_op jit(solution)/shard_map/ppermute | solution.py:372
  76.2 3.6 %collective-permute-start.3 = (f32[4,8,8,128]{3,2,1,0:T(8,128)S(1)}, f32[4,8,8,128]{3,2,1,0:T(8,128)S(1)}, u32[]{:S(2)}, u32[]{:S(2)}) collective-permute-start(f32[4,8,8,128]{3,2,1,0:T(8,128)S(1)} %all_gather.25.block), channel_id=1, source_target_pairs={{0,4},{4,8},{6,2},{8,12},{10,6},{12,16},{14,10},{16,20},{18,14},{2... | collective-permute-start | bytes 393224 | tf_op jit(solution)/shard_map/ppermute | solution.py:372
  79.7 0.0 collective-permute-done.5
  79.7 2.2 %collective-permute-done.4 = f32[4,8,8,128]{3,2,1,0:T(8,128)S(1)} collective-permute-done((f32[4,8,8,128]{3,2,1,0:T(8,128)S(1)}, f32[4,8,8,128]{3,2,1,0:T(8,128)S(1)}, u32[]{:S(2)}, u32[]{:S(2)}) %collective-permute-start.4) | collective-permute-done | bytes 131104 | tf_op jit(solution)/shard_map/ppermute | solution.py:372
  81.9 3.5 %collective-permute-done.3 = f32[4,8,8,128]{3,2,1,0:T(8,128)S(1)} collective-permute-done((f32[4,8,8,128]{3,2,1,0:T(8,128)S(1)}, f32[4,8,8,128]{3,2,1,0:T(8,128)S(1)}, u32[]{:S(2)}, u32[]{:S(2)}) %collective-permute-start.3) | collective-permute-done | bytes 131104 | tf_op jit(solution)/shard_map/ppermute | solution.py:372
  85.5 2.4 %all-gather.1 = f32[6,4,8,8,128]{4,3,2,1,0:T(8,128)S(1)} all-gather(f32[3,4,8,8,128]{4,3,2,1,0:T(8,128)S(1)} %pad_maximum_fusion), channel_id=3, replica_groups={{0,2},{4,6},{8,10},{12,14},{16,18},{20,22},{24,26},{28,30},{32,34},{36,..., dimensions={0}, use_global_device_ids=true | all-gather | bytes 1179648 | tf_op jit(solution)/shard_map/all_gather | solution.py:379
  87.8 2.4 %shard_map.40 = f32[512,128]{1,0:T(8,128)S(1)} custom-call(f32[8,128]{1,0:T(8,128)S(1)} %get-tuple-element.11.shifts, f32[8,8,8,256]{3,2,1,0:T(8,128)S(1)} %get-tuple-element.13.fine, f32[10,8,8,256]{3,2,1,0:T(8,128)S(1)} %get-tuple-element.14.source, f32[10,8,8,256]{3,2,1,0:T(8,128)S(1)} %get-tuple-element.15.inverse, ...), custom_call_target="tpu_custom_call" | custom-call | tf_op jit(solution)/shard_map/pallas_call | solution.py:304
  90.2 27.9 %all_to_all.23 = f32[16,32,128]{2,1,0:T(8,128)S(1)} all-to-all(f32[16,32,128]{2,1,0:T(8,128)S(1)} %bitcast.15), channel_id=1, replica_groups={{0,2,64,66,128,130,192,194,256,258,320,322,384,386,448,450},{4,6,68,70,..., dimensions={0} | all-to-all | bytes 524288 | tf_op jit(solution)/shard_map/all_to_all | solution.py:348
  118.1 0.7 shard_map.41
  (3 shorter events, 0.0 us)
Async XLA Ops:
  48.4 19.4 %collective-permute-start = (f32[768,128]{1,0:T(8,128)S(1)}, f32[768,128]{1,0:T(8,128)S(1)}, u32[]{:S(2)}, u32[]{:S(2)}) collective-permute-start(f32[768,128]{1,0:T(8,128)S(1)} %bitcast.11), channel_id=1, source_target_pairs={{2,4},{4,2},{6,8},{8,6},{10,12},{12,10},{14,16},{16,14},{18,20},{2... | collective-permute-start | bytes 1179656 | tf_op jit(solution)/shard_map/ppermute | solution.py:364
  50.3 12.3 %collective-permute-start.1 = (f32[256,128]{1,0:T(8,128)S(1)}, f32[256,128]{1,0:T(8,128)S(1)}, u32[]{:S(2)}, u32[]{:S(2)}) collective-permute-start(f32[256,128]{1,0:T(8,128)S(1)} %bitcast.19), channel_id=1, source_target_pairs={{0,1},{1,0},{2,3},{3,2},{4,5},{5,4},{6,7},{7,6},{8,9},{9,8},{10,11... | collective-permute-start | bytes 393224 | tf_op jit(solution)/shard_map/ppermute | solution.py:363
  53.8 14.0 %collective-permute-start.2 = (f32[256,128]{1,0:T(8,128)S(1)}, f32[256,128]{1,0:T(8,128)S(1)}, u32[]{:S(2)}, u32[]{:S(2)}) collective-permute-start(f32[256,128]{1,0:T(8,128)S(1)} %shard_map.38), channel_id=1, source_target_pairs={{2,5},{3,4},{4,3},{5,2},{6,9},{7,8},{8,7},{9,6},{10,13},{11,12},{1... | collective-permute-start | bytes 393224 | tf_op jit(solution)/shard_map/ppermute | solution.py:366
  71.8 7.9 %collective-permute-start.5 = (f32[4,8,8,128]{3,2,1,0:T(8,128)S(1)}, f32[4,8,8,128]{3,2,1,0:T(8,128)S(1)}, u32[]{:S(2)}, u32[]{:S(2)}) collective-permute-start(f32[4,8,8,128]{3,2,1,0:T(8,128)S(1)} %all_gather.25.block), channel_id=1, source_target_pairs={{0,12},{4,16},{8,20},{12,24},{14,2},{16,28},{18,6},{20,32},{22,10}... | collective-permute-start | bytes 393224 | tf_op jit(solution)/shard_map/ppermute | solution.py:372
  73.1 8.8 %collective-permute-start.4 = (f32[4,8,8,128]{3,2,1,0:T(8,128)S(1)}, f32[4,8,8,128]{3,2,1,0:T(8,128)S(1)}, u32[]{:S(2)}, u32[]{:S(2)}) collective-permute-start(f32[4,8,8,128]{3,2,1,0:T(8,128)S(1)} %all_gather.25.block), channel_id=1, source_target_pairs={{0,8},{4,12},{8,16},{10,2},{12,20},{14,6},{16,24},{18,10},{20,28},... | collective-permute-start | bytes 393224 | tf_op jit(solution)/shard_map/ppermute | solution.py:372
  76.2 9.3 %collective-permute-start.3 = (f32[4,8,8,128]{3,2,1,0:T(8,128)S(1)}, f32[4,8,8,128]{3,2,1,0:T(8,128)S(1)}, u32[]{:S(2)}, u32[]{:S(2)}) collective-permute-start(f32[4,8,8,128]{3,2,1,0:T(8,128)S(1)} %all_gather.25.block), channel_id=1, source_target_pairs={{0,4},{4,8},{6,2},{8,12},{10,6},{12,16},{14,10},{16,20},{18,14},{2... | collective-permute-start | bytes 393224 | tf_op jit(solution)/shard_map/ppermute | solution.py:372

commit v9 on v8

--- a/solution.py
+++ b/solution.py
@@ -128,8 +128,8 @@
         for i in range(4):
             both = planes[i, 4 * c : 4 * c + 4]
             for orbital in range(PX):
-                base = (orbital * PZ + c) * 48 + 32 + 4 * i
-                out[base : base + 4] = both
+                base = (orbital * PZ + c) * 48 + 32 + i
+                out[pl.ds(base, 4, stride=4), :] = both
     copies[1].wait()
     shift[...] = jnp.full((8, 128), numbers[place()[0]], F32)
     for orbital in range(PX):
@@ -140,9 +140,18 @@
                 out[base + 4 * i : base + 4 * i + 4] = held[orbital, i, 4 * c : 4 * c + 4]
 
 
-def cut_out(slab, out):
-    for piece in range(16):
-        out[16 * piece : 16 * piece + 16] = slab[48 * piece + 32 : 48 * piece + 48]
+def cut_out(slab, out, weights):
+    _, _, c = place()
+
+    def rows(first):
+        for piece in range(16):
+            out[32 * piece : 32 * piece + 32] = slab[48 * piece : 48 * piece + 32]
+            near = slab[48 * piece + 32 + first : 48 * piece + 44 + first]
+            out[512 + 12 * piece : 524 + 12 * piece] = near
+            weights[12 * piece : 12 * piece + 12] = near
+
+    pl.when(c == 0)(lambda: rows(0))
+    pl.when(c == 1)(lambda: rows(4))
 
 
 def down(shifts, cores, beside, cores_half, beside_half, fine_out, source, inverse, cut, field, potential, start):
@@ -154,17 +163,24 @@
     def unpack(blocks, halves):
         for row in range(12):
             block, other_half = blocks[row // 4], halves[row // 4]
+            apart = block is beside
+            piece, stride = (32, 64) if apart else (48, 96)
+            near = row % 4 - (apart and row < 4)
             for half in range(PZ):
                 lanes = slice(128 * half, 128 * half + 128)
                 for i in range(8):
-                    at = 48 * half + 4 * i + row % 4
-                    field[row, i, :, lanes] = block[pl.ds(at, PX, stride=96), :]
+                    at = piece * half + 4 * i + row % 4
+                    field[row, i, :, lanes] = block[pl.ds(at, PX, stride=stride), :]
                 if 1 <= row <= 10:
                     for i in range(4):
-                        at = 48 * half + 32 + 4 * i + row % 4
-                        potential[row - 1, 4 * band + i, :, lanes] = block[pl.ds(at, PX, stride=96), :]
-                        at = 16 * half + 4 * i + row % 4
-                        potential[row - 1, 4 * (1 - band) + i, :, lanes] = other_half[pl.ds(at, PX, stride=32), :]
+                        if apart:
+                            at, other, steps = 512 + 12 * half + 4 * near + i, 12 * half + 4 * near + i, (24, 24)
+                        else:
+                            at, other, steps = 48 * half + 32 + 4 * near + i, 16 * half + 4 * near + i, (96, 32)
+                        potential[row - 1, 4 * band + i, :, lanes] = block[pl.ds(at, PX, stride=steps[0]), :]
+                        potential[row - 1, 4 * (1 - band) + i, :, lanes] = other_half[
+                            pl.ds(other, PX, stride=steps[1]), :
+                        ]
 
     here = (cores.at[0], cores.at[1])
     here_half = (cores_half.at[0], cores_half.at[1])
@@ -361,8 +377,8 @@
     half = own.reshape(16, 48, 128)[:, 32:].reshape(256, 128)
     both = ("dom", "band")
     own_half = lax.ppermute(half, "band", [(0, 1), (1, 0)])
-    beside = lax.ppermute(own, "dom", pairs(to_beside))
-    (half,) = call(cut_out, [(256, 128)])(own)
+    given, half = call(cut_out, [(704, 128), (192, 128)])(own)
+    beside = lax.ppermute(given, "dom", pairs(to_beside))
     beside_half = lax.ppermute(half, both, pairs(to_beside, True))
     of_cores = lax.all_gather(own, "dom", axis_index_groups=cores, axis=0)
     of_cores_half = lax.all_gather(own_half, "dom", axis_index_groups=cores, axis=0)

time: 119 us -> 119 us (level)
  no operation moved by 1% of the time
where the time goes in v9:
time: 119 us; the launch traced here: 118 us
  blocking collectives  86.8 us (73%)
  starting transfers between devices  18.3 us (15%)
  waiting for transfers between devices  6.68 us (6%)
  Pallas kernels  6.12 us (5%)
    all_to_all x2, blocking collectives, swap_lines(): lax.all_to_all(value, 'dom', 0, 0, axis_index_groups=lines, tiled=True)  75.3 us
    ppermute x3, starting transfers between devices, body(): lax.ppermute(block, 'dom', pairs(lambda px, py, c, k=k: (px, py + k, 0) i...  7.72 us
    pallas_call x5, Pallas kernels, run(): pl.pallas_call(kernel, out_shape=[(pltpu.VMEM if anywhere else jax.ShapeD...  6.12 us
    ppermute x3, waiting for transfers between devices, body(): lax.ppermute(block, 'dom', pairs(lambda px, py, c, k=k: (px, py + k, 0) i...  5.84 us
    ppermute x1, starting transfers between devices, body(): beside_half = lax.ppermute(half, both, pairs(to_beside, True))  5.2 us
    all_gather x1, blocking collectives, body(): lax.all_gather(own_half, 'dom', axis_index_groups=cores, axis=0)  4.84 us
    ppermute x1, starting transfers between devices, body(): own_half = lax.ppermute(half, 'band', [(0, 1), (1, 0)])  3.48 us
  transfers between devices with their start and end apart: 6, of which 3 were waited for; matrix products, arithmetic and copies ran while one was open for 0% of the time, Pallas kernels for 0%

profile of v9, /device:TPU:32, one launch (start us, length us, event | category | flops | bytes accessed | tf_op | source)
XLA Modules:
  0.0 118.1 jit_solution(3527146592055521184)
XLA Ops:
  0.0 1.0 shard_map.37
  1.0 47.4 %all_to_all.22 = f32[16,48,128]{2,1,0:T(8,128)S(1)} all-to-all(f32[16,48,128]{2,1,0:T(8,128)S(1)} %bitcast.17), channel_id=1, replica_groups={{0,2,64,66,128,130,192,194,256,258,320,322,384,386,448,450},{4,6,68,70,..., dimensions={0} | all-to-all | bytes 786432 | tf_op jit(solution)/shard_map/all_to_all | solution.py:364
  48.4 1.9 %collective-permute-start = (f32[704,128]{1,0:T(8,128)S(1)}, f32[704,128]{1,0:T(8,128)S(1)}, u32[]{:S(2)}, u32[]{:S(2)}) collective-permute-start(f32[704,128]{1,0:T(8,128)S(1)} %get-tuple-element.15), channel_id=1, source_target_pairs={{2,4},{4,2},{6,8},{8,6},{10,12},{12,10},{14,16},{16,14},{18,20},{2... | collective-permute-start | bytes 1081352 | tf_op jit(solution)/shard_map/ppermute | solution.py:381
  50.3 3.5 %collective-permute-start.1 = (f32[256,128]{1,0:T(8,128)S(1)}, f32[256,128]{1,0:T(8,128)S(1)}, u32[]{:S(2)}, u32[]{:S(2)}) collective-permute-start(f32[256,128]{1,0:T(8,128)S(1)} %bitcast.18), channel_id=1, source_target_pairs={{0,1},{1,0},{2,3},{3,2},{4,5},{5,4},{6,7},{7,6},{8,9},{9,8},{10,11... | collective-permute-start | bytes 393224 | tf_op jit(solution)/shard_map/ppermute | solution.py:379
  53.8 5.2 %collective-permute-start.2 = (f32[192,128]{1,0:T(8,128)S(1)}, f32[192,128]{1,0:T(8,128)S(1)}, u32[]{:S(2)}, u32[]{:S(2)}) collective-permute-start(f32[192,128]{1,0:T(8,128)S(1)} %get-tuple-element.16), channel_id=1, source_target_pairs={{2,5},{3,4},{4,3},{5,2},{6,9},{7,8},{8,7},{9,6},{10,13},{11,12},{1... | collective-permute-start | bytes 294920 | tf_op jit(solution)/shard_map/ppermute | solution.py:382
  59.0 2.4 %all_gather.22.cores = f32[2,768,128]{2,1,0:T(8,128)S(1)} all-gather(f32[1,768,128]{2,1,0:T(8,128)S(1)} %bitcast.12), channel_id=1, replica_groups={{0,2},{4,6},{8,10},{12,14},{16,18},{20,22},{24,26},{28,30},{32,34},{36,..., dimensions={0}, use_global_device_ids=true | all-gather | bytes 1179648 | tf_op jit(solution)/shard_map/all_gather | solution.py:383
  61.4 0.8 collective-permute-done.1
  62.3 4.8 %all-gather = f32[512,128]{1,0:T(8,128)S(1)} all-gather(f32[256,128]{1,0:T(8,128)S(1)} %collective-permute-done.1), channel_id=2, replica_groups={{0,2},{4,6},{8,10},{12,14},{16,18},{20,22},{24,26},{28,30},{32,34},{36,..., dimensions={0}, use_global_device_ids=true | all-gather | bytes 393216 | tf_op jit(solution)/shard_map/all_gather | solution.py:384
  67.1 0.0 collective-permute-done.2.beside_half
  67.1 0.0 collective-permute-done.beside
  67.1 2.0 %shard_map.39 = (f32[8,8,8,256]{3,2,1,0:T(8,128)S(1)}, f32[10,8,8,256]{3,2,1,0:T(8,128)S(1)}, f32[10,8,8,256]{3,2,1,0:T(8,128)S(1)}, f32[2,8,8,128]{3,2,1,0:T(8,128)S(1)}) custom-call(f32[8,128]{1,0:T(8,128)S(1)} %get-tuple-element.13.shifts, f32[2,768,128]{2,1,0:T(8,128)S(1)} %all_gather.22.cores, f32[704,128]{1,0:T(8,128)S(1)} %collective-permute-done.beside, ...), custom_call_target="tpu_custom_call" | custom-call | tf_op jit(solution)/shard_map/pallas_call | solution.py:320
  69.1 1.9 %all_gather.25.block = f32[4,8,8,128]{3,2,1,0:T(8,128)S(1)} all-gather(f32[2,8,8,128]{3,2,1,0:T(8,128)S(1)} %get-tuple-element.20), channel_id=1, replica_groups={{0,2},{4,6},{8,10},{12,14},{16,18},{20,22},{24,26},{28,30},{32,34},{36,..., dimensions={0}, use_global_device_ids=true | all-gather | bytes 196608 | tf_op jit(solution)/shard_map/all_gather | solution.py:386
  71.0 1.3 %collective-permute-start.5 = (f32[4,8,8,128]{3,2,1,0:T(8,128)S(1)}, f32[4,8,8,128]{3,2,1,0:T(8,128)S(1)}, u32[]{:S(2)}, u32[]{:S(2)}) collective-permute-start(f32[4,8,8,128]{3,2,1,0:T(8,128)S(1)} %all_gather.25.block), channel_id=1, source_target_pairs={{0,12},{4,16},{8,20},{12,24},{14,2},{16,28},{18,6},{20,32},{22,10}... | collective-permute-start | bytes 393224 | tf_op jit(solution)/shard_map/ppermute | solution.py:388
  72.3 3.0 %collective-permute-start.4 = (f32[4,8,8,128]{3,2,1,0:T(8,128)S(1)}, f32[4,8,8,128]{3,2,1,0:T(8,128)S(1)}, u32[]{:S(2)}, u32[]{:S(2)}) collective-permute-start(f32[4,8,8,128]{3,2,1,0:T(8,128)S(1)} %all_gather.25.block), channel_id=1, source_target_pairs={{0,8},{4,12},{8,16},{10,2},{12,20},{14,6},{16,24},{18,10},{20,28},... | collective-permute-start | bytes 393224 | tf_op jit(solution)/shard_map/ppermute | solution.py:388
  75.3 3.4 %collective-permute-start.3 = (f32[4,8,8,128]{3,2,1,0:T(8,128)S(1)}, f32[4,8,8,128]{3,2,1,0:T(8,128)S(1)}, u32[]{:S(2)}, u32[]{:S(2)}) collective-permute-start(f32[4,8,8,128]{3,2,1,0:T(8,128)S(1)} %all_gather.25.block), channel_id=1, source_target_pairs={{0,4},{4,8},{6,2},{8,12},{10,6},{12,16},{14,10},{16,20},{18,14},{2... | collective-permute-start | bytes 393224 | tf_op jit(solution)/shard_map/ppermute | solution.py:388
  78.8 0.0 collective-permute-done.5
  78.8 2.2 %collective-permute-done.4 = f32[4,8,8,128]{3,2,1,0:T(8,128)S(1)} collective-permute-done((f32[4,8,8,128]{3,2,1,0:T(8,128)S(1)}, f32[4,8,8,128]{3,2,1,0:T(8,128)S(1)}, u32[]{:S(2)}, u32[]{:S(2)}) %collective-permute-start.4) | collective-permute-done | bytes 131104 | tf_op jit(solution)/shard_map/ppermute | solution.py:388
  80.9 3.7 %collective-permute-done.3 = f32[4,8,8,128]{3,2,1,0:T(8,128)S(1)} collective-permute-done((f32[4,8,8,128]{3,2,1,0:T(8,128)S(1)}, f32[4,8,8,128]{3,2,1,0:T(8,128)S(1)}, u32[]{:S(2)}, u32[]{:S(2)}) %collective-permute-start.3) | collective-permute-done | bytes 131104 | tf_op jit(solution)/shard_map/ppermute | solution.py:388
  84.6 2.4 %all-gather.1 = f32[6,4,8,8,128]{4,3,2,1,0:T(8,128)S(1)} all-gather(f32[3,4,8,8,128]{4,3,2,1,0:T(8,128)S(1)} %pad_maximum_fusion), channel_id=3, replica_groups={{0,2},{4,6},{8,10},{12,14},{16,18},{20,22},{24,26},{28,30},{32,34},{36,..., dimensions={0}, use_global_device_ids=true | all-gather | bytes 1179648 | tf_op jit(solution)/shard_map/all_gather | solution.py:395
  87.0 2.4 %shard_map.40 = f32[512,128]{1,0:T(8,128)S(1)} custom-call(f32[8,128]{1,0:T(8,128)S(1)} %get-tuple-element.13.shifts, f32[8,8,8,256]{3,2,1,0:T(8,128)S(1)} %get-tuple-element.17.fine, f32[10,8,8,256]{3,2,1,0:T(8,128)S(1)} %get-tuple-element.18.source, f32[10,8,8,256]{3,2,1,0:T(8,128)S(1)} %get-tuple-element.19.inverse, ...), custom_call_target="tpu_custom_call" | custom-call | tf_op jit(solution)/shard_map/pallas_call | solution.py:320
  89.4 27.9 %all_to_all.23 = f32[16,32,128]{2,1,0:T(8,128)S(1)} all-to-all(f32[16,32,128]{2,1,0:T(8,128)S(1)} %bitcast.14), channel_id=1, replica_groups={{0,2,64,66,128,130,192,194,256,258,320,322,384,386,448,450},{4,6,68,70,..., dimensions={0} | all-to-all | bytes 524288 | tf_op jit(solution)/shard_map/all_to_all | solution.py:364
  117.3 0.7 shard_map.41
  (3 shorter events, 0.1 us)
Async XLA Ops:
  48.4 18.7 %collective-permute-start = (f32[704,128]{1,0:T(8,128)S(1)}, f32[704,128]{1,0:T(8,128)S(1)}, u32[]{:S(2)}, u32[]{:S(2)}) collective-permute-start(f32[704,128]{1,0:T(8,128)S(1)} %get-tuple-element.15), channel_id=1, source_target_pairs={{2,4},{4,2},{6,8},{8,6},{10,12},{12,10},{14,16},{16,14},{18,20},{2... | collective-permute-start | bytes 1081352 | tf_op jit(solution)/shard_map/ppermute | solution.py:381
  50.3 11.9 %collective-permute-start.1 = (f32[256,128]{1,0:T(8,128)S(1)}, f32[256,128]{1,0:T(8,128)S(1)}, u32[]{:S(2)}, u32[]{:S(2)}) collective-permute-start(f32[256,128]{1,0:T(8,128)S(1)} %bitcast.18), channel_id=1, source_target_pairs={{0,1},{1,0},{2,3},{3,2},{4,5},{5,4},{6,7},{7,6},{8,9},{9,8},{10,11... | collective-permute-start | bytes 393224 | tf_op jit(solution)/shard_map/ppermute | solution.py:379
  53.8 13.3 %collective-permute-start.2 = (f32[192,128]{1,0:T(8,128)S(1)}, f32[192,128]{1,0:T(8,128)S(1)}, u32[]{:S(2)}, u32[]{:S(2)}) collective-permute-start(f32[192,128]{1,0:T(8,128)S(1)} %get-tuple-element.16), channel_id=1, source_target_pairs={{2,5},{3,4},{4,3},{5,2},{6,9},{7,8},{8,7},{9,6},{10,13},{11,12},{1... | collective-permute-start | bytes 294920 | tf_op jit(solution)/shard_map/ppermute | solution.py:382
  71.0 7.7 %collective-permute-start.5 = (f32[4,8,8,128]{3,2,1,0:T(8,128)S(1)}, f32[4,8,8,128]{3,2,1,0:T(8,128)S(1)}, u32[]{:S(2)}, u32[]{:S(2)}) collective-permute-start(f32[4,8,8,128]{3,2,1,0:T(8,128)S(1)} %all_gather.25.block), channel_id=1, source_target_pairs={{0,12},{4,16},{8,20},{12,24},{14,2},{16,28},{18,6},{20,32},{22,10}... | collective-permute-start | bytes 393224 | tf_op jit(solution)/shard_map/ppermute | solution.py:388
  72.3 8.6 %collective-permute-start.4 = (f32[4,8,8,128]{3,2,1,0:T(8,128)S(1)}, f32[4,8,8,128]{3,2,1,0:T(8,128)S(1)}, u32[]{:S(2)}, u32[]{:S(2)}) collective-permute-start(f32[4,8,8,128]{3,2,1,0:T(8,128)S(1)} %all_gather.25.block), channel_id=1, source_target_pairs={{0,8},{4,12},{8,16},{10,2},{12,20},{14,6},{16,24},{18,10},{20,28},... | collective-permute-start | bytes 393224 | tf_op jit(solution)/shard_map/ppermute | solution.py:388
  75.3 9.3 %collective-permute-start.3 = (f32[4,8,8,128]{3,2,1,0:T(8,128)S(1)}, f32[4,8,8,128]{3,2,1,0:T(8,128)S(1)}, u32[]{:S(2)}, u32[]{:S(2)}) collective-permute-start(f32[4,8,8,128]{3,2,1,0:T(8,128)S(1)} %all_gather.25.block), channel_id=1, source_target_pairs={{0,4},{4,8},{6,2},{8,12},{10,6},{12,16},{14,10},{16,20},{18,14},{2... | collective-permute-start | bytes 393224 | tf_op jit(solution)/shard_map/ppermute | solution.py:388

commit v10 on v9

--- a/solution.py
+++ b/solution.py
@@ -154,15 +154,12 @@
     pl.when(c == 1)(lambda: rows(4))
 
 
-def down(shifts, cores, beside, cores_half, beside_half, fine_out, source, inverse, cut, field, potential, start):
-    px, py, c = place()
-    size_y = lax.axis_size("dom") // (PX * PZ)
-    shift = jnp.concatenate([shifts[...]] * 2, axis=1)
-    band = lax.axis_index("band")
-
-    def unpack(blocks, halves):
+def begin(cores, beside, source, weights, field):
+    _, _, c = place()
+
+    def unpack(*blocks):
         for row in range(12):
-            block, other_half = blocks[row // 4], halves[row // 4]
+            block = blocks[row // 4]
             apart = block is beside
             piece, stride = (32, 64) if apart else (48, 96)
             near = row % 4 - (apart and row < 4)
@@ -173,32 +170,49 @@
                     field[row, i, :, lanes] = block[pl.ds(at, PX, stride=stride), :]
                 if 1 <= row <= 10:
                     for i in range(4):
-                        if apart:
-                            at, other, steps = 512 + 12 * half + 4 * near + i, 12 * half + 4 * near + i, (24, 24)
-                        else:
-                            at, other, steps = 48 * half + 32 + 4 * near + i, 16 * half + 4 * near + i, (96, 32)
-                        potential[row - 1, 4 * band + i, :, lanes] = block[pl.ds(at, PX, stride=steps[0]), :]
-                        potential[row - 1, 4 * (1 - band) + i, :, lanes] = other_half[
-                            pl.ds(other, PX, stride=steps[1]), :
-                        ]
-
-    here = (cores.at[0], cores.at[1])
-    here_half = (cores_half.at[0], cores_half.at[1])
-    pl.when(c == 0)(lambda: unpack((beside, *here), (beside_half, *here_half)))
-    pl.when(c == 1)(lambda: unpack((*here, beside), (*here_half, beside_half)))
+                        at, step = (512 + 12 * half, 24) if apart else (48 * half + 32, 96)
+                        weights[row - 1, i, :, lanes] = block[pl.ds(at + 4 * near + i, PX, stride=step), :]
+
+    pl.when(c == 0)(lambda: unpack(beside, cores.at[0], cores.at[1]))
+    pl.when(c == 1)(lambda: unpack(cores.at[0], cores.at[1], beside))
+    for row in range(10):
+        below, here, above = [take(field, row + d) for d in range(3)]
+        for i, (b, h, a, x) in enumerate(zip(below, here, above, along_x(here))):
+            source[row, i] = 0.5 * h + ((b + a) + (x + along_z(h, False))) * (1.0 / 12.0)
+
+
+def down(shifts, source, weights, cores_half, beside_half, fine_out, inverse, cut, potential, start):
+    px, py, c = place()
+    size_y = lax.axis_size("dom") // (PX * PZ)
+    shift = jnp.concatenate([shifts[...]] * 2, axis=1)
+    band = lax.axis_index("band")
+
+    def unpack(*halves):
+        for row in range(1, 11):
+            other_half = halves[row // 4]
+            apart = other_half is beside_half
+            near = row % 4 - (apart and row < 4)
+            for i in range(4):
+                potential[row - 1, 4 * band + i] = weights[row - 1, i]
+                for half in range(PZ):
+                    lanes = slice(128 * half, 128 * half + 128)
+                    at, step = (12 * half, 24) if apart else (16 * half, 32)
+                    potential[row - 1, 4 * (1 - band) + i, :, lanes] = other_half[
+                        pl.ds(at + 4 * near + i, PX, stride=step), :
+                    ]
+
+    pl.when(c == 0)(lambda: unpack(beside_half, cores_half.at[0], cores_half.at[1]))
+    pl.when(c == 1)(lambda: unpack(cores_half.at[0], cores_half.at[1], beside_half))
 
     def first(base, rows):
         for r in range(rows):
             row = base + r
             y = py * 8 + 4 * c + row - 3
             inside = jnp.where((y >= 0) & (y < 8 * size_y), OMEGA, 0.0).astype(F32)
-            below, here, above = [take(field, row + d) for d in range(3)]
-            for i, (b, h, a, x) in enumerate(zip(below, here, above, along_x(here))):
-                s = 0.5 * h + ((b + a) + (x + along_z(h, False))) * (1.0 / 12.0)
+            for i in range(8):
                 v = inside / (potential[row, i] + (4.0 * FINE + shift))
-                source[row, i] = s
                 inverse[row, i] = v
-                start[row, i] = v * s
+                start[row, i] = v * source[row, i]
 
     each(10, 2, first)
     sweep(start, source, inverse, fine_out, FINE, 8, 2, (0, 1, 1))
@@ -329,11 +343,15 @@
     return run
 
 
+def run_begin(cores, beside):
+    return call(begin, [(10, 8, 8, 256), (10, 4, 8, 256)], [(12, 8, 8, 256)])(cores, beside)
+
+
 def run_down(*args):
     return call(
         down,
-        [(8, 8, 8, 256), (10, 8, 8, 256), (10, 8, 8, 256), (2, 8, 8, 128)],
-        [(12, 8, 8, 256)] + [(10, 8, 8, 256)] * 2,
+        [(8, 8, 8, 256), (10, 8, 8, 256), (2, 8, 8, 128)],
+        [(10, 8, 8, 256)] * 2,
     )(*args)
 
 
@@ -381,8 +399,10 @@
     beside = lax.ppermute(given, "dom", pairs(to_beside))
     beside_half = lax.ppermute(half, both, pairs(to_beside, True))
     of_cores = lax.all_gather(own, "dom", axis_index_groups=cores, axis=0)
+    source, weights = run_begin(of_cores, beside)
+    source, own_half = lax.optimization_barrier((source, own_half))
     of_cores_half = lax.all_gather(own_half, "dom", axis_index_groups=cores, axis=0)
-    fine, source, inverse, cut = run_down(shift, of_cores, beside, of_cores_half, beside_half)
+    fine, inverse, cut = run_down(shift, source, weights, of_cores_half, beside_half)
     block = lax.all_gather(cut, "dom", axis_index_groups=cores, axis=0, tiled=True)
     sent = [
         lax.ppermute(

time: 119 us -> 119 us (level)
    pallas_call x5 -> x6, Pallas kernels: 6.12 us -> 6.18 us  [run(): pl.pallas_call(kernel, out_shape=[(pltpu.VMEM if anywhere else jax.ShapeD...]
  transfers between devices with their start and end apart: 6 -> 6, of which waited for: 3 -> 2; matrix products, arithmetic and copies ran while one was open for 0% -> 0% of each run, Pallas kernels for 0% -> 1%
where the time goes in v10:
time: 119 us; the launch traced here: 118 us
  blocking collectives  86.4 us (73%)
  starting transfers between devices  19.4 us (16%)
  Pallas kernels  6.18 us (5%)
  waiting for transfers between devices  6.14 us (5%)
    all_to_all x2, blocking collectives, swap_lines(): lax.all_to_all(value, 'dom', 0, 0, axis_index_groups=lines, tiled=True)  75.2 us
    ppermute x3, starting transfers between devices, body(): lax.ppermute(block, 'dom', pairs(lambda px, py, c, k=k: (px, py + k, 0) i...  8.83 us
    pallas_call x6, Pallas kernels, run(): pl.pallas_call(kernel, out_shape=[(pltpu.VMEM if anywhere else jax.ShapeD...  6.18 us
    ppermute x3, waiting for transfers between devices, body(): lax.ppermute(block, 'dom', pairs(lambda px, py, c, k=k: (px, py + k, 0) i...  6.13 us
    ppermute x1, starting transfers between devices, body(): beside_half = lax.ppermute(half, both, pairs(to_beside, True))  5.2 us
    all_gather x1, blocking collectives, body(): lax.all_gather(own_half, 'dom', axis_index_groups=cores, axis=0)  4.65 us
    ppermute x1, starting transfers between devices, body(): own_half = lax.ppermute(half, 'band', [(0, 1), (1, 0)])  3.48 us
  transfers between devices with their start and end apart: 6, of which 2 were waited for; matrix products, arithmetic and copies ran while one was open for 0% of the time, Pallas kernels for 1%

profile of v10, /device:TPU:32, one launch (start us, length us, event | category | flops | bytes accessed | tf_op | source)
XLA Modules:
  0.0 118.4 jit_solution(12292887131815042701)
XLA Ops:
  0.0 1.0 shard_map.37
  1.0 47.4 %all_to_all.22 = f32[16,48,128]{2,1,0:T(8,128)S(1)} all-to-all(f32[16,48,128]{2,1,0:T(8,128)S(1)} %bitcast.17), channel_id=1, replica_groups={{0,2,64,66,128,130,192,194,256,258,320,322,384,386,448,450},{4,6,68,70,..., dimensions={0} | all-to-all | bytes 786432 | tf_op jit(solution)/shard_map/all_to_all | solution.py:382
  48.4 1.9 %collective-permute-start = (f32[704,128]{1,0:T(8,128)S(1)}, f32[704,128]{1,0:T(8,128)S(1)}, u32[]{:S(2)}, u32[]{:S(2)}) collective-permute-start(f32[704,128]{1,0:T(8,128)S(1)} %get-tuple-element.18), channel_id=1, source_target_pairs={{2,4},{4,2},{6,8},{8,6},{10,12},{12,10},{14,16},{16,14},{18,20},{2... | collective-permute-start | bytes 1081352 | tf_op jit(solution)/shard_map/ppermute | solution.py:399
  50.3 3.5 %collective-permute-start.1 = (f32[256,128]{1,0:T(8,128)S(1)}, f32[256,128]{1,0:T(8,128)S(1)}, u32[]{:S(2)}, u32[]{:S(2)}) collective-permute-start(f32[256,128]{1,0:T(8,128)S(1)} %bitcast.18), channel_id=1, source_target_pairs={{0,1},{1,0},{2,3},{3,2},{4,5},{5,4},{6,7},{7,6},{8,9},{9,8},{10,11... | collective-permute-start | bytes 393224 | tf_op jit(solution)/shard_map/ppermute | solution.py:397
  53.8 5.2 %collective-permute-start.2 = (f32[192,128]{1,0:T(8,128)S(1)}, f32[192,128]{1,0:T(8,128)S(1)}, u32[]{:S(2)}, u32[]{:S(2)}) collective-permute-start(f32[192,128]{1,0:T(8,128)S(1)} %get-tuple-element.23), channel_id=1, source_target_pairs={{2,5},{3,4},{4,3},{5,2},{6,9},{7,8},{8,7},{9,6},{10,13},{11,12},{1... | collective-permute-start | bytes 294920 | tf_op jit(solution)/shard_map/ppermute | solution.py:400
  59.0 2.4 %all_gather.22.cores = f32[2,768,128]{2,1,0:T(8,128)S(1)} all-gather(f32[1,768,128]{2,1,0:T(8,128)S(1)} %bitcast.12), channel_id=1, replica_groups={{0,2},{4,6},{8,10},{12,14},{16,18},{20,22},{24,26},{28,30},{32,34},{36,..., dimensions={0}, use_global_device_ids=true | all-gather | bytes 1179648 | tf_op jit(solution)/shard_map/all_gather | solution.py:401
  61.4 0.0 collective-permute-done.beside
  61.4 1.0 shard_map.39
  62.4 0.0 collective-permute-done.1
  62.5 4.6 %all-gather = f32[512,128]{1,0:T(8,128)S(1)} all-gather(f32[256,128]{1,0:T(8,128)S(1)} %collective-permute-done.1), channel_id=2, replica_groups={{0,2},{4,6},{8,10},{12,14},{16,18},{20,22},{24,26},{28,30},{32,34},{36,..., dimensions={0}, use_global_device_ids=true | all-gather | bytes 393216 | tf_op jit(solution)/shard_map/all_gather | solution.py:404
  67.1 0.0 collective-permute-done.2.beside_half
  67.1 1.0 shard_map.40
  68.1 1.9 %all_gather.25.block = f32[4,8,8,128]{3,2,1,0:T(8,128)S(1)} all-gather(f32[2,8,8,128]{3,2,1,0:T(8,128)S(1)} %get-tuple-element.26), channel_id=1, replica_groups={{0,2},{4,6},{8,10},{12,14},{16,18},{20,22},{24,26},{28,30},{32,34},{36,..., dimensions={0}, use_global_device_ids=true | all-gather | bytes 196608 | tf_op jit(solution)/shard_map/all_gather | solution.py:406
  70.0 1.3 %collective-permute-start.5 = (f32[4,8,8,128]{3,2,1,0:T(8,128)S(1)}, f32[4,8,8,128]{3,2,1,0:T(8,128)S(1)}, u32[]{:S(2)}, u32[]{:S(2)}) collective-permute-start(f32[4,8,8,128]{3,2,1,0:T(8,128)S(1)} %all_gather.25.block), channel_id=1, source_target_pairs={{0,12},{4,16},{8,20},{12,24},{14,2},{16,28},{18,6},{20,32},{22,10}... | collective-permute-start | bytes 393224 | tf_op jit(solution)/shard_map/ppermute | solution.py:408
  71.3 4.4 %collective-permute-start.4 = (f32[4,8,8,128]{3,2,1,0:T(8,128)S(1)}, f32[4,8,8,128]{3,2,1,0:T(8,128)S(1)}, u32[]{:S(2)}, u32[]{:S(2)}) collective-permute-start(f32[4,8,8,128]{3,2,1,0:T(8,128)S(1)} %all_gather.25.block), channel_id=1, source_target_pairs={{0,8},{4,12},{8,16},{10,2},{12,20},{14,6},{16,24},{18,10},{20,28},... | collective-permute-start | bytes 393224 | tf_op jit(solution)/shard_map/ppermute | solution.py:408
  75.8 3.1 %collective-permute-start.3 = (f32[4,8,8,128]{3,2,1,0:T(8,128)S(1)}, f32[4,8,8,128]{3,2,1,0:T(8,128)S(1)}, u32[]{:S(2)}, u32[]{:S(2)}) collective-permute-start(f32[4,8,8,128]{3,2,1,0:T(8,128)S(1)} %all_gather.25.block), channel_id=1, source_target_pairs={{0,4},{4,8},{6,2},{8,12},{10,6},{12,16},{14,10},{16,20},{18,14},{2... | collective-permute-start | bytes 393224 | tf_op jit(solution)/shard_map/ppermute | solution.py:408
  78.9 0.0 collective-permute-done.5
  78.9 2.2 %collective-permute-done.4 = f32[4,8,8,128]{3,2,1,0:T(8,128)S(1)} collective-permute-done((f32[4,8,8,128]{3,2,1,0:T(8,128)S(1)}, f32[4,8,8,128]{3,2,1,0:T(8,128)S(1)}, u32[]{:S(2)}, u32[]{:S(2)}) %collective-permute-start.4) | collective-permute-done | bytes 131104 | tf_op jit(solution)/shard_map/ppermute | solution.py:408
  81.1 3.9 %collective-permute-done.3 = f32[4,8,8,128]{3,2,1,0:T(8,128)S(1)} collective-permute-done((f32[4,8,8,128]{3,2,1,0:T(8,128)S(1)}, f32[4,8,8,128]{3,2,1,0:T(8,128)S(1)}, u32[]{:S(2)}, u32[]{:S(2)}) %collective-permute-start.3) | collective-permute-done | bytes 131104 | tf_op jit(solution)/shard_map/ppermute | solution.py:408
  85.1 2.4 %all-gather.1 = f32[6,4,8,8,128]{4,3,2,1,0:T(8,128)S(1)} all-gather(f32[3,4,8,8,128]{4,3,2,1,0:T(8,128)S(1)} %pad_maximum_fusion), channel_id=3, replica_groups={{0,2},{4,6},{8,10},{12,14},{16,18},{20,22},{24,26},{28,30},{32,34},{36,..., dimensions={0}, use_global_device_ids=true | all-gather | bytes 1179648 | tf_op jit(solution)/shard_map/all_gather | solution.py:415
  87.4 2.4 %shard_map.41 = f32[512,128]{1,0:T(8,128)S(1)} custom-call(f32[8,128]{1,0:T(8,128)S(1)} %get-tuple-element.16.shifts, f32[8,8,8,256]{3,2,1,0:T(8,128)S(1)} %get-tuple-element.24.fine, f32[10,8,8,256]{3,2,1,0:T(8,128)S(1)} %get-tuple-element.20.source, f32[10,8,8,256]{3,2,1,0:T(8,128)S(1)} %get-tuple-element.25.inverse, ...), custom_call_target="tpu_custom_call" | custom-call | tf_op jit(solution)/shard_map/pallas_call | solution.py:334
  89.8 27.8 %all_to_all.23 = f32[16,32,128]{2,1,0:T(8,128)S(1)} all-to-all(f32[16,32,128]{2,1,0:T(8,128)S(1)} %bitcast.14), channel_id=1, replica_groups={{0,2,64,66,128,130,192,194,256,258,320,322,384,386,448,450},{4,6,68,70,..., dimensions={0} | all-to-all | bytes 524288 | tf_op jit(solution)/shard_map/all_to_all | solution.py:382
  117.6 0.7 shard_map.42
  (3 shorter events, 0.1 us)
Async XLA Ops:
  48.4 13.0 %collective-permute-start = (f32[704,128]{1,0:T(8,128)S(1)}, f32[704,128]{1,0:T(8,128)S(1)}, u32[]{:S(2)}, u32[]{:S(2)}) collective-permute-start(f32[704,128]{1,0:T(8,128)S(1)} %get-tuple-element.18), channel_id=1, source_target_pairs={{2,4},{4,2},{6,8},{8,6},{10,12},{12,10},{14,16},{16,14},{18,20},{2... | collective-permute-start | bytes 1081352 | tf_op jit(solution)/shard_map/ppermute | solution.py:399
  50.3 12.1 %collective-permute-start.1 = (f32[256,128]{1,0:T(8,128)S(1)}, f32[256,128]{1,0:T(8,128)S(1)}, u32[]{:S(2)}, u32[]{:S(2)}) collective-permute-start(f32[256,128]{1,0:T(8,128)S(1)} %bitcast.18), channel_id=1, source_target_pairs={{0,1},{1,0},{2,3},{3,2},{4,5},{5,4},{6,7},{7,6},{8,9},{9,8},{10,11... | collective-permute-start | bytes 393224 | tf_op jit(solution)/shard_map/ppermute | solution.py:397
  53.8 13.3 %collective-permute-start.2 = (f32[192,128]{1,0:T(8,128)S(1)}, f32[192,128]{1,0:T(8,128)S(1)}, u32[]{:S(2)}, u32[]{:S(2)}) collective-permute-start(f32[192,128]{1,0:T(8,128)S(1)} %get-tuple-element.23), channel_id=1, source_target_pairs={{2,5},{3,4},{4,3},{5,2},{6,9},{7,8},{8,7},{9,6},{10,13},{11,12},{1... | collective-permute-start | bytes 294920 | tf_op jit(solution)/shard_map/ppermute | solution.py:400
  70.0 8.9 %collective-permute-start.5 = (f32[4,8,8,128]{3,2,1,0:T(8,128)S(1)}, f32[4,8,8,128]{3,2,1,0:T(8,128)S(1)}, u32[]{:S(2)}, u32[]{:S(2)}) collective-permute-start(f32[4,8,8,128]{3,2,1,0:T(8,128)S(1)} %all_gather.25.block), channel_id=1, source_target_pairs={{0,12},{4,16},{8,20},{12,24},{14,2},{16,28},{18,6},{20,32},{22,10}... | collective-permute-start | bytes 393224 | tf_op jit(solution)/shard_map/ppermute | solution.py:408
  71.3 9.8 %collective-permute-start.4 = (f32[4,8,8,128]{3,2,1,0:T(8,128)S(1)}, f32[4,8,8,128]{3,2,1,0:T(8,128)S(1)}, u32[]{:S(2)}, u32[]{:S(2)}) collective-permute-start(f32[4,8,8,128]{3,2,1,0:T(8,128)S(1)} %all_gather.25.block), channel_id=1, source_target_pairs={{0,8},{4,12},{8,16},{10,2},{12,20},{14,6},{16,24},{18,10},{20,28},... | collective-permute-start | bytes 393224 | tf_op jit(solution)/shard_map/ppermute | solution.py:408
  75.8 9.3 %collective-permute-start.3 = (f32[4,8,8,128]{3,2,1,0:T(8,128)S(1)}, f32[4,8,8,128]{3,2,1,0:T(8,128)S(1)}, u32[]{:S(2)}, u32[]{:S(2)}) collective-permute-start(f32[4,8,8,128]{3,2,1,0:T(8,128)S(1)} %all_gather.25.block), channel_id=1, source_target_pairs={{0,4},{4,8},{6,2},{8,12},{10,6},{12,16},{14,10},{16,20},{18,14},{2... | collective-permute-start | bytes 393224 | tf_op jit(solution)/shard_map/ppermute | solution.py:408

commit v11 on v9

--- a/solution.py
+++ b/solution.py
@@ -390,9 +390,9 @@
             "dom",
             pairs(lambda px, py, c, k=k: (px, py + k, 0) if c == 0 else (px, py - k, 1)),
         )
-        for k in range(REACH, 0, -1)
-    ]
-    around = lax.all_gather(jnp.stack(sent[::-1]), "dom", axis_index_groups=cores, axis=0)
+        for k in (3, 1, 2)
+    ]
+    around = lax.all_gather(jnp.stack([sent[1], sent[2], sent[0]]), "dom", axis_index_groups=cores, axis=0)
     final = run_up(shift, fine, source, inverse, block, around)
     (correction,) = call(unpack, [(8, 8, 8, 128)])(swap_lines(final))
     return correction

time: 119 us -> 119 us (level)
  no operation moved by 1% of the time
where the time goes in v11:
time: 119 us; the launch traced here: 118 us
  blocking collectives  86.8 us (73%)
  starting transfers between devices  18.3 us (15%)
  waiting for transfers between devices  6.68 us (6%)
  Pallas kernels  6.12 us (5%)
    all_to_all x2, blocking collectives, swap_lines(): lax.all_to_all(value, 'dom', 0, 0, axis_index_groups=lines, tiled=True)  75.3 us
    ppermute x3, starting transfers between devices, body(): lax.ppermute(block, 'dom', pairs(lambda px, py, c, k=k: (px, py + k, 0) i...  7.72 us
    pallas_call x5, Pallas kernels, run(): pl.pallas_call(kernel, out_shape=[(pltpu.VMEM if anywhere else jax.ShapeD...  6.12 us
    ppermute x3, waiting for transfers between devices, body(): lax.ppermute(block, 'dom', pairs(lambda px, py, c, k=k: (px, py + k, 0) i...  5.84 us
    ppermute x1, starting transfers between devices, body(): beside_half = lax.ppermute(half, both, pairs(to_beside, True))  5.2 us
    all_gather x1, blocking collectives, body(): lax.all_gather(own_half, 'dom', axis_index_groups=cores, axis=0)  4.84 us
    ppermute x1, starting transfers between devices, body(): own_half = lax.ppermute(half, 'band', [(0, 1), (1, 0)])  3.48 us
  transfers between devices with their start and end apart: 6, of which 3 were waited for; matrix products, arithmetic and copies ran while one was open for 0% of the time, Pallas kernels for 0%

profile of v11, /device:TPU:32, one launch (start us, length us, event | category | flops | bytes accessed | tf_op | source)
XLA Modules:
  0.0 118.1 jit_solution(3527146592055521184)
XLA Ops:
  0.0 1.0 shard_map.37
  1.0 47.4 %all_to_all.22 = f32[16,48,128]{2,1,0:T(8,128)S(1)} all-to-all(f32[16,48,128]{2,1,0:T(8,128)S(1)} %bitcast.17), channel_id=1, replica_groups={{0,2,64,66,128,130,192,194,256,258,320,322,384,386,448,450},{4,6,68,70,..., dimensions={0} | all-to-all | bytes 786432 | tf_op jit(solution)/shard_map/all_to_all | solution.py:364
  48.4 1.9 %collective-permute-start = (f32[704,128]{1,0:T(8,128)S(1)}, f32[704,128]{1,0:T(8,128)S(1)}, u32[]{:S(2)}, u32[]{:S(2)}) collective-permute-start(f32[704,128]{1,0:T(8,128)S(1)} %get-tuple-element.15), channel_id=1, source_target_pairs={{2,4},{4,2},{6,8},{8,6},{10,12},{12,10},{14,16},{16,14},{18,20},{2... | collective-permute-start | bytes 1081352 | tf_op jit(solution)/shard_map/ppermute | solution.py:381
  50.3 3.5 %collective-permute-start.1 = (f32[256,128]{1,0:T(8,128)S(1)}, f32[256,128]{1,0:T(8,128)S(1)}, u32[]{:S(2)}, u32[]{:S(2)}) collective-permute-start(f32[256,128]{1,0:T(8,128)S(1)} %bitcast.18), channel_id=1, source_target_pairs={{0,1},{1,0},{2,3},{3,2},{4,5},{5,4},{6,7},{7,6},{8,9},{9,8},{10,11... | collective-permute-start | bytes 393224 | tf_op jit(solution)/shard_map/ppermute | solution.py:379
  53.8 5.2 %collective-permute-start.2 = (f32[192,128]{1,0:T(8,128)S(1)}, f32[192,128]{1,0:T(8,128)S(1)}, u32[]{:S(2)}, u32[]{:S(2)}) collective-permute-start(f32[192,128]{1,0:T(8,128)S(1)} %get-tuple-element.16), channel_id=1, source_target_pairs={{2,5},{3,4},{4,3},{5,2},{6,9},{7,8},{8,7},{9,6},{10,13},{11,12},{1... | collective-permute-start | bytes 294920 | tf_op jit(solution)/shard_map/ppermute | solution.py:382
  59.0 2.4 %all_gather.22.cores = f32[2,768,128]{2,1,0:T(8,128)S(1)} all-gather(f32[1,768,128]{2,1,0:T(8,128)S(1)} %bitcast.12), channel_id=1, replica_groups={{0,2},{4,6},{8,10},{12,14},{16,18},{20,22},{24,26},{28,30},{32,34},{36,..., dimensions={0}, use_global_device_ids=true | all-gather | bytes 1179648 | tf_op jit(solution)/shard_map/all_gather | solution.py:383
  61.4 0.8 collective-permute-done.1
  62.3 4.8 %all-gather = f32[512,128]{1,0:T(8,128)S(1)} all-gather(f32[256,128]{1,0:T(8,128)S(1)} %collective-permute-done.1), channel_id=2, replica_groups={{0,2},{4,6},{8,10},{12,14},{16,18},{20,22},{24,26},{28,30},{32,34},{36,..., dimensions={0}, use_global_device_ids=true | all-gather | bytes 393216 | tf_op jit(solution)/shard_map/all_gather | solution.py:384
  67.1 0.0 collective-permute-done.2.beside_half
  67.1 0.0 collective-permute-done.beside
  67.1 2.0 %shard_map.39 = (f32[8,8,8,256]{3,2,1,0:T(8,128)S(1)}, f32[10,8,8,256]{3,2,1,0:T(8,128)S(1)}, f32[10,8,8,256]{3,2,1,0:T(8,128)S(1)}, f32[2,8,8,128]{3,2,1,0:T(8,128)S(1)}) custom-call(f32[8,128]{1,0:T(8,128)S(1)} %get-tuple-element.13.shifts, f32[2,768,128]{2,1,0:T(8,128)S(1)} %all_gather.22.cores, f32[704,128]{1,0:T(8,128)S(1)} %collective-permute-done.beside, ...), custom_call_target="tpu_custom_call" | custom-call | tf_op jit(solution)/shard_map/pallas_call | solution.py:320
  69.1 1.9 %all_gather.25.block = f32[4,8,8,128]{3,2,1,0:T(8,128)S(1)} all-gather(f32[2,8,8,128]{3,2,1,0:T(8,128)S(1)} %get-tuple-element.20), channel_id=1, replica_groups={{0,2},{4,6},{8,10},{12,14},{16,18},{20,22},{24,26},{28,30},{32,34},{36,..., dimensions={0}, use_global_device_ids=true | all-gather | bytes 196608 | tf_op jit(solution)/shard_map/all_gather | solution.py:386
  71.0 1.3 %collective-permute-start.5 = (f32[4,8,8,128]{3,2,1,0:T(8,128)S(1)}, f32[4,8,8,128]{3,2,1,0:T(8,128)S(1)}, u32[]{:S(2)}, u32[]{:S(2)}) collective-permute-start(f32[4,8,8,128]{3,2,1,0:T(8,128)S(1)} %all_gather.25.block), channel_id=1, source_target_pairs={{0,12},{4,16},{8,20},{12,24},{14,2},{16,28},{18,6},{20,32},{22,10}... | collective-permute-start | bytes 393224 | tf_op jit(solution)/shard_map/ppermute | solution.py:388
  72.3 3.0 %collective-permute-start.4 = (f32[4,8,8,128]{3,2,1,0:T(8,128)S(1)}, f32[4,8,8,128]{3,2,1,0:T(8,128)S(1)}, u32[]{:S(2)}, u32[]{:S(2)}) collective-permute-start(f32[4,8,8,128]{3,2,1,0:T(8,128)S(1)} %all_gather.25.block), channel_id=1, source_target_pairs={{0,8},{4,12},{8,16},{10,2},{12,20},{14,6},{16,24},{18,10},{20,28},... | collective-permute-start | bytes 393224 | tf_op jit(solution)/shard_map/ppermute | solution.py:388
  75.3 3.4 %collective-permute-start.3 = (f32[4,8,8,128]{3,2,1,0:T(8,128)S(1)}, f32[4,8,8,128]{3,2,1,0:T(8,128)S(1)}, u32[]{:S(2)}, u32[]{:S(2)}) collective-permute-start(f32[4,8,8,128]{3,2,1,0:T(8,128)S(1)} %all_gather.25.block), channel_id=1, source_target_pairs={{0,4},{4,8},{6,2},{8,12},{10,6},{12,16},{14,10},{16,20},{18,14},{2... | collective-permute-start | bytes 393224 | tf_op jit(solution)/shard_map/ppermute | solution.py:388
  78.8 0.0 collective-permute-done.5
  78.8 2.2 %collective-permute-done.4 = f32[4,8,8,128]{3,2,1,0:T(8,128)S(1)} collective-permute-done((f32[4,8,8,128]{3,2,1,0:T(8,128)S(1)}, f32[4,8,8,128]{3,2,1,0:T(8,128)S(1)}, u32[]{:S(2)}, u32[]{:S(2)}) %collective-permute-start.4) | collective-permute-done | bytes 131104 | tf_op jit(solution)/shard_map/ppermute | solution.py:388
  80.9 3.7 %collective-permute-done.3 = f32[4,8,8,128]{3,2,1,0:T(8,128)S(1)} collective-permute-done((f32[4,8,8,128]{3,2,1,0:T(8,128)S(1)}, f32[4,8,8,128]{3,2,1,0:T(8,128)S(1)}, u32[]{:S(2)}, u32[]{:S(2)}) %collective-permute-start.3) | collective-permute-done | bytes 131104 | tf_op jit(solution)/shard_map/ppermute | solution.py:388
  84.6 2.4 %all-gather.1 = f32[6,4,8,8,128]{4,3,2,1,0:T(8,128)S(1)} all-gather(f32[3,4,8,8,128]{4,3,2,1,0:T(8,128)S(1)} %pad_maximum_fusion), channel_id=3, replica_groups={{0,2},{4,6},{8,10},{12,14},{16,18},{20,22},{24,26},{28,30},{32,34},{36,..., dimensions={0}, use_global_device_ids=true | all-gather | bytes 1179648 | tf_op jit(solution)/shard_map/all_gather | solution.py:395
  87.0 2.4 %shard_map.40 = f32[512,128]{1,0:T(8,128)S(1)} custom-call(f32[8,128]{1,0:T(8,128)S(1)} %get-tuple-element.13.shifts, f32[8,8,8,256]{3,2,1,0:T(8,128)S(1)} %get-tuple-element.17.fine, f32[10,8,8,256]{3,2,1,0:T(8,128)S(1)} %get-tuple-element.18.source, f32[10,8,8,256]{3,2,1,0:T(8,128)S(1)} %get-tuple-element.19.inverse, ...), custom_call_target="tpu_custom_call" | custom-call | tf_op jit(solution)/shard_map/pallas_call | solution.py:320
  89.4 27.9 %all_to_all.23 = f32[16,32,128]{2,1,0:T(8,128)S(1)} all-to-all(f32[16,32,128]{2,1,0:T(8,128)S(1)} %bitcast.14), channel_id=1, replica_groups={{0,2,64,66,128,130,192,194,256,258,320,322,384,386,448,450},{4,6,68,70,..., dimensions={0} | all-to-all | bytes 524288 | tf_op jit(solution)/shard_map/all_to_all | solution.py:364
  117.3 0.7 shard_map.41
  (3 shorter events, 0.1 us)
Async XLA Ops:
  48.4 18.7 %collective-permute-start = (f32[704,128]{1,0:T(8,128)S(1)}, f32[704,128]{1,0:T(8,128)S(1)}, u32[]{:S(2)}, u32[]{:S(2)}) collective-permute-start(f32[704,128]{1,0:T(8,128)S(1)} %get-tuple-element.15), channel_id=1, source_target_pairs={{2,4},{4,2},{6,8},{8,6},{10,12},{12,10},{14,16},{16,14},{18,20},{2... | collective-permute-start | bytes 1081352 | tf_op jit(solution)/shard_map/ppermute | solution.py:381
  50.3 11.9 %collective-permute-start.1 = (f32[256,128]{1,0:T(8,128)S(1)}, f32[256,128]{1,0:T(8,128)S(1)}, u32[]{:S(2)}, u32[]{:S(2)}) collective-permute-start(f32[256,128]{1,0:T(8,128)S(1)} %bitcast.18), channel_id=1, source_target_pairs={{0,1},{1,0},{2,3},{3,2},{4,5},{5,4},{6,7},{7,6},{8,9},{9,8},{10,11... | collective-permute-start | bytes 393224 | tf_op jit(solution)/shard_map/ppermute | solution.py:379
  53.8 13.3 %collective-permute-start.2 = (f32[192,128]{1,0:T(8,128)S(1)}, f32[192,128]{1,0:T(8,128)S(1)}, u32[]{:S(2)}, u32[]{:S(2)}) collective-permute-start(f32[192,128]{1,0:T(8,128)S(1)} %get-tuple-element.16), channel_id=1, source_target_pairs={{2,5},{3,4},{4,3},{5,2},{6,9},{7,8},{8,7},{9,6},{10,13},{11,12},{1... | collective-permute-start | bytes 294920 | tf_op jit(solution)/shard_map/ppermute | solution.py:382
  71.0 7.7 %collective-permute-start.5 = (f32[4,8,8,128]{3,2,1,0:T(8,128)S(1)}, f32[4,8,8,128]{3,2,1,0:T(8,128)S(1)}, u32[]{:S(2)}, u32[]{:S(2)}) collective-permute-start(f32[4,8,8,128]{3,2,1,0:T(8,128)S(1)} %all_gather.25.block), channel_id=1, source_target_pairs={{0,12},{4,16},{8,20},{12,24},{14,2},{16,28},{18,6},{20,32},{22,10}... | collective-permute-start | bytes 393224 | tf_op jit(solution)/shard_map/ppermute | solution.py:388
  72.3 8.6 %collective-permute-start.4 = (f32[4,8,8,128]{3,2,1,0:T(8,128)S(1)}, f32[4,8,8,128]{3,2,1,0:T(8,128)S(1)}, u32[]{:S(2)}, u32[]{:S(2)}) collective-permute-start(f32[4,8,8,128]{3,2,1,0:T(8,128)S(1)} %all_gather.25.block), channel_id=1, source_target_pairs={{0,8},{4,12},{8,16},{10,2},{12,20},{14,6},{16,24},{18,10},{20,28},... | collective-permute-start | bytes 393224 | tf_op jit(solution)/shard_map/ppermute | solution.py:388
  75.3 9.3 %collective-permute-start.3 = (f32[4,8,8,128]{3,2,1,0:T(8,128)S(1)}, f32[4,8,8,128]{3,2,1,0:T(8,128)S(1)}, u32[]{:S(2)}, u32[]{:S(2)}) collective-permute-start(f32[4,8,8,128]{3,2,1,0:T(8,128)S(1)} %all_gather.25.block), channel_id=1, source_target_pairs={{0,4},{4,8},{6,2},{8,12},{10,6},{12,16},{14,10},{16,20},{18,14},{2... | collective-permute-start | bytes 393224 | tf_op jit(solution)/shard_map/ppermute | solution.py:388

commit v12 on v9

--- a/solution.py
+++ b/solution.py
@@ -201,7 +201,7 @@
                 start[row, i] = v * s
 
     each(10, 2, first)
-    sweep(start, source, inverse, fine_out, FINE, 8, 2, (0, 1, 1))
+    sweep(start, source, inverse, fine_out, FINE, 8, 4, (0, 1, 1))
 
     pool = pooling(256, 128)
     means = []
@@ -245,7 +245,7 @@
             inverse1[row, i] = v
             other[row, i] = v * s
 
-    sweep(other, source1, inverse1, middle, MIDDLE, 26, 4, (1, 1, 1))
+    sweep(other, source1, inverse1, middle, MIDDLE, 26, 13, (1, 1, 1))
 
     pool = pooling(128, 128)
     spread = spreading(128, 128)
@@ -294,7 +294,7 @@
             work[row, i] = fine[row, i] + wide[at : at + 8]
 
     final = work.at[8:14]
-    sweep(work, source, inverse, final, FINE, 6, 2, (0, 1, 2))
+    sweep(work, source, inverse, final, FINE, 6, 3, (0, 1, 2))
     for row in range(4):
         new = sweep_row(
             [take(final, row + d) for d in range(3)], take(source, row + 3), take(inverse, row + 3), FINE

time: 119 us -> 119 us (level)
  no operation moved by 1% of the time
where the time goes in v12:
time: 119 us; the launch traced here: 118 us
  blocking collectives  86.8 us (73%)
  starting transfers between devices  18.3 us (15%)
  waiting for transfers between devices  6.68 us (6%)
  Pallas kernels  6.12 us (5%)
    all_to_all x2, blocking collectives, swap_lines(): lax.all_to_all(value, 'dom', 0, 0, axis_index_groups=lines, tiled=True)  75.3 us
    ppermute x3, starting transfers between devices, body(): lax.ppermute(block, 'dom', pairs(lambda px, py, c, k=k: (px, py + k, 0) i...  7.72 us
    pallas_call x5, Pallas kernels, run(): pl.pallas_call(kernel, out_shape=[(pltpu.VMEM if anywhere else jax.ShapeD...  6.12 us
    ppermute x3, waiting for transfers between devices, body(): lax.ppermute(block, 'dom', pairs(lambda px, py, c, k=k: (px, py + k, 0) i...  5.84 us
    ppermute x1, starting transfers between devices, body(): beside_half = lax.ppermute(half, both, pairs(to_beside, True))  5.2 us
    all_gather x1, blocking collectives, body(): lax.all_gather(own_half, 'dom', axis_index_groups=cores, axis=0)  4.84 us
    ppermute x1, starting transfers between devices, body(): own_half = lax.ppermute(half, 'band', [(0, 1), (1, 0)])  3.48 us
  transfers between devices with their start and end apart: 6, of which 3 were waited for; matrix products, arithmetic and copies ran while one was open for 0% of the time, Pallas kernels for 0%

profile of v12, /device:TPU:32, one launch (start us, length us, event | category | flops | bytes accessed | tf_op | source)
XLA Modules:
  0.0 118.1 jit_solution(3527146592055521184)
XLA Ops:
  0.0 1.0 shard_map.37
  1.0 47.4 %all_to_all.22 = f32[16,48,128]{2,1,0:T(8,128)S(1)} all-to-all(f32[16,48,128]{2,1,0:T(8,128)S(1)} %bitcast.17), channel_id=1, replica_groups={{0,2,64,66,128,130,192,194,256,258,320,322,384,386,448,450},{4,6,68,70,..., dimensions={0} | all-to-all | bytes 786432 | tf_op jit(solution)/shard_map/all_to_all | solution.py:364
  48.4 1.9 %collective-permute-start = (f32[704,128]{1,0:T(8,128)S(1)}, f32[704,128]{1,0:T(8,128)S(1)}, u32[]{:S(2)}, u32[]{:S(2)}) collective-permute-start(f32[704,128]{1,0:T(8,128)S(1)} %get-tuple-element.15), channel_id=1, source_target_pairs={{2,4},{4,2},{6,8},{8,6},{10,12},{12,10},{14,16},{16,14},{18,20},{2... | collective-permute-start | bytes 1081352 | tf_op jit(solution)/shard_map/ppermute | solution.py:381
  50.3 3.5 %collective-permute-start.1 = (f32[256,128]{1,0:T(8,128)S(1)}, f32[256,128]{1,0:T(8,128)S(1)}, u32[]{:S(2)}, u32[]{:S(2)}) collective-permute-start(f32[256,128]{1,0:T(8,128)S(1)} %bitcast.18), channel_id=1, source_target_pairs={{0,1},{1,0},{2,3},{3,2},{4,5},{5,4},{6,7},{7,6},{8,9},{9,8},{10,11... | collective-permute-start | bytes 393224 | tf_op jit(solution)/shard_map/ppermute | solution.py:379
  53.8 5.2 %collective-permute-start.2 = (f32[192,128]{1,0:T(8,128)S(1)}, f32[192,128]{1,0:T(8,128)S(1)}, u32[]{:S(2)}, u32[]{:S(2)}) collective-permute-start(f32[192,128]{1,0:T(8,128)S(1)} %get-tuple-element.16), channel_id=1, source_target_pairs={{2,5},{3,4},{4,3},{5,2},{6,9},{7,8},{8,7},{9,6},{10,13},{11,12},{1... | collective-permute-start | bytes 294920 | tf_op jit(solution)/shard_map/ppermute | solution.py:382
  59.0 2.4 %all_gather.22.cores = f32[2,768,128]{2,1,0:T(8,128)S(1)} all-gather(f32[1,768,128]{2,1,0:T(8,128)S(1)} %bitcast.12), channel_id=1, replica_groups={{0,2},{4,6},{8,10},{12,14},{16,18},{20,22},{24,26},{28,30},{32,34},{36,..., dimensions={0}, use_global_device_ids=true | all-gather | bytes 1179648 | tf_op jit(solution)/shard_map/all_gather | solution.py:383
  61.4 0.8 collective-permute-done.1
  62.3 4.8 %all-gather = f32[512,128]{1,0:T(8,128)S(1)} all-gather(f32[256,128]{1,0:T(8,128)S(1)} %collective-permute-done.1), channel_id=2, replica_groups={{0,2},{4,6},{8,10},{12,14},{16,18},{20,22},{24,26},{28,30},{32,34},{36,..., dimensions={0}, use_global_device_ids=true | all-gather | bytes 393216 | tf_op jit(solution)/shard_map/all_gather | solution.py:384
  67.1 0.0 collective-permute-done.2.beside_half
  67.1 0.0 collective-permute-done.beside
  67.1 2.0 %shard_map.39 = (f32[8,8,8,256]{3,2,1,0:T(8,128)S(1)}, f32[10,8,8,256]{3,2,1,0:T(8,128)S(1)}, f32[10,8,8,256]{3,2,1,0:T(8,128)S(1)}, f32[2,8,8,128]{3,2,1,0:T(8,128)S(1)}) custom-call(f32[8,128]{1,0:T(8,128)S(1)} %get-tuple-element.13.shifts, f32[2,768,128]{2,1,0:T(8,128)S(1)} %all_gather.22.cores, f32[704,128]{1,0:T(8,128)S(1)} %collective-permute-done.beside, ...), custom_call_target="tpu_custom_call" | custom-call | tf_op jit(solution)/shard_map/pallas_call | solution.py:320
  69.1 1.9 %all_gather.25.block = f32[4,8,8,128]{3,2,1,0:T(8,128)S(1)} all-gather(f32[2,8,8,128]{3,2,1,0:T(8,128)S(1)} %get-tuple-element.20), channel_id=1, replica_groups={{0,2},{4,6},{8,10},{12,14},{16,18},{20,22},{24,26},{28,30},{32,34},{36,..., dimensions={0}, use_global_device_ids=true | all-gather | bytes 196608 | tf_op jit(solution)/shard_map/all_gather | solution.py:386
  71.0 1.3 %collective-permute-start.5 = (f32[4,8,8,128]{3,2,1,0:T(8,128)S(1)}, f32[4,8,8,128]{3,2,1,0:T(8,128)S(1)}, u32[]{:S(2)}, u32[]{:S(2)}) collective-permute-start(f32[4,8,8,128]{3,2,1,0:T(8,128)S(1)} %all_gather.25.block), channel_id=1, source_target_pairs={{0,12},{4,16},{8,20},{12,24},{14,2},{16,28},{18,6},{20,32},{22,10}... | collective-permute-start | bytes 393224 | tf_op jit(solution)/shard_map/ppermute | solution.py:388
  72.3 3.0 %collective-permute-start.4 = (f32[4,8,8,128]{3,2,1,0:T(8,128)S(1)}, f32[4,8,8,128]{3,2,1,0:T(8,128)S(1)}, u32[]{:S(2)}, u32[]{:S(2)}) collective-permute-start(f32[4,8,8,128]{3,2,1,0:T(8,128)S(1)} %all_gather.25.block), channel_id=1, source_target_pairs={{0,8},{4,12},{8,16},{10,2},{12,20},{14,6},{16,24},{18,10},{20,28},... | collective-permute-start | bytes 393224 | tf_op jit(solution)/shard_map/ppermute | solution.py:388
  75.3 3.4 %collective-permute-start.3 = (f32[4,8,8,128]{3,2,1,0:T(8,128)S(1)}, f32[4,8,8,128]{3,2,1,0:T(8,128)S(1)}, u32[]{:S(2)}, u32[]{:S(2)}) collective-permute-start(f32[4,8,8,128]{3,2,1,0:T(8,128)S(1)} %all_gather.25.block), channel_id=1, source_target_pairs={{0,4},{4,8},{6,2},{8,12},{10,6},{12,16},{14,10},{16,20},{18,14},{2... | collective-permute-start | bytes 393224 | tf_op jit(solution)/shard_map/ppermute | solution.py:388
  78.8 0.0 collective-permute-done.5
  78.8 2.2 %collective-permute-done.4 = f32[4,8,8,128]{3,2,1,0:T(8,128)S(1)} collective-permute-done((f32[4,8,8,128]{3,2,1,0:T(8,128)S(1)}, f32[4,8,8,128]{3,2,1,0:T(8,128)S(1)}, u32[]{:S(2)}, u32[]{:S(2)}) %collective-permute-start.4) | collective-permute-done | bytes 131104 | tf_op jit(solution)/shard_map/ppermute | solution.py:388
  80.9 3.7 %collective-permute-done.3 = f32[4,8,8,128]{3,2,1,0:T(8,128)S(1)} collective-permute-done((f32[4,8,8,128]{3,2,1,0:T(8,128)S(1)}, f32[4,8,8,128]{3,2,1,0:T(8,128)S(1)}, u32[]{:S(2)}, u32[]{:S(2)}) %collective-permute-start.3) | collective-permute-done | bytes 131104 | tf_op jit(solution)/shard_map/ppermute | solution.py:388
  84.6 2.4 %all-gather.1 = f32[6,4,8,8,128]{4,3,2,1,0:T(8,128)S(1)} all-gather(f32[3,4,8,8,128]{4,3,2,1,0:T(8,128)S(1)} %pad_maximum_fusion), channel_id=3, replica_groups={{0,2},{4,6},{8,10},{12,14},{16,18},{20,22},{24,26},{28,30},{32,34},{36,..., dimensions={0}, use_global_device_ids=true | all-gather | bytes 1179648 | tf_op jit(solution)/shard_map/all_gather | solution.py:395
  87.0 2.4 %shard_map.40 = f32[512,128]{1,0:T(8,128)S(1)} custom-call(f32[8,128]{1,0:T(8,128)S(1)} %get-tuple-element.13.shifts, f32[8,8,8,256]{3,2,1,0:T(8,128)S(1)} %get-tuple-element.17.fine, f32[10,8,8,256]{3,2,1,0:T(8,128)S(1)} %get-tuple-element.18.source, f32[10,8,8,256]{3,2,1,0:T(8,128)S(1)} %get-tuple-element.19.inverse, ...), custom_call_target="tpu_custom_call" | custom-call | tf_op jit(solution)/shard_map/pallas_call | solution.py:320
  89.4 27.9 %all_to_all.23 = f32[16,32,128]{2,1,0:T(8,128)S(1)} all-to-all(f32[16,32,128]{2,1,0:T(8,128)S(1)} %bitcast.14), channel_id=1, replica_groups={{0,2,64,66,128,130,192,194,256,258,320,322,384,386,448,450},{4,6,68,70,..., dimensions={0} | all-to-all | bytes 524288 | tf_op jit(solution)/shard_map/all_to_all | solution.py:364
  117.3 0.7 shard_map.41
  (3 shorter events, 0.1 us)
Async XLA Ops:
  48.4 18.7 %collective-permute-start = (f32[704,128]{1,0:T(8,128)S(1)}, f32[704,128]{1,0:T(8,128)S(1)}, u32[]{:S(2)}, u32[]{:S(2)}) collective-permute-start(f32[704,128]{1,0:T(8,128)S(1)} %get-tuple-element.15), channel_id=1, source_target_pairs={{2,4},{4,2},{6,8},{8,6},{10,12},{12,10},{14,16},{16,14},{18,20},{2... | collective-permute-start | bytes 1081352 | tf_op jit(solution)/shard_map/ppermute | solution.py:381
  50.3 11.9 %collective-permute-start.1 = (f32[256,128]{1,0:T(8,128)S(1)}, f32[256,128]{1,0:T(8,128)S(1)}, u32[]{:S(2)}, u32[]{:S(2)}) collective-permute-start(f32[256,128]{1,0:T(8,128)S(1)} %bitcast.18), channel_id=1, source_target_pairs={{0,1},{1,0},{2,3},{3,2},{4,5},{5,4},{6,7},{7,6},{8,9},{9,8},{10,11... | collective-permute-start | bytes 393224 | tf_op jit(solution)/shard_map/ppermute | solution.py:379
  53.8 13.3 %collective-permute-start.2 = (f32[192,128]{1,0:T(8,128)S(1)}, f32[192,128]{1,0:T(8,128)S(1)}, u32[]{:S(2)}, u32[]{:S(2)}) collective-permute-start(f32[192,128]{1,0:T(8,128)S(1)} %get-tuple-element.16), channel_id=1, source_target_pairs={{2,5},{3,4},{4,3},{5,2},{6,9},{7,8},{8,7},{9,6},{10,13},{11,12},{1... | collective-permute-start | bytes 294920 | tf_op jit(solution)/shard_map/ppermute | solution.py:382
  71.0 7.7 %collective-permute-start.5 = (f32[4,8,8,128]{3,2,1,0:T(8,128)S(1)}, f32[4,8,8,128]{3,2,1,0:T(8,128)S(1)}, u32[]{:S(2)}, u32[]{:S(2)}) collective-permute-start(f32[4,8,8,128]{3,2,1,0:T(8,128)S(1)} %all_gather.25.block), channel_id=1, source_target_pairs={{0,12},{4,16},{8,20},{12,24},{14,2},{16,28},{18,6},{20,32},{22,10}... | collective-permute-start | bytes 393224 | tf_op jit(solution)/shard_map/ppermute | solution.py:388
  72.3 8.6 %collective-permute-start.4 = (f32[4,8,8,128]{3,2,1,0:T(8,128)S(1)}, f32[4,8,8,128]{3,2,1,0:T(8,128)S(1)}, u32[]{:S(2)}, u32[]{:S(2)}) collective-permute-start(f32[4,8,8,128]{3,2,1,0:T(8,128)S(1)} %all_gather.25.block), channel_id=1, source_target_pairs={{0,8},{4,12},{8,16},{10,2},{12,20},{14,6},{16,24},{18,10},{20,28},... | collective-permute-start | bytes 393224 | tf_op jit(solution)/shard_map/ppermute | solution.py:388
  75.3 9.3 %collective-permute-start.3 = (f32[4,8,8,128]{3,2,1,0:T(8,128)S(1)}, f32[4,8,8,128]{3,2,1,0:T(8,128)S(1)}, u32[]{:S(2)}, u32[]{:S(2)}) collective-permute-start(f32[4,8,8,128]{3,2,1,0:T(8,128)S(1)} %all_gather.25.block), channel_id=1, source_target_pairs={{0,4},{4,8},{6,2},{8,12},{10,6},{12,16},{14,10},{16,20},{18,14},{2... | collective-permute-start | bytes 393224 | tf_op jit(solution)/shard_map/ppermute | solution.py:388

commit v13 on v9

--- a/solution.py
+++ b/solution.py
@@ -283,7 +283,7 @@
             at = 16 * (row // 2 - 4) + 8 * (i // 2)
             other[row, i] = middle[row, i] + wide[at : at + 8]
 
-    sweep(other, source1, inverse1, middle, MIDDLE, 8, 4, (10, 10, 10))
+    sweep(other, source1, inverse1, middle, MIDDLE, 8, 8, (10, 10, 10))
     sweep(middle, source1, inverse1, other, MIDDLE, 6, 6, (11, 11, 11))
 
     spread = spreading(128, 256)

time: 119 us -> 119 us (level)
  no operation moved by 1% of the time
where the time goes in v13:
time: 119 us; the launch traced here: 118 us
  blocking collectives  86.8 us (73%)
  starting transfers between devices  18.3 us (15%)
  waiting for transfers between devices  6.68 us (6%)
  Pallas kernels  6.12 us (5%)
    all_to_all x2, blocking collectives, swap_lines(): lax.all_to_all(value, 'dom', 0, 0, axis_index_groups=lines, tiled=True)  75.3 us
    ppermute x3, starting transfers between devices, body(): lax.ppermute(block, 'dom', pairs(lambda px, py, c, k=k: (px, py + k, 0) i...  7.72 us
    pallas_call x5, Pallas kernels, run(): pl.pallas_call(kernel, out_shape=[(pltpu.VMEM if anywhere else jax.ShapeD...  6.12 us
    ppermute x3, waiting for transfers between devices, body(): lax.ppermute(block, 'dom', pairs(lambda px, py, c, k=k: (px, py + k, 0) i...  5.84 us
    ppermute x1, starting transfers between devices, body(): beside_half = lax.ppermute(half, both, pairs(to_beside, True))  5.2 us
    all_gather x1, blocking collectives, body(): lax.all_gather(own_half, 'dom', axis_index_groups=cores, axis=0)  4.84 us
    ppermute x1, starting transfers between devices, body(): own_half = lax.ppermute(half, 'band', [(0, 1), (1, 0)])  3.48 us
  transfers between devices with their start and end apart: 6, of which 3 were waited for; matrix products, arithmetic and copies ran while one was open for 0% of the time, Pallas kernels for 0%

profile of v13, /device:TPU:32, one launch (start us, length us, event | category | flops | bytes accessed | tf_op | source)
XLA Modules:
  0.0 118.1 jit_solution(3527146592055521184)
XLA Ops:
  0.0 1.0 shard_map.37
  1.0 47.4 %all_to_all.22 = f32[16,48,128]{2,1,0:T(8,128)S(1)} all-to-all(f32[16,48,128]{2,1,0:T(8,128)S(1)} %bitcast.17), channel_id=1, replica_groups={{0,2,64,66,128,130,192,194,256,258,320,322,384,386,448,450},{4,6,68,70,..., dimensions={0} | all-to-all | bytes 786432 | tf_op jit(solution)/shard_map/all_to_all | solution.py:364
  48.4 1.9 %collective-permute-start = (f32[704,128]{1,0:T(8,128)S(1)}, f32[704,128]{1,0:T(8,128)S(1)}, u32[]{:S(2)}, u32[]{:S(2)}) collective-permute-start(f32[704,128]{1,0:T(8,128)S(1)} %get-tuple-element.15), channel_id=1, source_target_pairs={{2,4},{4,2},{6,8},{8,6},{10,12},{12,10},{14,16},{16,14},{18,20},{2... | collective-permute-start | bytes 1081352 | tf_op jit(solution)/shard_map/ppermute | solution.py:381
  50.3 3.5 %collective-permute-start.1 = (f32[256,128]{1,0:T(8,128)S(1)}, f32[256,128]{1,0:T(8,128)S(1)}, u32[]{:S(2)}, u32[]{:S(2)}) collective-permute-start(f32[256,128]{1,0:T(8,128)S(1)} %bitcast.18), channel_id=1, source_target_pairs={{0,1},{1,0},{2,3},{3,2},{4,5},{5,4},{6,7},{7,6},{8,9},{9,8},{10,11... | collective-permute-start | bytes 393224 | tf_op jit(solution)/shard_map/ppermute | solution.py:379
  53.8 5.2 %collective-permute-start.2 = (f32[192,128]{1,0:T(8,128)S(1)}, f32[192,128]{1,0:T(8,128)S(1)}, u32[]{:S(2)}, u32[]{:S(2)}) collective-permute-start(f32[192,128]{1,0:T(8,128)S(1)} %get-tuple-element.16), channel_id=1, source_target_pairs={{2,5},{3,4},{4,3},{5,2},{6,9},{7,8},{8,7},{9,6},{10,13},{11,12},{1... | collective-permute-start | bytes 294920 | tf_op jit(solution)/shard_map/ppermute | solution.py:382
  59.0 2.4 %all_gather.22.cores = f32[2,768,128]{2,1,0:T(8,128)S(1)} all-gather(f32[1,768,128]{2,1,0:T(8,128)S(1)} %bitcast.12), channel_id=1, replica_groups={{0,2},{4,6},{8,10},{12,14},{16,18},{20,22},{24,26},{28,30},{32,34},{36,..., dimensions={0}, use_global_device_ids=true | all-gather | bytes 1179648 | tf_op jit(solution)/shard_map/all_gather | solution.py:383
  61.4 0.8 collective-permute-done.1
  62.3 4.8 %all-gather = f32[512,128]{1,0:T(8,128)S(1)} all-gather(f32[256,128]{1,0:T(8,128)S(1)} %collective-permute-done.1), channel_id=2, replica_groups={{0,2},{4,6},{8,10},{12,14},{16,18},{20,22},{24,26},{28,30},{32,34},{36,..., dimensions={0}, use_global_device_ids=true | all-gather | bytes 393216 | tf_op jit(solution)/shard_map/all_gather | solution.py:384
  67.1 0.0 collective-permute-done.2.beside_half
  67.1 0.0 collective-permute-done.beside
  67.1 2.0 %shard_map.39 = (f32[8,8,8,256]{3,2,1,0:T(8,128)S(1)}, f32[10,8,8,256]{3,2,1,0:T(8,128)S(1)}, f32[10,8,8,256]{3,2,1,0:T(8,128)S(1)}, f32[2,8,8,128]{3,2,1,0:T(8,128)S(1)}) custom-call(f32[8,128]{1,0:T(8,128)S(1)} %get-tuple-element.13.shifts, f32[2,768,128]{2,1,0:T(8,128)S(1)} %all_gather.22.cores, f32[704,128]{1,0:T(8,128)S(1)} %collective-permute-done.beside, ...), custom_call_target="tpu_custom_call" | custom-call | tf_op jit(solution)/shard_map/pallas_call | solution.py:320
  69.1 1.9 %all_gather.25.block = f32[4,8,8,128]{3,2,1,0:T(8,128)S(1)} all-gather(f32[2,8,8,128]{3,2,1,0:T(8,128)S(1)} %get-tuple-element.20), channel_id=1, replica_groups={{0,2},{4,6},{8,10},{12,14},{16,18},{20,22},{24,26},{28,30},{32,34},{36,..., dimensions={0}, use_global_device_ids=true | all-gather | bytes 196608 | tf_op jit(solution)/shard_map/all_gather | solution.py:386
  71.0 1.3 %collective-permute-start.5 = (f32[4,8,8,128]{3,2,1,0:T(8,128)S(1)}, f32[4,8,8,128]{3,2,1,0:T(8,128)S(1)}, u32[]{:S(2)}, u32[]{:S(2)}) collective-permute-start(f32[4,8,8,128]{3,2,1,0:T(8,128)S(1)} %all_gather.25.block), channel_id=1, source_target_pairs={{0,12},{4,16},{8,20},{12,24},{14,2},{16,28},{18,6},{20,32},{22,10}... | collective-permute-start | bytes 393224 | tf_op jit(solution)/shard_map/ppermute | solution.py:388
  72.3 3.0 %collective-permute-start.4 = (f32[4,8,8,128]{3,2,1,0:T(8,128)S(1)}, f32[4,8,8,128]{3,2,1,0:T(8,128)S(1)}, u32[]{:S(2)}, u32[]{:S(2)}) collective-permute-start(f32[4,8,8,128]{3,2,1,0:T(8,128)S(1)} %all_gather.25.block), channel_id=1, source_target_pairs={{0,8},{4,12},{8,16},{10,2},{12,20},{14,6},{16,24},{18,10},{20,28},... | collective-permute-start | bytes 393224 | tf_op jit(solution)/shard_map/ppermute | solution.py:388
  75.3 3.4 %collective-permute-start.3 = (f32[4,8,8,128]{3,2,1,0:T(8,128)S(1)}, f32[4,8,8,128]{3,2,1,0:T(8,128)S(1)}, u32[]{:S(2)}, u32[]{:S(2)}) collective-permute-start(f32[4,8,8,128]{3,2,1,0:T(8,128)S(1)} %all_gather.25.block), channel_id=1, source_target_pairs={{0,4},{4,8},{6,2},{8,12},{10,6},{12,16},{14,10},{16,20},{18,14},{2... | collective-permute-start | bytes 393224 | tf_op jit(solution)/shard_map/ppermute | solution.py:388
  78.8 0.0 collective-permute-done.5
  78.8 2.2 %collective-permute-done.4 = f32[4,8,8,128]{3,2,1,0:T(8,128)S(1)} collective-permute-done((f32[4,8,8,128]{3,2,1,0:T(8,128)S(1)}, f32[4,8,8,128]{3,2,1,0:T(8,128)S(1)}, u32[]{:S(2)}, u32[]{:S(2)}) %collective-permute-start.4) | collective-permute-done | bytes 131104 | tf_op jit(solution)/shard_map/ppermute | solution.py:388
  80.9 3.7 %collective-permute-done.3 = f32[4,8,8,128]{3,2,1,0:T(8,128)S(1)} collective-permute-done((f32[4,8,8,128]{3,2,1,0:T(8,128)S(1)}, f32[4,8,8,128]{3,2,1,0:T(8,128)S(1)}, u32[]{:S(2)}, u32[]{:S(2)}) %collective-permute-start.3) | collective-permute-done | bytes 131104 | tf_op jit(solution)/shard_map/ppermute | solution.py:388
  84.6 2.4 %all-gather.1 = f32[6,4,8,8,128]{4,3,2,1,0:T(8,128)S(1)} all-gather(f32[3,4,8,8,128]{4,3,2,1,0:T(8,128)S(1)} %pad_maximum_fusion), channel_id=3, replica_groups={{0,2},{4,6},{8,10},{12,14},{16,18},{20,22},{24,26},{28,30},{32,34},{36,..., dimensions={0}, use_global_device_ids=true | all-gather | bytes 1179648 | tf_op jit(solution)/shard_map/all_gather | solution.py:395
  87.0 2.4 %shard_map.40 = f32[512,128]{1,0:T(8,128)S(1)} custom-call(f32[8,128]{1,0:T(8,128)S(1)} %get-tuple-element.13.shifts, f32[8,8,8,256]{3,2,1,0:T(8,128)S(1)} %get-tuple-element.17.fine, f32[10,8,8,256]{3,2,1,0:T(8,128)S(1)} %get-tuple-element.18.source, f32[10,8,8,256]{3,2,1,0:T(8,128)S(1)} %get-tuple-element.19.inverse, ...), custom_call_target="tpu_custom_call" | custom-call | tf_op jit(solution)/shard_map/pallas_call | solution.py:320
  89.4 27.9 %all_to_all.23 = f32[16,32,128]{2,1,0:T(8,128)S(1)} all-to-all(f32[16,32,128]{2,1,0:T(8,128)S(1)} %bitcast.14), channel_id=1, replica_groups={{0,2,64,66,128,130,192,194,256,258,320,322,384,386,448,450},{4,6,68,70,..., dimensions={0} | all-to-all | bytes 524288 | tf_op jit(solution)/shard_map/all_to_all | solution.py:364
  117.3 0.7 shard_map.41
  (3 shorter events, 0.1 us)
Async XLA Ops:
  48.4 18.7 %collective-permute-start = (f32[704,128]{1,0:T(8,128)S(1)}, f32[704,128]{1,0:T(8,128)S(1)}, u32[]{:S(2)}, u32[]{:S(2)}) collective-permute-start(f32[704,128]{1,0:T(8,128)S(1)} %get-tuple-element.15), channel_id=1, source_target_pairs={{2,4},{4,2},{6,8},{8,6},{10,12},{12,10},{14,16},{16,14},{18,20},{2... | collective-permute-start | bytes 1081352 | tf_op jit(solution)/shard_map/ppermute | solution.py:381
  50.3 11.9 %collective-permute-start.1 = (f32[256,128]{1,0:T(8,128)S(1)}, f32[256,128]{1,0:T(8,128)S(1)}, u32[]{:S(2)}, u32[]{:S(2)}) collective-permute-start(f32[256,128]{1,0:T(8,128)S(1)} %bitcast.18), channel_id=1, source_target_pairs={{0,1},{1,0},{2,3},{3,2},{4,5},{5,4},{6,7},{7,6},{8,9},{9,8},{10,11... | collective-permute-start | bytes 393224 | tf_op jit(solution)/shard_map/ppermute | solution.py:379
  53.8 13.3 %collective-permute-start.2 = (f32[192,128]{1,0:T(8,128)S(1)}, f32[192,128]{1,0:T(8,128)S(1)}, u32[]{:S(2)}, u32[]{:S(2)}) collective-permute-start(f32[192,128]{1,0:T(8,128)S(1)} %get-tuple-element.16), channel_id=1, source_target_pairs={{2,5},{3,4},{4,3},{5,2},{6,9},{7,8},{8,7},{9,6},{10,13},{11,12},{1... | collective-permute-start | bytes 294920 | tf_op jit(solution)/shard_map/ppermute | solution.py:382
  71.0 7.7 %collective-permute-start.5 = (f32[4,8,8,128]{3,2,1,0:T(8,128)S(1)}, f32[4,8,8,128]{3,2,1,0:T(8,128)S(1)}, u32[]{:S(2)}, u32[]{:S(2)}) collective-permute-start(f32[4,8,8,128]{3,2,1,0:T(8,128)S(1)} %all_gather.25.block), channel_id=1, source_target_pairs={{0,12},{4,16},{8,20},{12,24},{14,2},{16,28},{18,6},{20,32},{22,10}... | collective-permute-start | bytes 393224 | tf_op jit(solution)/shard_map/ppermute | solution.py:388
  72.3 8.6 %collective-permute-start.4 = (f32[4,8,8,128]{3,2,1,0:T(8,128)S(1)}, f32[4,8,8,128]{3,2,1,0:T(8,128)S(1)}, u32[]{:S(2)}, u32[]{:S(2)}) collective-permute-start(f32[4,8,8,128]{3,2,1,0:T(8,128)S(1)} %all_gather.25.block), channel_id=1, source_target_pairs={{0,8},{4,12},{8,16},{10,2},{12,20},{14,6},{16,24},{18,10},{20,28},... | collective-permute-start | bytes 393224 | tf_op jit(solution)/shard_map/ppermute | solution.py:388
  75.3 9.3 %collective-permute-start.3 = (f32[4,8,8,128]{3,2,1,0:T(8,128)S(1)}, f32[4,8,8,128]{3,2,1,0:T(8,128)S(1)}, u32[]{:S(2)}, u32[]{:S(2)}) collective-permute-start(f32[4,8,8,128]{3,2,1,0:T(8,128)S(1)} %all_gather.25.block), channel_id=1, source_target_pairs={{0,4},{4,8},{6,2},{8,12},{10,6},{12,16},{14,10},{16,20},{18,14},{2... | collective-permute-start | bytes 393224 | tf_op jit(solution)/shard_map/ppermute | solution.py:388
